TPU v7x, 256 devices: a whole 4x4x8 slice. The times are simulated.
256 devices in a mesh: tp: 16 (over z, x_hi), fsdp: 16 (over y, x_lo, core).
Axes of the slice: x: 4 (x_hi: 2, x_lo: 2; x = x_hi * 2 + x_lo), y: 4, z: 8, core: 2. Of those that a mesh axis runs over, the one named last changes fastest.
Arguments:
- activations: bfloat16 [16, 1024, 8192], P('fsdp', 'tp'), may hold values from -6 to 6
- grad_output: bfloat16 [16, 1024, 28672], P('fsdp', None, 'tp'), may hold values from -0.01171875 to 0.01171875
- projection: bfloat16 [8192, 512], P('fsdp'), may hold values from -0.25 to 0.25
- piece_lengths: int32 [16], replicated, may hold values from 1 to 48, 512 in all
- piece_owners: int32 [16], replicated, may hold values from 0 to 15, as said below
- first_moment: float32 [768, 28672], P('fsdp', 'tp'), may hold values from -3 to 3
- second_moment: float32 [768, 28672], P('fsdp', 'tp'), may hold values from 0.0005 to 0.005
Outputs:
- weight_delta: bfloat16 [8192, 28672], P('fsdp', 'tp')
- new_first: float32 [768, 28672], P('fsdp', 'tp')
- new_second: float32 [768, 28672], P('fsdp', 'tp')
Inputs may be any that keep to these rules, and one draw needn't show every extreme that they name: `piece_lengths`: the lengths sum to 512; one of them is exactly 48. `piece_owners`: each owner appears exactly once.
All inputs are finite; a program needn't handle non-finite values.
Results may differ from a plain program's by a relative error of at most 0.0052.
Values may be sent and summed in bfloat16 or wider, within the bound.
No kernel may reach another device: no remote copies, remote signals or barrier semaphores. Data moves between devices by JAX's collectives and lax.ppermute only.
A program may use at most 128 MiB of HBM per device.

v0:
```python
import jax
import jax.numpy as jnp
from jax import lax
from jax.sharding import PartitionSpec as P

STEP = 10


beta_one = 0.9
beta_two = 0.999
adam_eps = 1e-08


def slot_table(piece_lengths, piece_owners, owner_count, slot_count):
    owner_order = jnp.arange(owner_count, dtype=jnp.int32)
    piece_starts = jnp.cumsum(piece_lengths) - piece_lengths
    matches = (piece_owners[None, :] == owner_order[:, None]).astype(jnp.int32)
    own_start = jnp.sum(matches * piece_starts[None, :], axis=1)
    own_length = jnp.sum(matches * piece_lengths[None, :], axis=1)
    slot_offsets = jnp.arange(slot_count, dtype=jnp.int32)
    rank_rows = own_start[:, None] + slot_offsets[None, :]
    live_rows = slot_offsets[None, :] < own_length[:, None]
    return (rank_rows.reshape(-1), live_rows.reshape(-1))


def adam_rows(gradient, live_rows, first_moment, second_moment):
    live_mask = live_rows[:, None]
    new_first = jnp.where(live_mask, beta_one * first_moment + (1.0 - beta_one) * gradient, 0.0)
    new_second = jnp.where(
        live_mask, beta_two * second_moment + (1.0 - beta_two) * gradient * gradient, 0.0
    )
    first_hat = new_first / (1.0 - beta_one**STEP)
    second_hat = new_second / (1.0 - beta_two**STEP)
    update = jnp.where(live_mask, first_hat / (jnp.sqrt(second_hat) + adam_eps), 0.0)
    return (new_first, new_second, update.astype(jnp.bfloat16))


def per_device(
    activations, grad_output, projection, piece_lengths, piece_owners, first_moment, second_moment
):
    own_tokens = activations[0]
    out_grads = grad_output[0]
    rank_count = projection.shape[1]
    full_projection = lax.all_gather(projection, "fsdp", axis=0, tiled=True)
    projected = jnp.dot(
        lax.all_gather(own_tokens, "tp", axis=0, tiled=True),
        full_projection,
        preferred_element_type=jnp.float32,
    ).astype(jnp.bfloat16)
    gradient = lax.dot_general(
        projected, out_grads, (((0,), (0,)), ((), ())), preferred_element_type=jnp.float32
    )
    owner_count = lax.axis_size("fsdp")
    myself = lax.axis_index("fsdp")
    slot_count = first_moment.shape[0]
    rank_rows, live_rows = slot_table(piece_lengths, piece_owners, owner_count, slot_count)
    safe_rows = jnp.clip(rank_rows, 0, rank_count - 1)
    mine_rows = lax.dynamic_slice_in_dim(safe_rows, myself * slot_count, slot_count, 0)
    summed = lax.psum(gradient, "fsdp")
    picked = jnp.take(summed, mine_rows, axis=0)
    my_live = lax.dynamic_slice_in_dim(live_rows, myself * slot_count, slot_count, 0)
    new_first, new_second, update = adam_rows(picked, my_live, first_moment, second_moment)
    chosen = jnp.where(
        live_rows[None, :], jnp.take(projection, safe_rows, axis=1), jnp.zeros((), jnp.bfloat16)
    )
    weight_delta = jnp.dot(
        chosen,
        lax.all_gather(update, "fsdp", axis=0, tiled=True),
        preferred_element_type=jnp.float32,
    )
    return (weight_delta.astype(jnp.bfloat16), new_first, new_second)


def solution(mesh):
    return jax.shard_map(
        per_device,
        mesh=mesh,
        in_specs=(
            P("fsdp", "tp", None),
            P("fsdp", None, "tp"),
            P("fsdp", None),
            P(),
            P(),
            P("fsdp", "tp"),
            P("fsdp", "tp"),
        ),
        out_specs=(P("fsdp", "tp"), P("fsdp", "tp"), P("fsdp", "tp")),
        check_vma=False,
    )
```

profile of v0, /device:TPU:1, one launch (start us, length us, event | category | flops | bytes accessed | tf_op | source)
XLA Modules:
  0.0 507.0 jit_solution(15747705924977625758)
XLA Ops:
  7.2 0.7 all-gather.5.cloned.1.call-update
  7.9 0.7 all-gather.9.cloned.1.call-update
  8.7 60.1 %all-gather.5.cloned.1.call-done = bf16[8192,512]{1,0:T(8,128)(2,1)} async-done(((bf16[512,512]{1,0:T(8,128)(2,1)}), bf16[8192,512]{1,0:T(8,128)(2,1)}) %all-gather.5.cloned.1.call-update) | async-done | bytes 8388624 | tf_op jit(solution)/shard_map/all_gather | solution.py:44
  68.8 227.8 %all-gather.9.cloned.1.call-done = bf16[1,1024,8192]{2,1,0:T(8,128)(2,1)} async-done(((bf16[1,64,8192]{2,1,0:T(8,128)(2,1)}), bf16[1,1024,8192]{2,1,0:T(8,128)(2,1)}) %all-gather.9.cloned.1.call-update) | async-done | bytes 16777232 | tf_op jit(solution)/shard_map/all_gather | solution.py:46
  296.6 22.2 %fusion.2 = f32[512,1792]{1,0:T(8,128)} fusion(bf16[1,1024,1792]{2,1,0:T(8,128)(2,1)} %param.8, bf16[8192,512]{1,0:T(8,128)(2,1)} %all-gather.5.cloned.1.call-done, bf16[1,1024,8192]{2,1,0:T(8,128)(2,1)} %all-gather.9.cloned.1.call-done), kind=kOutput, calls=%fused_computation.4 | convolution fusion | flops 10469507072 | bytes 32505856 | tf_op jit(solution)/shard_map/dot_general | solution.py:50
  318.8 0.2 all-gather.7.cloned.1.call-start
  319.0 0.4 copy-done.3
  319.4 0.1 copy.14
  319.5 0.1 reduce
  319.7 0.1 select_reduce_fusion.1
  319.8 0.1 iota_compare_fusion.1
  319.9 0.1 lt.55
  319.9 0.1 add_clamp_fusion
  320.0 0.1 min.16
  320.1 0.1 dynamic_slice.6
  320.2 0.1 compare_and_fusion.1
  320.3 131.9 %all-reduce.2.cloned.1.call-done = f32[512,1792]{1,0:T(8,128)} async-done(((f32[512,1792]{1,0:T(8,128)}), f32[512,1792]{1,0:T(8,128)}) %all-reduce.2.cloned.1.call-update) | async-done | bytes 3670032 | tf_op jit(solution)/shard_map/psum | solution.py:59
  452.2 2.9 gather_fusion.1
  455.1 1.1 select_convert_fusion
  456.2 0.1 min.18
  456.3 0.2 copy.15
  456.6 2.7 gather_fusion
  459.3 36.4 %all-gather.7.cloned.1.call-done = bf16[768,1792]{1,0:T(8,128)(2,1)} async-done(((bf16[48,1792]{1,0:T(8,128)(2,1)}), bf16[768,1792]{1,0:T(8,128)(2,1)}) %all-gather.7.cloned.1.call-update) | async-done | bytes 2752528 | tf_op jit(solution)/shard_map/all_gather | solution.py:68
  495.7 4.8 convolution_convert_fusion
  (20 shorter events, 0.2 us)
Async XLA Ops:
  7.2 61.6 %all-gather.5.cloned.1.call-start = ((), (), s32[]{:S(2)}) async-start(), calls=%async_computation | async-start | bytes 8912896 | tf_op jit(solution)/shard_map/all_gather | solution.py:44
  7.9 288.7 %all-gather.9.cloned.1.call-start = ((), (), s32[]{:S(2)}) async-start(), calls=%async_computation.3 | async-start | bytes 17825792 | tf_op jit(solution)/shard_map/all_gather | solution.py:46
  8.6 443.5 %all-reduce.2.cloned.1.call-start = ((), (), s32[]{:S(2)}) async-start(), calls=%async_computation.1 | async-start | bytes 7340032 | tf_op jit(solution)/shard_map/psum | solution.py:59
  318.8 0.7 copy-start.3
  318.8 0.9 copy-start.4
  318.8 136.3 %copy-start.1 = (f32[48,1792]{1,0:T(8,128)S(1)}, f32[48,1792]{1,0:T(8,128)}, u32[]{:S(2)}) copy-start(f32[48,1792]{1,0:T(8,128)} %param.12) | copy-start | bytes 1032196
  318.8 136.3 %copy-start.2 = (f32[48,1792]{1,0:T(8,128)S(1)}, f32[48,1792]{1,0:T(8,128)}, u32[]{:S(2)}) copy-start(f32[48,1792]{1,0:T(8,128)} %param.13) | copy-start | bytes 1032196
  318.8 137.5 %copy-start = (bf16[512,512]{1,0:T(8,128)(2,1)S(1)}, bf16[512,512]{1,0:T(8,128)(2,1)}, u32[]{:S(2)}) copy-start(bf16[512,512]{1,0:T(8,128)(2,1)} %param.9) | copy-start | bytes 1572868
  318.8 176.9 %all-gather.7.cloned.1.call-start = ((), (), s32[]{:S(2)}) async-start(), calls=%async_computation.2 | async-start | bytes 2924544 | tf_op jit(solution)/shard_map/all_gather | solution.py:68
Sparse Core Ops, SparseCore 0:
  9.8 58.8 all-gather.4
  71.3 225.1 all-gather.8
  318.9 133.1 all-reduce.1
  456.3 39.3 all-gather.6
where the time goes:
time: 507 us
  waiting for transfers between devices  458 us (90%)
  matrix products  27 us (5%)
  between operations  13.9 us (3%)
  local copies, waits for them, and re-layouts  6.57 us (1%)
    all_gather x1, waiting for transfers between devices, per_device(): lax.all_gather(own_tokens, 'tp', axis=0, tiled=True)  228 us
    psum x1, waiting for transfers between devices, per_device(): summed = lax.psum(gradient, 'fsdp')  132 us
    all_gather x1, waiting for transfers between devices, per_device(): full_projection = lax.all_gather(projection, 'fsdp', axis=0, tiled=True)  60.1 us
    all_gather x1, waiting for transfers between devices, per_device(): lax.all_gather(update, 'fsdp', axis=0, tiled=True)  36.4 us
    dot_general x1, matrix products, per_device(): lax.dot_general(projected, out_grads, (((0,), (0,)), ((), ())), preferred...  22.2 us
  transfers between devices with their start and end apart: 4, of which 4 were waited for; matrix products, arithmetic and copies ran while one was open for 1% of the time, Pallas kernels for 0%

commit v1 on v0

v1 whole, which is shorter than its diff:
```python
import functools

import jax
import jax.numpy as jnp
from jax import lax
from jax.experimental import pallas as pl
from jax.experimental.pallas import tpu as pltpu
from jax.sharding import PartitionSpec as P

STEP = 10
beta_one = 0.9
beta_two = 0.999
adam_eps = 1e-08

F32 = jnp.float32
BF16 = jnp.bfloat16

CHIPS = [(dy, dx) for dy in range(4) for dx in range(2)]


def fsdp_shift(value, dy, dx, dk):
    pairs = [
        (i, ((i // 4 + dy) % 4) * 4 + ((i // 2 % 2) ^ dx) * 2 + ((i % 2) ^ dk)) for i in range(16)
    ]
    return lax.ppermute(value, "fsdp", pairs)


def tp_shift(value, dz, dh):
    pairs = [(i, ((i // 2 + dz) % 8) * 2 + ((i % 2) ^ dh)) for i in range(16)]
    return lax.ppermute(value, "tp", pairs)


def front_kernel(where_ref, a0, a1, a2, a3, p0, p1, p2, p3, o0, o1, o2, o3):
    low = where_ref[1]
    total = None
    for r, p in enumerate((p0, p1, p2, p3)):
        columns = pl.ds(pl.multiple_of((low ^ r) * 512, 512), 512)
        rows = jnp.concatenate([a[:, columns] for a in (a0, a1, a2, a3)], axis=0)
        term = jnp.dot(rows, p[...], preferred_element_type=F32)
        total = term if total is None else total + term
    for s, o in enumerate((o0, o1, o2, o3)):
        o[...] = total[s * 64 : (s + 1) * 64].astype(o.dtype)


def front(where, tokens, received, blocks):
    whole = lambda shape: pl.BlockSpec(shape, lambda i, w: (0, 0))
    return pl.pallas_call(
        front_kernel,
        grid_spec=pltpu.PrefetchScalarGridSpec(
            num_scalar_prefetch=1,
            grid=(1,),
            in_specs=[pl.BlockSpec((64, 2048), lambda i, w: (0, w[0]))]
            + [whole((64, 2048))] * 3
            + [whole((512, 512))] * 4,
            out_specs=[whole((64, 512))] * 4,
        ),
        out_shape=[jax.ShapeDtypeStruct((64, 512), F32)] * 4,
        cost_estimate=pl.CostEstimate(flops=2 * 256 * 2048 * 512, bytes_accessed=3 << 20, transcendentals=0),
        name="front",
    )(where, tokens, *received, *blocks)


def gradient_kernel(where_ref, b0, b1, b2, b3, b4, b5, b6, b7, select, grads, out, left):
    @pl.when(pl.program_id(0) == 0)
    def _():
        z = where_ref[2]
        for d, b in enumerate((b0, b1, b2, b3, b4, b5, b6, b7)):
            place = pl.ds(pl.multiple_of(lax.rem(z + 8 - d, 8) * 128, 128), 128)
            left[:, place] = lax.dot_general(
                select[...], b[...], (((1,), (1,)), ((), ())), preferred_element_type=F32
            ).astype(BF16)

    out[...] = jnp.dot(left[...], grads[...], preferred_element_type=F32).astype(out.dtype)


def gradient_rows(where, blocks, select, grads, dtype, name):
    rows = select.shape[0]
    width = 256
    whole = lambda shape: pl.BlockSpec(shape, lambda i, w: (0, 0))
    return pl.pallas_call(
        gradient_kernel,
        grid_spec=pltpu.PrefetchScalarGridSpec(
            num_scalar_prefetch=1,
            grid=(1792 // width,),
            in_specs=[whole((128, 512))] * 8
            + [whole((rows, 512)), pl.BlockSpec((1024, width), lambda i, w: (0, i))],
            out_specs=pl.BlockSpec((rows, width), lambda i, w: (0, i)),
            scratch_shapes=[pltpu.VMEM((rows, 1024), BF16)],
        ),
        out_shape=jax.ShapeDtypeStruct((rows, 1792), dtype),
        cost_estimate=pl.CostEstimate(
            flops=2 * rows * 1024 * 1792, bytes_accessed=6 << 20, transcendentals=0
        ),
        name=name,
    )(where, *blocks, select, grads)


def slots_of(owners, piece_lengths, piece_owners):
    starts = jnp.cumsum(piece_lengths) - piece_lengths
    matches = (piece_owners[None, :] == owners[:, None]).astype(jnp.int32)
    own_start = jnp.sum(matches * starts[None, :], axis=1)
    own_length = jnp.sum(matches * piece_lengths[None, :], axis=1)
    offsets = jnp.arange(48, dtype=jnp.int32)
    rows = own_start[:, None] + offsets[None, :]
    live = offsets[None, :] < own_length[:, None]
    return jnp.where(live, rows, -1).reshape(-1)


def one_hot(rows):
    return (rows[:, None] == jnp.arange(512, dtype=jnp.int32)[None, :]).astype(BF16)


def adam_rows(gradient, live_rows, first_moment, second_moment):
    live_mask = live_rows[:, None]
    new_first = jnp.where(live_mask, beta_one * first_moment + (1.0 - beta_one) * gradient, 0.0)
    new_second = jnp.where(
        live_mask, beta_two * second_moment + (1.0 - beta_two) * gradient * gradient, 0.0
    )
    first_hat = new_first / (1.0 - beta_one**STEP)
    second_hat = new_second / (1.0 - beta_two**STEP)
    update = jnp.where(live_mask, first_hat / (jnp.sqrt(second_hat) + adam_eps), 0.0)
    return (new_first, new_second, update.astype(BF16))


def per_device(
    activations, grad_output, projection, piece_lengths, piece_owners, first_moment, second_moment
):
    tokens = activations[0]
    grads = grad_output[0]
    f = lax.axis_index("fsdp").astype(jnp.int32)
    c = lax.axis_index("tp").astype(jnp.int32)
    y, x, core = f // 4, f // 2 % 2, f % 2
    z, h = c // 2, c % 2
    where = jnp.stack([y, f % 4, z])

    received = [
        fsdp_shift(lax.dynamic_slice(tokens, (0, (y + s) % 4 * 2048), (64, 2048)), s, 0, 0)
        for s in (1, 2, 3)
    ]
    over_x = fsdp_shift(projection, 0, 1, 0)
    over_core = fsdp_shift(projection, 0, 0, 1)
    over_both = fsdp_shift(over_x, 0, 0, 1)
    partial = front(where, tokens, received, (projection, over_core, over_x, over_both))
    total = partial[0]
    for s in (1, 2, 3):
        total = total + fsdp_shift(partial[s], -s, 0, 0)
    projected = total.astype(BF16)

    partner = tp_shift(projected, 0, 1)
    block = jnp.where(
        h == 0,
        jnp.concatenate([projected, partner], axis=0),
        jnp.concatenate([partner, projected], axis=0),
    )
    blocks = [block] + [tp_shift(block, d, 0) for d in range(1, 8)]

    ahead = jnp.stack([(y + dy) % 4 * 4 + (x ^ dx) * 2 for dy, dx in CHIPS])
    behind = jnp.stack([(y - dy) % 4 * 4 + (x ^ dx) * 2 for dy, dx in CHIPS])
    other = 1 - core
    keep_rows = slots_of(ahead + core, piece_lengths, piece_owners)
    give_rows = slots_of(ahead + other, piece_lengths, piece_owners)
    give = gradient_rows(where, blocks, one_hot(give_rows), grads, BF16, "give")
    keep = gradient_rows(where, blocks, one_hot(keep_rows), grads, F32, "keep")
    pair = keep + fsdp_shift(give, 0, 0, 1).astype(F32)
    picked = pair[:48]
    for i, (dy, dx) in enumerate(CHIPS):
        if i:
            piece = pair[48 * i : 48 * i + 48].astype(BF16)
            picked = picked + fsdp_shift(piece, dy, dx, 0).astype(F32)

    new_first, new_second, update = adam_rows(
        picked, keep_rows[:48] >= 0, first_moment, second_moment
    )

    same = one_hot(slots_of(behind + core, piece_lengths, piece_owners))
    cross = one_hot(slots_of(behind + other, piece_lengths, piece_owners))
    over = (((1,), (1,)), ((), ()))
    chosen_same = lax.dot_general(projection, same, over, preferred_element_type=F32).astype(BF16)
    chosen_cross = lax.dot_general(projection, cross, over, preferred_element_type=F32).astype(BF16)
    updates = jnp.concatenate(
        [update] + [fsdp_shift(update, dy, dx, 0) for dy, dx in CHIPS[1:]], axis=0
    )
    crossed = fsdp_shift(updates, 0, 0, 1)
    weight_delta = jnp.dot(chosen_same, updates, preferred_element_type=F32) + jnp.dot(
        chosen_cross, crossed, preferred_element_type=F32
    )
    return (weight_delta.astype(BF16), new_first, new_second)


def solution(mesh):
    return jax.shard_map(
        per_device,
        mesh=mesh,
        in_specs=(
            P("fsdp", "tp", None),
            P("fsdp", None, "tp"),
            P("fsdp", None),
            P(),
            P(),
            P("fsdp", "tp"),
            P("fsdp", "tp"),
        ),
        out_specs=(P("fsdp", "tp"), P("fsdp", "tp"), P("fsdp", "tp")),
        check_vma=False,
    )
```

time: 507 us -> 179 us (0.35)
  waiting for transfers between devices: 458 us -> 90.9 us
  starting transfers between devices: 0.34 us -> 45.4 us
  Pallas kernels: 0 us -> 22.1 us
  matrix products: 27 us -> 8.09 us
  between operations: 13.9 us -> 0.9 us
  other arithmetic: 1.68 us -> 7.46 us
    all_gather x3 -> x0, waiting for transfers between devices: 324 us -> none  [the longest x1 228 us: per_device(): lax.all_gather(own_tokens, 'tp', axis=0, tiled=True)]
    psum x1 -> x0, waiting for transfers between devices: 132 us -> none  [per_device(): summed = lax.psum(gradient, 'fsdp')]
    ppermute x0 -> x33, waiting for transfers between devices: none -> 90.9 us  [the longest x25 70.9 us: fsdp_shift(): return lax.ppermute(value, 'fsdp', pairs)]
    ppermute x0 -> x33, starting transfers between devices: none -> 45.4 us  [the longest x25 27.3 us: fsdp_shift(): return lax.ppermute(value, 'fsdp', pairs)]
    pallas_call x0 -> x3, Pallas kernels: none -> 22.1 us  [the longest x2 18 us: gradient_rows(): pl.pallas_call(gradient_kernel, grid_spec=pltpu.PrefetchScalarGridSpec(nu...]
    dot_general x2, matrix products: 27 us -> 8.09 us  [the longest x1 4.79 us: per_device(): jnp.dot(chosen_same, updates, preferred_element_type=F32)]
    gather x2 -> x0, local copies, waits for them, and re-layouts: 5.56 us -> none  [the longest x1 2.87 us: per_device(): picked = jnp.take(summed, mine_rows, axis=0)]
  transfers between devices with their start and end apart: 4 -> 33, of which waited for: 4 -> 21; matrix products, arithmetic and copies ran while one was open for 1% -> 3% of each run, Pallas kernels for 0% -> 5%
where the time goes in v1:
time: 179 us; the launch traced here: 178 us
  waiting for transfers between devices  90.9 us (51%)
  starting transfers between devices  45.4 us (25%)
  Pallas kernels  22.1 us (12%)
  matrix products  8.09 us (5%)
  other arithmetic  7.46 us (4%)
  local copies, waits for them, and re-layouts  3.6 us (2%)
    ppermute x25, waiting for transfers between devices, fsdp_shift(): return lax.ppermute(value, 'fsdp', pairs)  70.9 us
    ppermute x25, starting transfers between devices, fsdp_shift(): return lax.ppermute(value, 'fsdp', pairs)  27.3 us
    ppermute x8, waiting for transfers between devices, tp_shift(): return lax.ppermute(value, 'tp', pairs)  19.9 us
    ppermute x8, starting transfers between devices, tp_shift(): return lax.ppermute(value, 'tp', pairs)  18.1 us
    pallas_call x2, Pallas kernels, gradient_rows(): pl.pallas_call(gradient_kernel, grid_spec=pltpu.PrefetchScalarGridSpec(nu...  18 us
    dot_general x1, matrix products, per_device(): jnp.dot(chosen_same, updates, preferred_element_type=F32)  4.79 us
    pallas_call x1, Pallas kernels, front(): pl.pallas_call(front_kernel, grid_spec=pltpu.PrefetchScalarGridSpec(num_s...  4.09 us
  transfers between devices with their start and end apart: 33, of which 21 were waited for; matrix products, arithmetic and copies ran while one was open for 3% of the time, Pallas kernels for 5%

profile of v1, /device:TPU:1, one launch (start us, length us, event | category | flops | bytes accessed | tf_op | source)
XLA Modules:
  0.0 178.5 jit_solution(2204788764608682993)
XLA Ops:
  4.1 9.3 %collective-permute-done.4.p2 = bf16[512,512]{1,0:T(8,128)(2,1)S(1)} collective-permute-done((bf16[512,512]{1,0:T(8,128)(2,1)}, bf16[512,512]{1,0:T(8,128)(2,1)S(1)}, u32[]{:S(2)}, u32[]{:S(2)}) %collective-permute-start.4) | collective-permute-done | bytes 524320 | tf_op jit(solution)/shard_map/ppermute | solution.py:25
  17.0 3.1 %collective-permute-start.2 = (bf16[64,2048]{1,0:T(8,128)(2,1)S(1)}, bf16[64,2048]{1,0:T(8,128)(2,1)S(1)}, u32[]{:S(2)}, u32[]{:S(2)}) collective-permute-start(bf16[64,2048]{1,0:T(8,128)(2,1)S(1)} %get-tuple-element.32), channel_id=1, source_target_pairs={{0,12},{1,13},{2,14},{3,15},{4,0},{5,1},{6,2},{7,3},{8,4},{9,5},{1... | collective-permute-start | bytes 786440 | tf_op jit(solution)/shard_map/ppermute | solution.py:25
  22.8 8.3 %collective-permute-done.2.a3 = bf16[64,2048]{1,0:T(8,128)(2,1)S(1)} collective-permute-done((bf16[64,2048]{1,0:T(8,128)(2,1)S(1)}, bf16[64,2048]{1,0:T(8,128)(2,1)S(1)}, u32[]{:S(2)}, u32[]{:S(2)}) %collective-permute-start.2) | collective-permute-done | bytes 262176 | tf_op jit(solution)/shard_map/ppermute | solution.py:25
  34.4 4.1 %front.1 = (f32[64,512]{1,0:T(8,128)}, f32[64,512]{1,0:T(8,128)}, f32[64,512]{1,0:T(8,128)}, f32[64,512]{1,0:T(8,128)}) custom-call(s32[3]{0:T(128)} %pad_add_fusion.where_ref, bf16[64,8192]{1,0:T(8,128)(2,1)} %bitcast.34, bf16[64,2048]{1,0:T(8,128)(2,1)} %copy-done.15, bf16[64,2048]{1,0:T(8,128)(2,1)} %copy-done.16, bf16[64,2048]{1,0:T(8,128)(2,1)} %copy-done.14, ...), custom_call_target="tpu_custom_call" | custom-call | flops 536870912 | bytes 3145728 | tf_op jit(solution)/shard_map/front/pallas_call | solution.py:47
  41.0 2.7 %collective-permute-done.6 = f32[64,512]{1,0:T(8,128)S(1)} collective-permute-done((f32[64,512]{1,0:T(8,128)}, f32[64,512]{1,0:T(8,128)S(1)}, u32[]{:S(2)}, u32[]{:S(2)}) %collective-permute-start.6) | collective-permute-done | bytes 131104 | tf_op jit(solution)/shard_map/ppermute | solution.py:25
  45.6 3.3 %collective-permute-done.8 = f32[64,512]{1,0:T(8,128)S(1)} collective-permute-done((f32[64,512]{1,0:T(8,128)}, f32[64,512]{1,0:T(8,128)S(1)}, u32[]{:S(2)}, u32[]{:S(2)}) %collective-permute-start.8) | collective-permute-done | bytes 131104 | tf_op jit(solution)/shard_map/ppermute | solution.py:25
  49.9 2.8 %collective-permute-start.9 = (bf16[64,512]{1,0:T(8,128)(2,1)S(1)}, bf16[64,512]{1,0:T(8,128)(2,1)S(1)}, u32[]{:S(2)}, u32[]{:S(2)}) collective-permute-start(bf16[64,512]{1,0:T(8,128)(2,1)S(1)} %add_convert_fusion.1), channel_id=1, source_target_pairs={{0,16},{16,0},{32,48},{48,32},{64,80},{80,64},{96,112},{112,96},{1... | collective-permute-start | bytes 196616 | tf_op jit(solution)/shard_map/ppermute | solution.py:30
  54.6 5.6 %collective-permute-start.16 = (bf16[128,512]{1,0:T(8,128)(2,1)S(1)}, bf16[128,512]{1,0:T(8,128)(2,1)S(1)}, u32[]{:S(2)}, u32[]{:S(2)}) collective-permute-start(bf16[128,512]{1,0:T(8,128)(2,1)S(1)} %maximum_select_fusion.b0), channel_id=1, source_target_pairs={{0,224},{16,240},{32,0},{48,16},{64,32},{80,48},{96,64},{112,80},{... | collective-permute-start | bytes 393224 | tf_op jit(solution)/shard_map/ppermute | solution.py:30
  62.1 4.5 %collective-permute-start.13 = (bf16[128,512]{1,0:T(8,128)(2,1)S(1)}, bf16[128,512]{1,0:T(8,128)(2,1)S(1)}, u32[]{:S(2)}, u32[]{:S(2)}) collective-permute-start(bf16[128,512]{1,0:T(8,128)(2,1)S(1)} %maximum_select_fusion.b0), channel_id=1, source_target_pairs={{0,128},{16,144},{32,160},{48,176},{64,192},{80,208},{96,224},{112... | collective-permute-start | bytes 393224 | tf_op jit(solution)/shard_map/ppermute | solution.py:30
  72.3 5.3 %collective-permute-done.12.b3 = bf16[128,512]{1,0:T(8,128)(2,1)S(1)} collective-permute-done((bf16[128,512]{1,0:T(8,128)(2,1)S(1)}, bf16[128,512]{1,0:T(8,128)(2,1)S(1)}, u32[]{:S(2)}, u32[]{:S(2)}) %collective-permute-start.12) | collective-permute-done | bytes 131104 | tf_op jit(solution)/shard_map/ppermute | solution.py:30
  77.6 7.7 %collective-permute-done.11.b2 = bf16[128,512]{1,0:T(8,128)(2,1)S(1)} collective-permute-done((bf16[128,512]{1,0:T(8,128)(2,1)S(1)}, bf16[128,512]{1,0:T(8,128)(2,1)S(1)}, u32[]{:S(2)}, u32[]{:S(2)}) %collective-permute-start.11) | collective-permute-done | bytes 131104 | tf_op jit(solution)/shard_map/ppermute | solution.py:30
  85.3 4.1 %collective-permute-done.10.b1 = bf16[128,512]{1,0:T(8,128)(2,1)S(1)} collective-permute-done((bf16[128,512]{1,0:T(8,128)(2,1)S(1)}, bf16[128,512]{1,0:T(8,128)(2,1)S(1)}, u32[]{:S(2)}, u32[]{:S(2)}) %collective-permute-start.10) | collective-permute-done | bytes 131104 | tf_op jit(solution)/shard_map/ppermute | solution.py:30
  90.0 8.9 %give.1 = bf16[384,1792]{1,0:T(8,128)(2,1)} custom-call(s32[3]{0:T(128)} %pad_add_fusion.where_ref, bf16[128,512]{1,0:T(8,128)(2,1)} %copy-done.1, bf16[128,512]{1,0:T(8,128)(2,1)} %copy-done.8, bf16[128,512]{1,0:T(8,128)(2,1)} %copy-done.7, bf16[128,512]{1,0:T(8,128)(2,1)} %copy-done.6, bf16[128,512]{1,0:T(8,128)(2,1)} %copy-done.5, ...), custom_call_target="tpu_custom_call" | custom-call | flops 1409286144 | bytes 6291456 | tf_op jit(solution)/shard_map/give/pallas_call | solution.py:80
  102.0 9.2 %keep.1 = f32[384,1792]{1,0:T(8,128)} custom-call(s32[3]{0:T(128)} %pad_add_fusion.where_ref, bf16[128,512]{1,0:T(8,128)(2,1)} %copy-done.1, bf16[128,512]{1,0:T(8,128)(2,1)} %copy-done.8, bf16[128,512]{1,0:T(8,128)(2,1)} %copy-done.7, bf16[128,512]{1,0:T(8,128)(2,1)} %copy-done.6, bf16[128,512]{1,0:T(8,128)(2,1)} %copy-done.5, bf16[128,512]{1,0:T(8,128)(2,1)} %copy-done.4, ...), custom_call_target="tpu_custom_call" | custom-call | flops 1409286144 | bytes 6291456 | tf_op jit(solution)/shard_map/keep/pallas_call | solution.py:80
  115.0 3.8 %collective-permute-start.22 = (bf16[48,1792]{1,0:T(8,128)(2,1)S(1)}, bf16[48,1792]{1,0:T(8,128)(2,1)S(1)}, u32[]{:S(2)}, u32[]{:S(2)}) collective-permute-start(bf16[48,1792]{1,0:T(8,128)(2,1)S(1)} %get-tuple-element.28), channel_id=1, source_target_pairs={{0,10},{1,11},{2,8},{3,9},{4,14},{5,15},{6,12},{7,13},{8,2},{9,3},... | collective-permute-start | bytes 516104 | tf_op jit(solution)/shard_map/ppermute | solution.py:25
  120.0 3.6 %collective-permute-done.24 = bf16[48,1792]{1,0:T(8,128)(2,1)S(1)} collective-permute-done((bf16[48,1792]{1,0:T(8,128)(2,1)S(1)}, bf16[48,1792]{1,0:T(8,128)(2,1)S(1)}, u32[]{:S(2)}, u32[]{:S(2)}) %collective-permute-start.24) | collective-permute-done | bytes 172064 | tf_op jit(solution)/shard_map/ppermute | solution.py:25
  123.5 4.1 %collective-permute-done.23 = bf16[48,1792]{1,0:T(8,128)(2,1)S(1)} collective-permute-done((bf16[48,1792]{1,0:T(8,128)(2,1)S(1)}, bf16[48,1792]{1,0:T(8,128)(2,1)S(1)}, u32[]{:S(2)}, u32[]{:S(2)}) %collective-permute-start.23) | collective-permute-done | bytes 172064 | tf_op jit(solution)/shard_map/ppermute | solution.py:25
  128.2 5.3 %collective-permute-done.21 = bf16[48,1792]{1,0:T(8,128)(2,1)S(1)} collective-permute-done((bf16[48,1792]{1,0:T(8,128)(2,1)S(1)}, bf16[48,1792]{1,0:T(8,128)(2,1)S(1)}, u32[]{:S(2)}, u32[]{:S(2)}) %collective-permute-start.21) | collective-permute-done | bytes 172064 | tf_op jit(solution)/shard_map/ppermute | solution.py:25
  133.5 4.1 %collective-permute-done.19 = bf16[48,1792]{1,0:T(8,128)(2,1)S(1)} collective-permute-done((bf16[48,1792]{1,0:T(8,128)(2,1)S(1)}, bf16[48,1792]{1,0:T(8,128)(2,1)S(1)}, u32[]{:S(2)}, u32[]{:S(2)}) %collective-permute-start.19) | collective-permute-done | bytes 172064 | tf_op jit(solution)/shard_map/ppermute | solution.py:25
  140.5 2.8 %collective-permute-start.29 = (bf16[48,1792]{1,0:T(8,128)(2,1)S(1)}, bf16[48,1792]{1,0:T(8,128)(2,1)S(1)}, u32[]{:S(2)}, u32[]{:S(2)}) collective-permute-start(bf16[48,1792]{1,0:T(8,128)(2,1)S(1)} %get-tuple-element.20), channel_id=1, source_target_pairs={{0,10},{1,11},{2,8},{3,9},{4,14},{5,15},{6,12},{7,13},{8,2},{9,3},... | collective-permute-start | bytes 516104 | tf_op jit(solution)/shard_map/ppermute | solution.py:25
  144.5 13.9 %collective-permute-done.26 = bf16[48,1792]{1,0:T(8,128)(2,1)S(1)} collective-permute-done((bf16[48,1792]{1,0:T(8,128)(2,1)S(1)}, bf16[48,1792]{1,0:T(8,128)(2,1)S(1)}, u32[]{:S(2)}, u32[]{:S(2)}) %collective-permute-start.26) | collective-permute-done | bytes 172064 | tf_op jit(solution)/shard_map/ppermute | solution.py:25
  158.5 7.5 %collective-permute-done.27 = bf16[48,1792]{1,0:T(8,128)(2,1)S(1)} collective-permute-done((bf16[48,1792]{1,0:T(8,128)(2,1)S(1)}, bf16[48,1792]{1,0:T(8,128)(2,1)S(1)}, u32[]{:S(2)}, u32[]{:S(2)}) %collective-permute-start.27) | collective-permute-done | bytes 172064 | tf_op jit(solution)/shard_map/ppermute | solution.py:25
  170.4 3.3 %fusion = f32[512,1792]{1,0:T(8,128)} fusion(bf16[384,1792]{1,0:T(8,128)(2,1)S(1)} %collective-permute-done.32, bf16[512,512]{1,0:T(8,128)(2,1)S(1)} %copy-done, s32[384]{0:T(512)S(1)} %select_n.178), kind=kOutput, calls=%fused_computation.4 | convolution fusion | flops 906362880 | bytes 5572096 | tf_op jit(solution)/shard_map/dot_general | solution.py:184
  173.7 4.8 %add_convert_fusion = bf16[512,1792]{1,0:T(8,128)(2,1)} fusion(f32[512,1792]{1,0:T(8,128)} %fusion, bf16[384,1792]{1,0:T(8,128)(2,1)S(1)} %constant_dynamic-update-slice_fusion, bf16[512,512]{1,0:T(8,128)(2,1)S(1)} %copy-done, s32[384]{0:T(512)S(1)} %select_n.158), kind=kOutput, calls=%fused_computation | convolution fusion | flops 908197888 | bytes 7407104 | tf_op jit(solution)/shard_map/dot_general | solution.py:184
  (118 shorter events, 45.5 us)
Async XLA Ops:
  0.6 12.8 %collective-permute-start.4 = (bf16[512,512]{1,0:T(8,128)(2,1)}, bf16[512,512]{1,0:T(8,128)(2,1)S(1)}, u32[]{:S(2)}, u32[]{:S(2)}) collective-permute-start(bf16[512,512]{1,0:T(8,128)(2,1)} %p0.1), channel_id=1, source_target_pairs={{0,2},{1,3},{2,0},{3,1},{4,6},{5,7},{6,4},{7,5},{8,10},{9,11},{10,... | collective-permute-start | bytes 1572872 | tf_op jit(solution)/shard_map/ppermute | solution.py:25
  2.8 30.6 %collective-permute-start.3 = (bf16[512,512]{1,0:T(8,128)(2,1)}, bf16[512,512]{1,0:T(8,128)(2,1)S(1)}, u32[]{:S(2)}, u32[]{:S(2)}) collective-permute-start(bf16[512,512]{1,0:T(8,128)(2,1)} %p0.1), channel_id=1, source_target_pairs={{0,1},{1,0},{2,3},{3,2},{4,5},{5,4},{6,7},{7,6},{8,9},{9,8},{10,11... | collective-permute-start | bytes 1572872 | tf_op jit(solution)/shard_map/ppermute | solution.py:25
  13.4 19.9 %collective-permute-start.5 = (bf16[512,512]{1,0:T(8,128)(2,1)S(1)}, bf16[512,512]{1,0:T(8,128)(2,1)S(1)}, u32[]{:S(2)}, u32[]{:S(2)}) collective-permute-start(bf16[512,512]{1,0:T(8,128)(2,1)S(1)} %collective-permute-done.4.p2), channel_id=1, source_target_pairs={{0,1},{1,0},{2,3},{3,2},{4,5},{5,4},{6,7},{7,6},{8,9},{9,8},{10,11... | collective-permute-start | bytes 1572872 | tf_op jit(solution)/shard_map/ppermute | solution.py:25
  17.0 14.1 %collective-permute-start.2 = (bf16[64,2048]{1,0:T(8,128)(2,1)S(1)}, bf16[64,2048]{1,0:T(8,128)(2,1)S(1)}, u32[]{:S(2)}, u32[]{:S(2)}) collective-permute-start(bf16[64,2048]{1,0:T(8,128)(2,1)S(1)} %get-tuple-element.32), channel_id=1, source_target_pairs={{0,12},{1,13},{2,14},{3,15},{4,0},{5,1},{6,2},{7,3},{8,4},{9,5},{1... | collective-permute-start | bytes 786440 | tf_op jit(solution)/shard_map/ppermute | solution.py:25
  20.1 11.0 %collective-permute-start = (bf16[64,2048]{1,0:T(8,128)(2,1)S(1)}, bf16[64,2048]{1,0:T(8,128)(2,1)S(1)}, u32[]{:S(2)}, u32[]{:S(2)}) collective-permute-start(bf16[64,2048]{1,0:T(8,128)(2,1)S(1)} %get-tuple-element.33), channel_id=1, source_target_pairs={{0,4},{1,5},{2,6},{3,7},{4,8},{5,9},{6,10},{7,11},{8,12},{9,13},{1... | collective-permute-start | bytes 786440 | tf_op jit(solution)/shard_map/ppermute | solution.py:25
  20.1 13.2 %collective-permute-start.1 = (bf16[64,2048]{1,0:T(8,128)(2,1)S(1)}, bf16[64,2048]{1,0:T(8,128)(2,1)S(1)}, u32[]{:S(2)}, u32[]{:S(2)}) collective-permute-start(bf16[64,2048]{1,0:T(8,128)(2,1)S(1)} %get-tuple-element.34), channel_id=1, source_target_pairs={{0,8},{1,9},{2,10},{3,11},{4,12},{5,13},{6,14},{7,15},{8,0},{9,1},... | collective-permute-start | bytes 786440 | tf_op jit(solution)/shard_map/ppermute | solution.py:25
  54.6 11.9 %collective-permute-start.16 = (bf16[128,512]{1,0:T(8,128)(2,1)S(1)}, bf16[128,512]{1,0:T(8,128)(2,1)S(1)}, u32[]{:S(2)}, u32[]{:S(2)}) collective-permute-start(bf16[128,512]{1,0:T(8,128)(2,1)S(1)} %maximum_select_fusion.b0), channel_id=1, source_target_pairs={{0,224},{16,240},{32,0},{48,16},{64,32},{80,48},{96,64},{112,80},{... | collective-permute-start | bytes 393224 | tf_op jit(solution)/shard_map/ppermute | solution.py:30
  61.6 10.7 %collective-permute-start.14 = (bf16[128,512]{1,0:T(8,128)(2,1)S(1)}, bf16[128,512]{1,0:T(8,128)(2,1)S(1)}, u32[]{:S(2)}, u32[]{:S(2)}) collective-permute-start(bf16[128,512]{1,0:T(8,128)(2,1)S(1)} %maximum_select_fusion.b0), channel_id=1, source_target_pairs={{0,160},{16,176},{32,192},{48,208},{64,224},{80,240},{96,0},{112,1... | collective-permute-start | bytes 393224 | tf_op jit(solution)/shard_map/ppermute | solution.py:30
  62.1 10.2 %collective-permute-start.13 = (bf16[128,512]{1,0:T(8,128)(2,1)S(1)}, bf16[128,512]{1,0:T(8,128)(2,1)S(1)}, u32[]{:S(2)}, u32[]{:S(2)}) collective-permute-start(bf16[128,512]{1,0:T(8,128)(2,1)S(1)} %maximum_select_fusion.b0), channel_id=1, source_target_pairs={{0,128},{16,144},{32,160},{48,176},{64,192},{80,208},{96,224},{112... | collective-permute-start | bytes 393224 | tf_op jit(solution)/shard_map/ppermute | solution.py:30
  66.6 11.0 %collective-permute-start.12 = (bf16[128,512]{1,0:T(8,128)(2,1)S(1)}, bf16[128,512]{1,0:T(8,128)(2,1)S(1)}, u32[]{:S(2)}, u32[]{:S(2)}) collective-permute-start(bf16[128,512]{1,0:T(8,128)(2,1)S(1)} %maximum_select_fusion.b0), channel_id=1, source_target_pairs={{0,96},{16,112},{32,128},{48,144},{64,160},{80,176},{96,192},{112,... | collective-permute-start | bytes 393224 | tf_op jit(solution)/shard_map/ppermute | solution.py:30
  66.6 18.7 %collective-permute-start.11 = (bf16[128,512]{1,0:T(8,128)(2,1)S(1)}, bf16[128,512]{1,0:T(8,128)(2,1)S(1)}, u32[]{:S(2)}, u32[]{:S(2)}) collective-permute-start(bf16[128,512]{1,0:T(8,128)(2,1)S(1)} %maximum_select_fusion.b0), channel_id=1, source_target_pairs={{0,64},{16,80},{32,96},{48,112},{64,128},{80,144},{96,160},{112,17... | collective-permute-start | bytes 393224 | tf_op jit(solution)/shard_map/ppermute | solution.py:30
  68.8 20.6 %collective-permute-start.10 = (bf16[128,512]{1,0:T(8,128)(2,1)S(1)}, bf16[128,512]{1,0:T(8,128)(2,1)S(1)}, u32[]{:S(2)}, u32[]{:S(2)}) collective-permute-start(bf16[128,512]{1,0:T(8,128)(2,1)S(1)} %maximum_select_fusion.b0), channel_id=1, source_target_pairs={{0,32},{16,48},{32,64},{48,80},{64,96},{80,112},{96,128},{112,144}... | collective-permute-start | bytes 393224 | tf_op jit(solution)/shard_map/ppermute | solution.py:30
  98.9 12.3 %collective-permute-start.17 = (bf16[384,1792]{1,0:T(8,128)(2,1)}, bf16[384,1792]{1,0:T(8,128)(2,1)S(1)}, u32[]{:S(2)}, u32[]{:S(2)}) collective-permute-start(bf16[384,1792]{1,0:T(8,128)(2,1)} %give.1), channel_id=1, source_target_pairs={{0,1},{1,0},{2,3},{3,2},{4,5},{5,4},{6,7},{7,6},{8,9},{9,8},{10,11... | collective-permute-start | bytes 4128776 | tf_op jit(solution)/shard_map/ppermute | solution.py:25
  114.6 8.9 %collective-permute-start.24 = (bf16[48,1792]{1,0:T(8,128)(2,1)S(1)}, bf16[48,1792]{1,0:T(8,128)(2,1)S(1)}, u32[]{:S(2)}, u32[]{:S(2)}) collective-permute-start(bf16[48,1792]{1,0:T(8,128)(2,1)S(1)} %get-tuple-element.26), channel_id=1, source_target_pairs={{0,14},{1,15},{2,12},{3,13},{4,2},{5,3},{6,0},{7,1},{8,6},{9,7},{1... | collective-permute-start | bytes 516104 | tf_op jit(solution)/shard_map/ppermute | solution.py:25
  114.6 13.1 %collective-permute-start.23 = (bf16[48,1792]{1,0:T(8,128)(2,1)S(1)}, bf16[48,1792]{1,0:T(8,128)(2,1)S(1)}, u32[]{:S(2)}, u32[]{:S(2)}) collective-permute-start(bf16[48,1792]{1,0:T(8,128)(2,1)S(1)} %get-tuple-element.27), channel_id=1, source_target_pairs={{0,12},{1,13},{2,14},{3,15},{4,0},{5,1},{6,2},{7,3},{8,4},{9,5},{1... | collective-permute-start | bytes 516104 | tf_op jit(solution)/shard_map/ppermute | solution.py:25
  115.0 13.2 %collective-permute-start.22 = (bf16[48,1792]{1,0:T(8,128)(2,1)S(1)}, bf16[48,1792]{1,0:T(8,128)(2,1)S(1)}, u32[]{:S(2)}, u32[]{:S(2)}) collective-permute-start(bf16[48,1792]{1,0:T(8,128)(2,1)S(1)} %get-tuple-element.28), channel_id=1, source_target_pairs={{0,10},{1,11},{2,8},{3,9},{4,14},{5,15},{6,12},{7,13},{8,2},{9,3},... | collective-permute-start | bytes 516104 | tf_op jit(solution)/shard_map/ppermute | solution.py:25
  118.8 14.8 %collective-permute-start.21 = (bf16[48,1792]{1,0:T(8,128)(2,1)S(1)}, bf16[48,1792]{1,0:T(8,128)(2,1)S(1)}, u32[]{:S(2)}, u32[]{:S(2)}) collective-permute-start(bf16[48,1792]{1,0:T(8,128)(2,1)S(1)} %get-tuple-element.29), channel_id=1, source_target_pairs={{0,8},{1,9},{2,10},{3,11},{4,12},{5,13},{6,14},{7,15},{8,0},{9,1},... | collective-permute-start | bytes 516104 | tf_op jit(solution)/shard_map/ppermute | solution.py:25
  119.4 14.1 %collective-permute-start.20 = (bf16[48,1792]{1,0:T(8,128)(2,1)S(1)}, bf16[48,1792]{1,0:T(8,128)(2,1)S(1)}, u32[]{:S(2)}, u32[]{:S(2)}) collective-permute-start(bf16[48,1792]{1,0:T(8,128)(2,1)S(1)} %get-tuple-element.30), channel_id=1, source_target_pairs={{0,6},{1,7},{2,4},{3,5},{4,10},{5,11},{6,8},{7,9},{8,14},{9,15},{1... | collective-permute-start | bytes 516104 | tf_op jit(solution)/shard_map/ppermute | solution.py:25
  123.5 14.1 %collective-permute-start.19 = (bf16[48,1792]{1,0:T(8,128)(2,1)S(1)}, bf16[48,1792]{1,0:T(8,128)(2,1)S(1)}, u32[]{:S(2)}, u32[]{:S(2)}) collective-permute-start(bf16[48,1792]{1,0:T(8,128)(2,1)S(1)} %get-tuple-element.31), channel_id=1, source_target_pairs={{0,4},{1,5},{2,6},{3,7},{4,8},{5,9},{6,10},{7,11},{8,12},{9,13},{1... | collective-permute-start | bytes 516104 | tf_op jit(solution)/shard_map/ppermute | solution.py:25
  139.2 27.0 %collective-permute-start.31 = (bf16[48,1792]{1,0:T(8,128)(2,1)S(1)}, bf16[48,1792]{1,0:T(8,128)(2,1)S(1)}, u32[]{:S(2)}, u32[]{:S(2)}) collective-permute-start(bf16[48,1792]{1,0:T(8,128)(2,1)S(1)} %get-tuple-element.20), channel_id=1, source_target_pairs={{0,14},{1,15},{2,12},{3,13},{4,2},{5,3},{6,0},{7,1},{8,6},{9,7},{1... | collective-permute-start | bytes 516104 | tf_op jit(solution)/shard_map/ppermute | solution.py:25
  139.9 26.2 %collective-permute-start.30 = (bf16[48,1792]{1,0:T(8,128)(2,1)S(1)}, bf16[48,1792]{1,0:T(8,128)(2,1)S(1)}, u32[]{:S(2)}, u32[]{:S(2)}) collective-permute-start(bf16[48,1792]{1,0:T(8,128)(2,1)S(1)} %get-tuple-element.20), channel_id=1, source_target_pairs={{0,12},{1,13},{2,14},{3,15},{4,0},{5,1},{6,2},{7,3},{8,4},{9,5},{1... | collective-permute-start | bytes 516104 | tf_op jit(solution)/shard_map/ppermute | solution.py:25
  140.5 25.6 %collective-permute-start.29 = (bf16[48,1792]{1,0:T(8,128)(2,1)S(1)}, bf16[48,1792]{1,0:T(8,128)(2,1)S(1)}, u32[]{:S(2)}, u32[]{:S(2)}) collective-permute-start(bf16[48,1792]{1,0:T(8,128)(2,1)S(1)} %get-tuple-element.20), channel_id=1, source_target_pairs={{0,10},{1,11},{2,8},{3,9},{4,14},{5,15},{6,12},{7,13},{8,2},{9,3},... | collective-permute-start | bytes 516104 | tf_op jit(solution)/shard_map/ppermute | solution.py:25
  143.3 22.8 %collective-permute-start.28 = (bf16[48,1792]{1,0:T(8,128)(2,1)S(1)}, bf16[48,1792]{1,0:T(8,128)(2,1)S(1)}, u32[]{:S(2)}, u32[]{:S(2)}) collective-permute-start(bf16[48,1792]{1,0:T(8,128)(2,1)S(1)} %get-tuple-element.20), channel_id=1, source_target_pairs={{0,8},{1,9},{2,10},{3,11},{4,12},{5,13},{6,14},{7,15},{8,0},{9,1},... | collective-permute-start | bytes 516104 | tf_op jit(solution)/shard_map/ppermute | solution.py:25
  144.3 14.1 %collective-permute-start.26 = (bf16[48,1792]{1,0:T(8,128)(2,1)S(1)}, bf16[48,1792]{1,0:T(8,128)(2,1)S(1)}, u32[]{:S(2)}, u32[]{:S(2)}) collective-permute-start(bf16[48,1792]{1,0:T(8,128)(2,1)S(1)} %get-tuple-element.20), channel_id=1, source_target_pairs={{0,4},{1,5},{2,6},{3,7},{4,8},{5,9},{6,10},{7,11},{8,12},{9,13},{1... | collective-permute-start | bytes 516104 | tf_op jit(solution)/shard_map/ppermute | solution.py:25
  (28 other events, 332.0 us)

commit v2 on v0

v2 whole, which is shorter than its diff:
```python
import functools

import jax
import jax.numpy as jnp
from jax import lax
from jax.experimental import pallas as pl
from jax.experimental.pallas import tpu as pltpu
from jax.sharding import PartitionSpec as P

STEP = 10
beta_one = 0.9
beta_two = 0.999
adam_eps = 1e-08

F32 = jnp.float32
BF16 = jnp.bfloat16

CHIP_GROUPS = [[2 * chip + core for chip in range(8)] for core in range(2)]
FF = 1792
VMEM = pltpu.VMEM


def fsdp_flip(value, flip):
    return lax.ppermute(value, "fsdp", [(i, i ^ flip) for i in range(16)])


def y_shift(value, dy):
    return lax.ppermute(value, "fsdp", [(i, (i + 4 * dy) % 16) for i in range(16)])


def tp_shift(value, dz, dh):
    pairs = [(i, ((i // 2 + dz) % 8) * 2 + ((i % 2) ^ dh)) for i in range(16)]
    return lax.ppermute(value, "tp", pairs)


SCALARS = pl.BlockSpec(memory_space=pltpu.SMEM)


def in_vmem(count):
    return [pl.BlockSpec(memory_space=VMEM)] * count


def local_call(kernel, name, out_shape, operands, flops, scratch=(), limit=24, aliases=None):
    size = sum(v.size * v.dtype.itemsize for v in operands)
    return pl.pallas_call(
        kernel,
        in_specs=[SCALARS] + in_vmem(len(operands) - 1),
        out_specs=in_vmem(len(out_shape)),
        out_shape=out_shape,
        scratch_shapes=scratch,
        input_output_aliases=aliases or {},
        cost_estimate=pl.CostEstimate(flops=flops, bytes_accessed=size, transcendentals=0),
        compiler_params=pltpu.CompilerParams(vmem_limit_bytes=limit << 20),
        name=name,
    )(*operands)


def front_kernel(where, a0, a1, a2, a3, p0, p1, p2, p3, o0, o1, o2, o3):
    low = where[0]
    total = None
    for r, p in enumerate((p0, p1, p2, p3)):
        columns = pl.ds(pl.multiple_of((low ^ r) * 512, 512), 512)
        rows = jnp.concatenate([a[:, columns] for a in (a0, a1, a2, a3)], axis=0)
        term = jnp.dot(rows, p[...], preferred_element_type=F32)
        total = term if total is None else total + term
    for i, o in enumerate((o0, o1, o2, o3)):
        o[...] = total[i * 64 : (i + 1) * 64]


def total_kernel(_, a, b, c, d, out):
    out[...] = (a[...] + b[...] + c[...] + d[...]).astype(BF16)


def join_kernel(where, mine, partner, out):
    first = where[20] == 0
    here, there = mine[...].astype(F32), partner[...].astype(F32)
    rows = jnp.concatenate(
        [jnp.where(first, here, there), jnp.where(first, there, here)], axis=0
    )
    out[...] = rows.T.astype(BF16)


def token_rows(where, grads, offset):
    row = lax.rem(where[1] + offset, 8) * 128
    return grads[pl.ds(pl.multiple_of(row, 128), 128), :]


def sum_kernel(offsets, where, *refs):
    count = len(offsets)
    blocks, grads, rest, out = refs[:count], refs[count], refs[count + 1 : -1], refs[-1]
    left = jnp.concatenate([b[...] for b in blocks], axis=1)
    right = jnp.concatenate([token_rows(where, grads, o) for o in offsets], axis=0)
    total = jnp.dot(left, right, preferred_element_type=F32)
    for before in rest:
        total = total + before[...]
    out[...] = total


def rows_from(table, start):
    low = lax.rem(start, 8)
    rows = table[pl.ds(pl.multiple_of(start - low, 8), 56), :]
    return pltpu.roll(rows, lax.rem(56 - low, 56), 0)[:48]


def last_kernel(offsets, where, *refs):
    give, keep, table = refs[-3:]
    table[512:560, :] = jnp.zeros((48, FF), F32)
    sum_kernel(offsets, where, *refs[:-3], table.at[0:512, :])
    core = where[2]
    for i in range(8):
        give[i] = rows_from(table, where[4 + 2 * i + 1 - core]).astype(give.dtype)
        keep[i] = rows_from(table, where[4 + 2 * i + core]).astype(keep.dtype)


def half_delta_kernel(_, chosen, updates, out):
    out[...] = jnp.dot(chosen[...], updates[...], preferred_element_type=F32)


def delta_kernel(_, chosen, updates, before, out):
    product = jnp.dot(chosen[...], updates[...], preferred_element_type=F32)
    out[...] = (before[...] + product).astype(BF16)


def moments_kernel(where, terms, first, second, new_first, new_second, spread):
    live = lax.broadcasted_iota(jnp.int32, (48, FF), 0) < where[3]
    gradient = terms[0].astype(F32)
    for i in range(1, 8):
        gradient = gradient + terms[i].astype(F32)
    one, two, update = adam_rows(gradient, live, first[...], second[...])
    new_first[...] = one
    new_second[...] = two
    for i in range(8):
        spread[i] = update


def adam_rows(gradient, live_mask, first_moment, second_moment):
    new_first = jnp.where(live_mask, beta_one * first_moment + (1.0 - beta_one) * gradient, 0.0)
    new_second = jnp.where(
        live_mask, beta_two * second_moment + (1.0 - beta_two) * gradient * gradient, 0.0
    )
    first_hat = new_first / (1.0 - beta_one**STEP)
    second_hat = new_second / (1.0 - beta_two**STEP)
    update = jnp.where(live_mask, first_hat / (jnp.sqrt(second_hat) + adam_eps), 0.0)
    return (new_first, new_second, update.astype(BF16))


def per_device(
    activations, grad_output, projection, piece_lengths, piece_owners, first_moment, second_moment
):
    tokens = activations[0]
    grads = grad_output[0]
    f = lax.axis_index("fsdp").astype(jnp.int32)
    c = lax.axis_index("tp").astype(jnp.int32)
    y, core = f // 4, f % 2
    z, h = c // 2, c % 2

    owner_order = jnp.arange(16, dtype=jnp.int32)
    starts = jnp.cumsum(piece_lengths) - piece_lengths
    matches = (piece_owners[None, :] == owner_order[:, None]).astype(jnp.int32)
    own_start = jnp.sum(matches * starts[None, :], axis=1)
    own_length = jnp.sum(matches * piece_lengths[None, :], axis=1)
    mine = jnp.sum(jnp.where(owner_order == f, own_length, 0))
    where = jnp.concatenate([jnp.stack([f % 4, z, core, mine]), own_start, h[None]]).astype(jnp.int32)
    offsets = jnp.arange(48, dtype=jnp.int32)
    rows = own_start[:, None] + offsets[None, :]
    live = offsets[None, :] < own_length[:, None]

    slices = [lax.dynamic_slice(tokens, (0, (y + s) % 4 * 2048), (64, 2048)) for s in range(4)]
    slices[1], slices[2], slices[3], block = lax.optimization_barrier(
        (slices[1], slices[2], slices[3], projection)
    )
    for s in (1, 3, 2):
        slices[s] = y_shift(slices[s], s)
    over_x = fsdp_flip(block, 2)
    over_core = fsdp_flip(block, 1)
    over_both = fsdp_flip(over_x, 1)

    over = (((1,), (1,)), ((), ()))

    def chosen_of(side):
        marks = jnp.where(live, rows, -1).reshape(8, 2, 48)
        marks = jnp.where(side == 0, marks[:, 0], marks[:, 1]).reshape(-1)
        hot = (marks[:, None] == jnp.arange(512, dtype=jnp.int32)[None, :]).astype(BF16)
        return lax.dot_general(projection, hot, over, preferred_element_type=F32).astype(BF16)

    same, cross = chosen_of(core), chosen_of(1 - core)
    same, cross, where, slices[2] = lax.optimization_barrier((same, cross, where, slices[2]))
    partial = local_call(
        front_kernel,
        "front",
        [jax.ShapeDtypeStruct((64, 512), F32)] * 4,
        (where, *slices, block, over_core, over_x, over_both),
        2 * 256 * 2048 * 512,
    )
    (projected,) = local_call(
        total_kernel,
        "total",
        [jax.ShapeDtypeStruct((64, 512), BF16)],
        (where, partial[0], *[y_shift(partial[s], -s) for s in (1, 3, 2)]),
        64 * 512 * 4,
        limit=4,
    )

    (own,) = local_call(
        join_kernel,
        "join",
        [jax.ShapeDtypeStruct((512, 128), BF16)],
        (where, projected, tp_shift(projected, 0, 1)),
        64 * 512 * 4,
        limit=4,
    )
    up1, down1 = tp_shift(own, 1, 0), tp_shift(own, -1, 0)
    up2, down2 = tp_shift(own, 2, 0), tp_shift(own, -2, 0)
    far = tp_shift(own, 4, 0)
    up3, down3 = tp_shift(up2, 1, 0), tp_shift(down2, -1, 0)
    table = [jax.ShapeDtypeStruct((512, FF), F32)]
    one = 2 * 512 * 128 * FF
    (gradient,) = local_call(
        functools.partial(sum_kernel, (0, 7, 1)),
        "near_terms",
        table,
        (where, own, up1, down1, grads),
        3 * one,
    )
    (gradient,) = local_call(
        functools.partial(sum_kernel, (6, 2, 4)),
        "far_terms",
        table,
        (where, up2, down2, far, grads, gradient),
        3 * one,
        aliases={5: 0},
    )
    give, keep = local_call(
        functools.partial(last_kernel, (5, 3)),
        "last_terms",
        [jax.ShapeDtypeStruct((8, 48, FF), BF16), jax.ShapeDtypeStruct((8, 48, FF), F32)],
        (where, up3, down3, grads, gradient),
        2 * one,
        scratch=[pltpu.VMEM((560, FF), F32)],
    )
    pair = (keep + fsdp_flip(give, 1).astype(F32)).astype(BF16)
    terms = lax.all_to_all(pair, "fsdp", 0, 0, axis_index_groups=CHIP_GROUPS)
    new_first, new_second, spread = local_call(
        moments_kernel,
        "moments",
        [
            jax.ShapeDtypeStruct((48, FF), F32),
            jax.ShapeDtypeStruct((48, FF), F32),
            jax.ShapeDtypeStruct((8, 48, FF), BF16),
        ],
        (where, terms, first_moment, second_moment),
        48 * FF * 30,
    )
    updates = lax.all_to_all(spread, "fsdp", 0, 0, axis_index_groups=CHIP_GROUPS)
    updates = updates.reshape(384, FF)
    crossed = fsdp_flip(updates, 1)
    (half,) = local_call(
        half_delta_kernel, "half_delta", table, (where, same, updates), 2 * 512 * 384 * FF
    )
    (weight_delta,) = local_call(
        delta_kernel,
        "delta",
        [jax.ShapeDtypeStruct((512, FF), BF16)],
        (where, cross, crossed, half),
        2 * 512 * 384 * FF,
    )
    return (weight_delta, new_first, new_second)


def solution(mesh):
    return jax.shard_map(
        per_device,
        mesh=mesh,
        in_specs=(
            P("fsdp", "tp", None),
            P("fsdp", None, "tp"),
            P("fsdp", None),
            P(),
            P(),
            P("fsdp", "tp"),
            P("fsdp", "tp"),
        ),
        out_specs=(P("fsdp", "tp"), P("fsdp", "tp"), P("fsdp", "tp")),
        check_vma=False,
    )
```

time: 507 us -> 128 us (0.25)
  waiting for transfers between devices: 458 us -> 23.8 us
  blocking collectives: 0 us -> 42.1 us
  starting transfers between devices: 0.34 us -> 40.1 us
  matrix products: 27 us -> 1.15 us
  Pallas kernels: 0 us -> 15.6 us
  between operations: 13.9 us -> 0.9 us
    all_gather x3 -> x0, waiting for transfers between devices: 324 us -> none  [the longest x1 228 us: per_device(): lax.all_gather(own_tokens, 'tp', axis=0, tiled=True)]
    psum x1 -> x0, waiting for transfers between devices: 132 us -> none  [per_device(): summed = lax.psum(gradient, 'fsdp')]
    all_to_all x0 -> x2, blocking collectives: none -> 42.1 us  [the longest x1 21.3 us: per_device(): terms = lax.all_to_all(pair, 'fsdp', 0, 0, axis_index_groups=CHIP_GROUPS)]
    ppermute x0 -> x19, starting transfers between devices: none -> 40.1 us  [the longest x8 16.7 us: tp_shift(): return lax.ppermute(value, 'tp', pairs)]
    dot_general x2, matrix products: 27 us -> 1.15 us  [chosen_of(): lax.dot_general(projection, hot, over, preferred_element_type=F32)]
    ppermute x0 -> x19, waiting for transfers between devices: none -> 23.8 us  [the longest x6 8.87 us: y_shift(): lax.ppermute(value, 'fsdp', [(i, (i + 4 * dy) % 16) for i in range(16)])]
    pallas_call x0 -> x9, Pallas kernels: none -> 15.6 us  [local_call(): pl.pallas_call(kernel, in_specs=[SCALARS] + in_vmem(len(operands) - 1), o...]
    gather x2 -> x0, local copies, waits for them, and re-layouts: 5.56 us -> none  [the longest x1 2.87 us: per_device(): picked = jnp.take(summed, mine_rows, axis=0)]
  transfers between devices with their start and end apart: 4 -> 19, of which waited for: 4 -> 11; matrix products, arithmetic and copies ran while one was open for 1% -> 3% of each run, Pallas kernels for 0% -> 4%
where the time goes in v2:
time: 128 us
  blocking collectives  42.1 us (33%)
  starting transfers between devices  40.1 us (31%)
  waiting for transfers between devices  23.8 us (19%)
  Pallas kernels  15.6 us (12%)
  local copies, waits for them, and re-layouts  3.21 us (3%)
  other arithmetic  1.33 us (1%)
    all_to_all x1, blocking collectives, per_device(): terms = lax.all_to_all(pair, 'fsdp', 0, 0, axis_index_groups=CHIP_GROUPS)  21.3 us
    all_to_all x1, blocking collectives, per_device(): lax.all_to_all(spread, 'fsdp', 0, 0, axis_index_groups=CHIP_GROUPS)  20.8 us
    ppermute x8, starting transfers between devices, tp_shift(): return lax.ppermute(value, 'tp', pairs)  16.7 us
    pallas_call x9, Pallas kernels, local_call(): pl.pallas_call(kernel, in_specs=[SCALARS] + in_vmem(len(operands) - 1), o...  15.6 us
    ppermute x5, starting transfers between devices, fsdp_flip(): return lax.ppermute(value, 'fsdp', [(i, i ^ flip) for i in range(16)])  14.4 us
    ppermute x6, starting transfers between devices, y_shift(): lax.ppermute(value, 'fsdp', [(i, (i + 4 * dy) % 16) for i in range(16)])  8.96 us
    ppermute x6, waiting for transfers between devices, y_shift(): lax.ppermute(value, 'fsdp', [(i, (i + 4 * dy) % 16) for i in range(16)])  8.87 us
    ppermute x8, waiting for transfers between devices, tp_shift(): return lax.ppermute(value, 'tp', pairs)  8.11 us
  transfers between devices with their start and end apart: 19, of which 11 were waited for; matrix products, arithmetic and copies ran while one was open for 3% of the time, Pallas kernels for 4%

profile of v2, /device:TPU:1, one launch (start us, length us, event | category | flops | bytes accessed | tf_op | source)
XLA Modules:
  0.0 128.2 jit_solution(15637319977731302310)
XLA Ops:
  0.8 2.1 %dynamic-slice_bitcast_fusion = (bf16[64,2048]{1,0:T(8,128)(2,1)S(1)}, bf16[64,2048]{1,0:T(8,128)(2,1)}, bf16[64,2048]{1,0:T(8,128)(2,1)}, bf16[64,2048]{1,0:T(8,128)(2,1)}) fusion(bf16[1,64,8192]{2,1,0:T(8,128)(2,1)} %param.7, s32[]{:T(128)S(6)} %select_n.108, s32[]{:T(128)S(6)} %select_n.104, s32[]{:T(128)S(6)} %select_n.102, s32[]{:T(128)S(6)} %select_n.106), kind=kLoop, calls=%fused_computation.9 | loop fusion | bytes 2097168 | tf_op jit(solution)/shard_map/dynamic_slice | solution.py:168
  2.9 2.0 %collective-permute-start.4 = (bf16[512,512]{1,0:T(8,128)(2,1)S(1)}, bf16[512,512]{1,0:T(8,128)(2,1)S(1)}, u32[]{:S(2)}, u32[]{:S(2)}) collective-permute-start(bf16[512,512]{1,0:T(8,128)(2,1)S(1)} %copy-done.1), channel_id=1, source_target_pairs={{0,2},{1,3},{2,0},{3,1},{4,6},{5,7},{6,4},{7,5},{8,10},{9,11},{10,... | collective-permute-start | bytes 1572872 | tf_op jit(solution)/shard_map/ppermute | solution.py:24
  6.2 2.6 %collective-permute-start = (bf16[64,2048]{1,0:T(8,128)(2,1)}, bf16[64,2048]{1,0:T(8,128)(2,1)S(1)}, u32[]{:S(2)}, u32[]{:S(2)}) collective-permute-start(bf16[64,2048]{1,0:T(8,128)(2,1)} %get-tuple-element.20), channel_id=1, source_target_pairs={{0,8},{1,9},{2,10},{3,11},{4,12},{5,13},{6,14},{7,15},{8,0},{9,1},... | collective-permute-start | bytes 786440 | tf_op jit(solution)/shard_map/ppermute | solution.py:28
  9.2 2.3 %collective-permute-start.2 = (bf16[64,2048]{1,0:T(8,128)(2,1)}, bf16[64,2048]{1,0:T(8,128)(2,1)S(1)}, u32[]{:S(2)}, u32[]{:S(2)}) collective-permute-start(bf16[64,2048]{1,0:T(8,128)(2,1)} %get-tuple-element.25), channel_id=1, source_target_pairs={{0,12},{1,13},{2,14},{3,15},{4,0},{5,1},{6,2},{7,3},{8,4},{9,5},{1... | collective-permute-start | bytes 786440 | tf_op jit(solution)/shard_map/ppermute | solution.py:28
  12.2 3.0 %collective-permute-done.4.p2 = bf16[512,512]{1,0:T(8,128)(2,1)S(1)} collective-permute-done((bf16[512,512]{1,0:T(8,128)(2,1)S(1)}, bf16[512,512]{1,0:T(8,128)(2,1)S(1)}, u32[]{:S(2)}, u32[]{:S(2)}) %collective-permute-start.4) | collective-permute-done | bytes 524320 | tf_op jit(solution)/shard_map/ppermute | solution.py:24
  15.2 2.6 %collective-permute-start.5 = (bf16[512,512]{1,0:T(8,128)(2,1)S(1)}, bf16[512,512]{1,0:T(8,128)(2,1)S(1)}, u32[]{:S(2)}, u32[]{:S(2)}) collective-permute-start(bf16[512,512]{1,0:T(8,128)(2,1)S(1)} %collective-permute-done.4.p2), channel_id=1, source_target_pairs={{0,1},{1,0},{2,3},{3,2},{4,5},{5,4},{6,7},{7,6},{8,9},{9,8},{10,11... | collective-permute-start | bytes 1572872 | tf_op jit(solution)/shard_map/ppermute | solution.py:24
  23.1 2.4 %collective-permute-start.6 = (f32[64,512]{1,0:T(8,128)S(1)}, f32[64,512]{1,0:T(8,128)S(1)}, u32[]{:S(2)}, u32[]{:S(2)}) collective-permute-start(f32[64,512]{1,0:T(8,128)S(1)} %get-tuple-element.28), channel_id=1, source_target_pairs={{0,12},{1,13},{2,14},{3,15},{4,0},{5,1},{6,2},{7,3},{8,4},{9,5},{1... | collective-permute-start | bytes 393224 | tf_op jit(solution)/shard_map/ppermute | solution.py:28
  27.9 6.3 %collective-permute-done.7.c = f32[64,512]{1,0:T(8,128)S(1)} collective-permute-done((f32[64,512]{1,0:T(8,128)S(1)}, f32[64,512]{1,0:T(8,128)S(1)}, u32[]{:S(2)}, u32[]{:S(2)}) %collective-permute-start.7) | collective-permute-done | bytes 131104 | tf_op jit(solution)/shard_map/ppermute | solution.py:28
  34.8 2.5 %collective-permute-start.9 = (bf16[64,512]{1,0:T(8,128)(2,1)S(1)}, bf16[64,512]{1,0:T(8,128)(2,1)S(1)}, u32[]{:S(2)}, u32[]{:S(2)}) collective-permute-start(bf16[64,512]{1,0:T(8,128)(2,1)S(1)} %total.1.mine), channel_id=1, source_target_pairs={{0,16},{16,0},{32,48},{48,32},{64,80},{80,64},{96,112},{112,96},{1... | collective-permute-start | bytes 196616 | tf_op jit(solution)/shard_map/ppermute | solution.py:33
  37.3 2.2 %collective-permute-done.9.partner = bf16[64,512]{1,0:T(8,128)(2,1)S(1)} collective-permute-done((bf16[64,512]{1,0:T(8,128)(2,1)S(1)}, bf16[64,512]{1,0:T(8,128)(2,1)S(1)}, u32[]{:S(2)}, u32[]{:S(2)}) %collective-permute-start.9) | collective-permute-done | bytes 65568 | tf_op jit(solution)/shard_map/ppermute | solution.py:33
  40.1 6.1 %collective-permute-start.12 = (bf16[512,128]{1,0:T(8,128)(2,1)S(1)}, bf16[512,128]{1,0:T(8,128)(2,1)S(1)}, u32[]{:S(2)}, u32[]{:S(2)}) collective-permute-start(bf16[512,128]{1,0:T(8,128)(2,1)S(1)} %join.1.refs_0_), channel_id=1, source_target_pairs={{0,192},{16,208},{32,224},{48,240},{64,0},{80,16},{96,32},{112,48}... | collective-permute-start | bytes 393224 | tf_op jit(solution)/shard_map/ppermute | solution.py:33
  46.2 3.1 %collective-permute-start.16 = (bf16[512,128]{1,0:T(8,128)(2,1)S(1)}, bf16[512,128]{1,0:T(8,128)(2,1)S(1)}, u32[]{:S(2)}, u32[]{:S(2)}) collective-permute-start(bf16[512,128]{1,0:T(8,128)(2,1)S(1)} %join.1.refs_0_), channel_id=1, source_target_pairs={{0,224},{16,240},{32,0},{48,16},{64,32},{80,48},{96,64},{112,80},{... | collective-permute-start | bytes 393224 | tf_op jit(solution)/shard_map/ppermute | solution.py:33
  50.9 2.2 %collective-permute-start.13 = (bf16[512,128]{1,0:T(8,128)(2,1)S(1)}, bf16[512,128]{1,0:T(8,128)(2,1)S(1)}, u32[]{:S(2)}, u32[]{:S(2)}) collective-permute-start(bf16[512,128]{1,0:T(8,128)(2,1)S(1)} %collective-permute-done.12.refs_1_), channel_id=1, source_target_pairs={{0,224},{16,240},{32,0},{48,16},{64,32},{80,48},{96,64},{112,80},{... | collective-permute-start | bytes 393224 | tf_op jit(solution)/shard_map/ppermute | solution.py:33
  58.3 2.4 %collective-permute-done.14.refs_2_ = bf16[512,128]{1,0:T(8,128)(2,1)S(1)} collective-permute-done((bf16[512,128]{1,0:T(8,128)(2,1)S(1)}, bf16[512,128]{1,0:T(8,128)(2,1)S(1)}, u32[]{:S(2)}, u32[]{:S(2)}) %collective-permute-start.14) | collective-permute-done | bytes 131104 | tf_op jit(solution)/shard_map/ppermute | solution.py:33
  60.7 2.3 %far_terms.1.refs_3_ = f32[512,1792]{1,0:T(8,128)S(1)} custom-call(s32[21]{0:T(128)S(1)} %concatenate.3.where._, bf16[512,128]{1,0:T(8,128)(2,1)S(1)} %collective-permute-done.10.refs_0_, bf16[512,128]{1,0:T(8,128)(2,1)S(1)} %collective-permute-done.12.refs_1_, bf16[512,128]{1,0:T(8,128)(2,1)S(1)} %collective-permute-done.14.refs_2_, ...), custom_call_target="tpu_custom_call", output_to_operand_aliasing={{}: (5, {})} | custom-call | flops 704643072 | bytes 7733332 | tf_op jit(solution)/shard_map/far_terms/pallas_call | solution.py:45
  64.2 3.0 %last_terms.1 = (bf16[8,48,1792]{2,1,0:T(8,128)(2,1)S(1)}, f32[8,48,1792]{2,1,0:T(8,128)S(1)}) custom-call(s32[21]{0:T(128)S(1)} %concatenate.3.where._, bf16[512,128]{1,0:T(8,128)(2,1)S(1)} %collective-permute-done.11.refs_0_, bf16[512,128]{1,0:T(8,128)(2,1)S(1)} %collective-permute-done.13.refs_1_, bf16[1024,1792]{1,0:T(8,128)(2,1)S(1)} %bitcast.24, ...), custom_call_target="tpu_custom_call" | custom-call | flops 469762048 | bytes 7602260 | tf_op jit(solution)/shard_map/last_terms/pallas_call | solution.py:45
  67.1 6.3 %collective-permute-start.17 = (bf16[8,48,1792]{2,1,0:T(8,128)(2,1)S(1)}, bf16[8,48,1792]{2,1,0:T(8,128)(2,1)S(1)}, u32[]{:S(2)}, u32[]{:S(2)}) collective-permute-start(bf16[8,48,1792]{2,1,0:T(8,128)(2,1)S(1)} %get-tuple-element.32), channel_id=1, source_target_pairs={{0,1},{1,0},{2,3},{3,2},{4,5},{5,4},{6,7},{7,6},{8,9},{9,8},{10,11... | collective-permute-start | bytes 4128776 | tf_op jit(solution)/shard_map/ppermute | solution.py:24
  73.5 2.8 %collective-permute-done.17 = bf16[8,48,1792]{2,1,0:T(8,128)(2,1)S(1)} collective-permute-done((bf16[8,48,1792]{2,1,0:T(8,128)(2,1)S(1)}, bf16[8,48,1792]{2,1,0:T(8,128)(2,1)S(1)}, u32[]{:S(2)}, u32[]{:S(2)}) %collective-permute-start.17) | collective-permute-done | bytes 1376288 | tf_op jit(solution)/shard_map/ppermute | solution.py:24
  76.5 21.3 %all_to_all.10.terms = bf16[8,48,1792]{2,1,0:T(8,128)(2,1)S(1)} all-to-all(bf16[8,48,1792]{2,1,0:T(8,128)(2,1)S(1)} %add_convert_fusion), channel_id=1, replica_groups={{0,2,4,6,8,10,12,14},{1,3,5,7,9,11,13,15},{16,18,20,22,24,26,28,30},{17..., dimensions={0} | all-to-all | bytes 2752512 | tf_op jit(solution)/shard_map/all_to_all | solution.py:242
  97.8 1.7 %moments.1 = (f32[48,1792]{1,0:T(8,128)}, f32[48,1792]{1,0:T(8,128)}, bf16[8,48,1792]{2,1,0:T(8,128)(2,1)S(1)}) custom-call(s32[21]{0:T(128)S(1)} %concatenate.3.where._, bf16[8,48,1792]{2,1,0:T(8,128)(2,1)S(1)} %all_to_all.10.terms, f32[48,1792]{1,0:T(8,128)S(1)} %copy-done.2, f32[48,1792]{1,0:T(8,128)S(1)} %copy-done.3), custom_call_target="tpu_custom_call" | custom-call | flops 2580480 | bytes 2064468 | tf_op jit(solution)/shard_map/moments/pallas_call | solution.py:45
  99.5 20.8 %all_to_all.11 = bf16[8,48,1792]{2,1,0:T(8,128)(2,1)S(1)} all-to-all(bf16[8,48,1792]{2,1,0:T(8,128)(2,1)S(1)} %get-tuple-element.33), channel_id=1, replica_groups={{0,2,4,6,8,10,12,14},{1,3,5,7,9,11,13,15},{16,18,20,22,24,26,28,30},{17..., dimensions={0} | all-to-all | bytes 2752512 | tf_op jit(solution)/shard_map/all_to_all | solution.py:254
  120.4 2.2 %collective-permute-start.18 = (bf16[384,1792]{1,0:T(8,128)(2,1)S(1)}, bf16[384,1792]{1,0:T(8,128)(2,1)S(1)}, u32[]{:S(2)}, u32[]{:S(2)}) collective-permute-start(bf16[384,1792]{1,0:T(8,128)(2,1)S(1)} %bitcast.25), channel_id=1, source_target_pairs={{0,1},{1,0},{2,3},{3,2},{4,5},{5,4},{6,7},{7,6},{8,9},{9,8},{10,11... | collective-permute-start | bytes 4128776 | tf_op jit(solution)/shard_map/ppermute | solution.py:24
  122.6 1.7 %half_delta.1.before = f32[512,1792]{1,0:T(8,128)S(1)} custom-call(s32[21]{0:T(128)S(1)} %concatenate.3.where._, bf16[512,384]{1,0:T(8,128)(2,1)S(1)} %fusion.chosen, bf16[384,1792]{1,0:T(8,128)(2,1)S(1)} %bitcast.26), custom_call_target="tpu_custom_call" | custom-call | flops 704643072 | bytes 1769556 | tf_op jit(solution)/shard_map/half_delta/pallas_call | solution.py:45
  125.3 2.9 %delta.1 = bf16[512,1792]{1,0:T(8,128)(2,1)} custom-call(s32[21]{0:T(128)S(1)} %concatenate.3.where._, bf16[512,384]{1,0:T(8,128)(2,1)S(1)} %fusion.1.chosen, bf16[384,1792]{1,0:T(8,128)(2,1)S(1)} %collective-permute-done.18.updates, f32[512,1792]{1,0:T(8,128)S(1)} %half_delta.1.before), custom_call_target="tpu_custom_call" | custom-call | flops 704643072 | bytes 5439572 | tf_op jit(solution)/shard_map/delta/pallas_call | solution.py:45
  (54 shorter events, 20.6 us)
Async XLA Ops:
  0.6 10.9 %copy-start.4 = (s32[16]{0:T(128)S(1)}, s32[16]{0:T(128)}, u32[]{:S(2)}) copy-start(s32[16]{0:T(128)} %param.10) | copy-start | bytes 196
  0.7 11.1 %copy-start.5 = (s32[16]{0:T(128)S(1)}, s32[16]{0:T(128)}, u32[]{:S(2)}) copy-start(s32[16]{0:T(128)} %param.11) | copy-start | bytes 196
  2.9 12.3 %collective-permute-start.4 = (bf16[512,512]{1,0:T(8,128)(2,1)S(1)}, bf16[512,512]{1,0:T(8,128)(2,1)S(1)}, u32[]{:S(2)}, u32[]{:S(2)}) collective-permute-start(bf16[512,512]{1,0:T(8,128)(2,1)S(1)} %copy-done.1), channel_id=1, source_target_pairs={{0,2},{1,3},{2,0},{3,1},{4,6},{5,7},{6,4},{7,5},{8,10},{9,11},{10,... | collective-permute-start | bytes 1572872 | tf_op jit(solution)/shard_map/ppermute | solution.py:24
  4.9 16.9 %collective-permute-start.3 = (bf16[512,512]{1,0:T(8,128)(2,1)S(1)}, bf16[512,512]{1,0:T(8,128)(2,1)S(1)}, u32[]{:S(2)}, u32[]{:S(2)}) collective-permute-start(bf16[512,512]{1,0:T(8,128)(2,1)S(1)} %copy-done.1), channel_id=1, source_target_pairs={{0,1},{1,0},{2,3},{3,2},{4,5},{5,4},{6,7},{7,6},{8,9},{9,8},{10,11... | collective-permute-start | bytes 1572872 | tf_op jit(solution)/shard_map/ppermute | solution.py:24
  6.2 14.1 %collective-permute-start = (bf16[64,2048]{1,0:T(8,128)(2,1)}, bf16[64,2048]{1,0:T(8,128)(2,1)S(1)}, u32[]{:S(2)}, u32[]{:S(2)}) collective-permute-start(bf16[64,2048]{1,0:T(8,128)(2,1)} %get-tuple-element.20), channel_id=1, source_target_pairs={{0,8},{1,9},{2,10},{3,11},{4,12},{5,13},{6,14},{7,15},{8,0},{9,1},... | collective-permute-start | bytes 786440 | tf_op jit(solution)/shard_map/ppermute | solution.py:28
  8.8 13.0 %collective-permute-start.1 = (bf16[64,2048]{1,0:T(8,128)(2,1)}, bf16[64,2048]{1,0:T(8,128)(2,1)S(1)}, u32[]{:S(2)}, u32[]{:S(2)}) collective-permute-start(bf16[64,2048]{1,0:T(8,128)(2,1)} %get-tuple-element.23), channel_id=1, source_target_pairs={{0,4},{1,5},{2,6},{3,7},{4,8},{5,9},{6,10},{7,11},{8,12},{9,13},{1... | collective-permute-start | bytes 786440 | tf_op jit(solution)/shard_map/ppermute | solution.py:28
  9.2 12.6 %collective-permute-start.2 = (bf16[64,2048]{1,0:T(8,128)(2,1)}, bf16[64,2048]{1,0:T(8,128)(2,1)S(1)}, u32[]{:S(2)}, u32[]{:S(2)}) collective-permute-start(bf16[64,2048]{1,0:T(8,128)(2,1)} %get-tuple-element.25), channel_id=1, source_target_pairs={{0,12},{1,13},{2,14},{3,15},{4,0},{5,1},{6,2},{7,3},{8,4},{9,5},{1... | collective-permute-start | bytes 786440 | tf_op jit(solution)/shard_map/ppermute | solution.py:28
  15.2 6.6 %collective-permute-start.5 = (bf16[512,512]{1,0:T(8,128)(2,1)S(1)}, bf16[512,512]{1,0:T(8,128)(2,1)S(1)}, u32[]{:S(2)}, u32[]{:S(2)}) collective-permute-start(bf16[512,512]{1,0:T(8,128)(2,1)S(1)} %collective-permute-done.4.p2), channel_id=1, source_target_pairs={{0,1},{1,0},{2,3},{3,2},{4,5},{5,4},{6,7},{7,6},{8,9},{9,8},{10,11... | collective-permute-start | bytes 1572872 | tf_op jit(solution)/shard_map/ppermute | solution.py:24
  21.8 34.8 %copy-start = (bf16[1,1024,1792]{2,1,0:T(8,128)(2,1)S(1)}, bf16[1,1024,1792]{2,1,0:T(8,128)(2,1)}, u32[]{:S(2)}) copy-start(bf16[1,1024,1792]{2,1,0:T(8,128)(2,1)} %param.8) | copy-start | bytes 11010052
  23.1 4.8 %collective-permute-start.6 = (f32[64,512]{1,0:T(8,128)S(1)}, f32[64,512]{1,0:T(8,128)S(1)}, u32[]{:S(2)}, u32[]{:S(2)}) collective-permute-start(f32[64,512]{1,0:T(8,128)S(1)} %get-tuple-element.28), channel_id=1, source_target_pairs={{0,12},{1,13},{2,14},{3,15},{4,0},{5,1},{6,2},{7,3},{8,4},{9,5},{1... | collective-permute-start | bytes 393224 | tf_op jit(solution)/shard_map/ppermute | solution.py:28
  25.5 8.7 %collective-permute-start.7 = (f32[64,512]{1,0:T(8,128)S(1)}, f32[64,512]{1,0:T(8,128)S(1)}, u32[]{:S(2)}, u32[]{:S(2)}) collective-permute-start(f32[64,512]{1,0:T(8,128)S(1)} %get-tuple-element.29), channel_id=1, source_target_pairs={{0,4},{1,5},{2,6},{3,7},{4,8},{5,9},{6,10},{7,11},{8,12},{9,13},{1... | collective-permute-start | bytes 393224 | tf_op jit(solution)/shard_map/ppermute | solution.py:28
  25.5 8.7 %collective-permute-start.8 = (f32[64,512]{1,0:T(8,128)S(1)}, f32[64,512]{1,0:T(8,128)S(1)}, u32[]{:S(2)}, u32[]{:S(2)}) collective-permute-start(f32[64,512]{1,0:T(8,128)S(1)} %get-tuple-element.30), channel_id=1, source_target_pairs={{0,8},{1,9},{2,10},{3,11},{4,12},{5,13},{6,14},{7,15},{8,0},{9,1},... | collective-permute-start | bytes 393224 | tf_op jit(solution)/shard_map/ppermute | solution.py:28
  34.8 4.7 %collective-permute-start.9 = (bf16[64,512]{1,0:T(8,128)(2,1)S(1)}, bf16[64,512]{1,0:T(8,128)(2,1)S(1)}, u32[]{:S(2)}, u32[]{:S(2)}) collective-permute-start(bf16[64,512]{1,0:T(8,128)(2,1)S(1)} %total.1.mine), channel_id=1, source_target_pairs={{0,16},{16,0},{32,48},{48,32},{64,80},{80,64},{96,112},{112,96},{1... | collective-permute-start | bytes 196616 | tf_op jit(solution)/shard_map/ppermute | solution.py:33
  40.1 10.8 %collective-permute-start.12 = (bf16[512,128]{1,0:T(8,128)(2,1)S(1)}, bf16[512,128]{1,0:T(8,128)(2,1)S(1)}, u32[]{:S(2)}, u32[]{:S(2)}) collective-permute-start(bf16[512,128]{1,0:T(8,128)(2,1)S(1)} %join.1.refs_0_), channel_id=1, source_target_pairs={{0,192},{16,208},{32,224},{48,240},{64,0},{80,16},{96,32},{112,48}... | collective-permute-start | bytes 393224 | tf_op jit(solution)/shard_map/ppermute | solution.py:33
  46.2 7.0 %collective-permute-start.10 = (bf16[512,128]{1,0:T(8,128)(2,1)S(1)}, bf16[512,128]{1,0:T(8,128)(2,1)S(1)}, u32[]{:S(2)}, u32[]{:S(2)}) collective-permute-start(bf16[512,128]{1,0:T(8,128)(2,1)S(1)} %join.1.refs_0_), channel_id=1, source_target_pairs={{0,64},{16,80},{32,96},{48,112},{64,128},{80,144},{96,160},{112,17... | collective-permute-start | bytes 393224 | tf_op jit(solution)/shard_map/ppermute | solution.py:33
  46.2 9.1 %collective-permute-start.16 = (bf16[512,128]{1,0:T(8,128)(2,1)S(1)}, bf16[512,128]{1,0:T(8,128)(2,1)S(1)}, u32[]{:S(2)}, u32[]{:S(2)}) collective-permute-start(bf16[512,128]{1,0:T(8,128)(2,1)S(1)} %join.1.refs_0_), channel_id=1, source_target_pairs={{0,224},{16,240},{32,0},{48,16},{64,32},{80,48},{96,64},{112,80},{... | collective-permute-start | bytes 393224 | tf_op jit(solution)/shard_map/ppermute | solution.py:33
  49.3 7.3 %collective-permute-start.15 = (bf16[512,128]{1,0:T(8,128)(2,1)S(1)}, bf16[512,128]{1,0:T(8,128)(2,1)S(1)}, u32[]{:S(2)}, u32[]{:S(2)}) collective-permute-start(bf16[512,128]{1,0:T(8,128)(2,1)S(1)} %join.1.refs_0_), channel_id=1, source_target_pairs={{0,32},{16,48},{32,64},{48,80},{64,96},{80,112},{96,128},{112,144}... | collective-permute-start | bytes 393224 | tf_op jit(solution)/shard_map/ppermute | solution.py:33
  49.4 11.4 %collective-permute-start.14 = (bf16[512,128]{1,0:T(8,128)(2,1)S(1)}, bf16[512,128]{1,0:T(8,128)(2,1)S(1)}, u32[]{:S(2)}, u32[]{:S(2)}) collective-permute-start(bf16[512,128]{1,0:T(8,128)(2,1)S(1)} %join.1.refs_0_), channel_id=1, source_target_pairs={{0,128},{16,144},{32,160},{48,176},{64,192},{80,208},{96,224},{112... | collective-permute-start | bytes 393224 | tf_op jit(solution)/shard_map/ppermute | solution.py:33
  50.9 12.0 %collective-permute-start.13 = (bf16[512,128]{1,0:T(8,128)(2,1)S(1)}, bf16[512,128]{1,0:T(8,128)(2,1)S(1)}, u32[]{:S(2)}, u32[]{:S(2)}) collective-permute-start(bf16[512,128]{1,0:T(8,128)(2,1)S(1)} %collective-permute-done.12.refs_1_), channel_id=1, source_target_pairs={{0,224},{16,240},{32,0},{48,16},{64,32},{80,48},{96,64},{112,80},{... | collective-permute-start | bytes 393224 | tf_op jit(solution)/shard_map/ppermute | solution.py:33
  53.2 11.0 %collective-permute-start.11 = (bf16[512,128]{1,0:T(8,128)(2,1)S(1)}, bf16[512,128]{1,0:T(8,128)(2,1)S(1)}, u32[]{:S(2)}, u32[]{:S(2)}) collective-permute-start(bf16[512,128]{1,0:T(8,128)(2,1)S(1)} %collective-permute-done.10.refs_0_), channel_id=1, source_target_pairs={{0,32},{16,48},{32,64},{48,80},{64,96},{80,112},{96,128},{112,144}... | collective-permute-start | bytes 393224 | tf_op jit(solution)/shard_map/ppermute | solution.py:33
  67.1 9.1 %collective-permute-start.17 = (bf16[8,48,1792]{2,1,0:T(8,128)(2,1)S(1)}, bf16[8,48,1792]{2,1,0:T(8,128)(2,1)S(1)}, u32[]{:S(2)}, u32[]{:S(2)}) collective-permute-start(bf16[8,48,1792]{2,1,0:T(8,128)(2,1)S(1)} %get-tuple-element.32), channel_id=1, source_target_pairs={{0,1},{1,0},{2,3},{3,2},{4,5},{5,4},{6,7},{7,6},{8,9},{9,8},{10,11... | collective-permute-start | bytes 4128776 | tf_op jit(solution)/shard_map/ppermute | solution.py:24
  76.5 21.3 %copy-start.2 = (f32[48,1792]{1,0:T(8,128)S(1)}, f32[48,1792]{1,0:T(8,128)}, u32[]{:S(2)}) copy-start(f32[48,1792]{1,0:T(8,128)} %first.1) | copy-start | bytes 1032196
  76.5 21.3 %copy-start.3 = (f32[48,1792]{1,0:T(8,128)S(1)}, f32[48,1792]{1,0:T(8,128)}, u32[]{:S(2)}) copy-start(f32[48,1792]{1,0:T(8,128)} %second.1) | copy-start | bytes 1032196
  120.4 5.0 %collective-permute-start.18 = (bf16[384,1792]{1,0:T(8,128)(2,1)S(1)}, bf16[384,1792]{1,0:T(8,128)(2,1)S(1)}, u32[]{:S(2)}, u32[]{:S(2)}) collective-permute-start(bf16[384,1792]{1,0:T(8,128)(2,1)S(1)} %bitcast.25), channel_id=1, source_target_pairs={{0,1},{1,0},{2,3},{3,2},{4,5},{5,4},{6,7},{7,6},{8,9},{9,8},{10,11... | collective-permute-start | bytes 4128776 | tf_op jit(solution)/shard_map/ppermute | solution.py:24
  (1 other events, 2.3 us)

commit v3 on v2

v3 whole, which is shorter than its diff:
```python
import functools

import jax
import jax.numpy as jnp
from jax import lax
from jax.experimental import pallas as pl
from jax.experimental.pallas import tpu as pltpu
from jax.sharding import PartitionSpec as P

STEP = 10
beta_one = 0.9
beta_two = 0.999
adam_eps = 1e-08

F32 = jnp.float32
BF16 = jnp.bfloat16

LOW, Z, CORE, H, Y, X, F, START, LENGTH = 0, 1, 2, 3, 4, 5, 6, 16, 32
TO_CHIPS = [(1, 1), (3, 1), (2, 1), (1, 0), (3, 0), (0, 1), (2, 0), (0, 0)]
FROM_CHIPS = [(0, 0), (0, 1), (3, 0), (1, 0), (2, 0), (3, 1), (1, 1), (2, 1)]
FF = 1792
VMEM = pltpu.VMEM


def fsdp_flip(value, flip):
    return lax.ppermute(value, "fsdp", [(i, i ^ flip) for i in range(16)])


def y_shift(value, dy):
    return lax.ppermute(value, "fsdp", [(i, (i + 4 * dy) % 16) for i in range(16)])


def tp_shift(value, dz, dh):
    pairs = [(i, ((i // 2 + dz) % 8) * 2 + ((i % 2) ^ dh)) for i in range(16)]
    return lax.ppermute(value, "tp", pairs)


SCALARS = pl.BlockSpec(memory_space=pltpu.SMEM)
ANYWHERE = pl.BlockSpec(memory_space=pl.ANY)


def in_vmem(count):
    return [pl.BlockSpec(memory_space=VMEM)] * count


def local_call(
    kernel, name, out_shape, operands, flops, scratch=(), limit=24, aliases=None, anywhere=(0, 0)
):
    size = sum(v.size * v.dtype.itemsize for v in operands)
    return pl.pallas_call(
        kernel,
        in_specs=[SCALARS] + in_vmem(len(operands) - 1 - anywhere[0]) + [ANYWHERE] * anywhere[0],
        out_specs=in_vmem(len(out_shape) - anywhere[1]) + [ANYWHERE] * anywhere[1],
        out_shape=out_shape,
        scratch_shapes=scratch,
        input_output_aliases=aliases or {},
        cost_estimate=pl.CostEstimate(flops=flops, bytes_accessed=size, transcendentals=0),
        compiler_params=pltpu.CompilerParams(vmem_limit_bytes=limit << 20),
        name=name,
    )(*operands)


def table_kernel(lengths, owners, out):
    f = lax.axis_index("fsdp").astype(jnp.int32)
    c = lax.axis_index("tp").astype(jnp.int32)
    facts = {LOW: f % 4, Z: c // 2, CORE: f % 2, H: c % 2, Y: f // 4, X: f // 2 % 2, F: f}
    for place, value in facts.items():
        out[place] = value
    start = jnp.int32(0)
    for piece in range(16):
        owner = owners[piece]
        out[START + owner] = start
        out[LENGTH + owner] = lengths[piece]
        start = start + lengths[piece]


def scalar_table(lengths, owners):
    return pl.pallas_call(
        table_kernel,
        in_specs=[SCALARS] * 2,
        out_specs=SCALARS,
        out_shape=jax.ShapeDtypeStruct((48,), jnp.int32),
        cost_estimate=pl.CostEstimate(flops=0, bytes_accessed=512, transcendentals=0),
        compiler_params=pltpu.CompilerParams(vmem_limit_bytes=1 << 20),
        name="table",
    )(lengths, owners)


def owner_of(where, dy, dx, other):
    chip = lax.rem(where[Y] + dy, 4) * 2 + (where[X] ^ dx)
    return chip * 2 + (where[CORE] ^ other)


def choose_kernel(where, source, *refs):
    *outs, projection, semaphore = refs
    copy = pltpu.make_async_copy(source, projection, semaphore)
    copy.start()
    row = lax.broadcasted_iota(jnp.int32, (48, 512), 1)
    slot = lax.broadcasted_iota(jnp.int32, (48, 512), 0)
    for other, out in enumerate(outs):
        marks = []
        for dy, dx in FROM_CHIPS:
            owner = owner_of(where, dy, dx, other)
            live = (row == where[START + owner] + slot) & (slot < where[LENGTH + owner])
            marks.append(jnp.where(live, 1.0, 0.0))
        hot = jnp.concatenate(marks, axis=0).astype(BF16)
        if other == 0:
            copy.wait()
        out[...] = lax.dot_general(
            projection[...], hot, (((1,), (1,)), ((), ())), preferred_element_type=F32
        ).astype(BF16)


def token_product(where, r, tokens, block):
    columns = pl.ds(pl.multiple_of((where[LOW] ^ r) * 512, 512), 512)
    rows = jnp.concatenate([t[:, columns] for t in tokens], axis=0)
    return jnp.dot(rows, block[...], preferred_element_type=F32)


def front_kernel(where, a0, a1, a2, a3, p1, p2, p0, out, here, semaphore):
    copy = pltpu.make_async_copy(p0, here, semaphore)
    copy.start()
    tokens = (a0, a1, a2, a3)
    total = token_product(where, 1, tokens, p1) + token_product(where, 2, tokens, p2)
    copy.wait()
    out[...] = total + token_product(where, 0, tokens, here)


def front_rest_kernel(where, a0, a1, a2, a3, p3, before, o0, o1, o2, o3):
    total = before[...] + token_product(where, 3, (a0, a1, a2, a3), p3)
    for i, o in enumerate((o0, o1, o2, o3)):
        o[...] = total[i * 64 : (i + 1) * 64].astype(o.dtype)


def total_kernel(_, a, b, c, d, out):
    others = b[...].astype(F32) + c[...].astype(F32) + d[...].astype(F32)
    out[...] = (a[...] + others).astype(BF16)


def join_kernel(where, mine, partner, out):
    first = where[H] == 0
    here, there = mine[...].astype(F32), partner[...].astype(F32)
    rows = jnp.concatenate(
        [jnp.where(first, here, there), jnp.where(first, there, here)], axis=0
    )
    out[...] = rows.T.astype(BF16)


def token_rows(where, grads, offset):
    row = lax.rem(where[Z] + offset, 8) * 128
    return grads[pl.ds(pl.multiple_of(row, 128), 128), :]


def sum_kernel(offsets, where, *refs):
    count = len(offsets)
    blocks, grads, rest, out = refs[:count], refs[count], refs[count + 1 : -1], refs[-1]
    left = jnp.concatenate([b[...] for b in blocks], axis=1)
    right = jnp.concatenate([token_rows(where, grads, o) for o in offsets], axis=0)
    total = jnp.dot(left, right, preferred_element_type=F32)
    for before in rest:
        total = total + before[...]
    out[...] = total


def rows_from(table, start):
    low = lax.rem(start, 8)
    rows = table[pl.ds(pl.multiple_of(start - low, 8), 56), :]
    return pltpu.roll(rows, lax.rem(56 - low, 56), 0)[:48]


def last_kernel(offsets, where, *refs):
    give, keep, table = refs[-3:]
    table[512:560, :] = jnp.zeros((48, FF), F32)
    sum_kernel(offsets, where, *refs[:-3], table.at[0:512, :])
    for i, (dy, dx) in enumerate(TO_CHIPS):
        give[i] = rows_from(table, where[START + owner_of(where, dy, dx, 1)]).astype(BF16)
        keep[i] = rows_from(table, where[START + owner_of(where, dy, dx, 0)])


def pair_kernel(_, keep, given, *outs):
    for i, out in enumerate(outs):
        out[...] = (keep[i] + given[i].astype(F32)).astype(out.dtype)


def add_kernel(_, *refs):
    total = refs[0][...]
    for r in refs[1:-1]:
        total = total + r[...].astype(F32)
    refs[-1][...] = total.astype(BF16)


def moments_kernel(where, own, t1, t2, t3, t4, first, second, new_first, new_second, update):
    live = lax.broadcasted_iota(jnp.int32, (48, FF), 0) < where[LENGTH + where[F]]
    gradient = own[...]
    for t in (t1, t2, t3, t4):
        gradient = gradient + t[...].astype(F32)
    one, two, three = adam_rows(gradient, live, first[...], second[...])
    new_first[...] = one
    new_second[...] = two
    update[...] = three


def half_delta_kernel(_, chosen, updates, out):
    out[...] = jnp.dot(chosen[...], updates[...], preferred_element_type=F32)


def delta_kernel(_, chosen, updates, before, out, whole, semaphores):
    copies = []
    for i in range(7):
        columns = slice(256 * i, 256 * i + 256)
        product = jnp.dot(chosen[...], updates[:, columns], preferred_element_type=F32)
        whole[:, columns] = (before[:, columns] + product).astype(BF16)
        copy = pltpu.make_async_copy(
            whole.at[:, pl.ds(256 * i, 256)], out.at[:, pl.ds(256 * i, 256)], semaphores.at[i]
        )
        copy.start()
        copies.append(copy)
    for copy in copies:
        copy.wait()


def adam_rows(gradient, live_mask, first_moment, second_moment):
    new_first = jnp.where(live_mask, beta_one * first_moment + (1.0 - beta_one) * gradient, 0.0)
    new_second = jnp.where(
        live_mask, beta_two * second_moment + (1.0 - beta_two) * gradient * gradient, 0.0
    )
    first_hat = new_first / (1.0 - beta_one**STEP)
    second_hat = new_second / (1.0 - beta_two**STEP)
    update = jnp.where(live_mask, first_hat / (jnp.sqrt(second_hat) + adam_eps), 0.0)
    return (new_first, new_second, update.astype(BF16))


def per_device(
    activations, grad_output, projection, piece_lengths, piece_owners, first_moment, second_moment
):
    tokens = activations[0]
    grads = grad_output[0]
    y = lax.axis_index("fsdp").astype(jnp.int32) // 4
    slices = [lax.dynamic_slice(tokens, (0, (y + s) % 4 * 2048), (64, 2048)) for s in range(4)]
    *slices[1:], block, lengths = lax.optimization_barrier(
        (*slices[1:], projection, piece_lengths)
    )
    where = scalar_table(lengths, piece_owners)
    for s in (1, 3, 2):
        slices[s] = y_shift(slices[s], s)
    over_x = fsdp_flip(block, 2)
    over_core = fsdp_flip(block, 1)

    chosen = local_call(
        choose_kernel,
        "choose",
        [jax.ShapeDtypeStruct((512, 384), BF16)] * 2,
        (where, projection),
        2 * 512 * 512 * 768,
        scratch=[pltpu.VMEM((512, 512), BF16), pltpu.SemaphoreType.DMA],
        limit=8,
        anywhere=(1, 0),
    )
    over_x, where, *slices[1:] = lax.optimization_barrier((over_x, where, *slices[1:]))
    over_both = fsdp_flip(over_x, 1)
    (partial,) = local_call(
        front_kernel,
        "front",
        [jax.ShapeDtypeStruct((256, 512), F32)],
        (where, *slices, over_core, over_x, block),
        2 * 256 * 1536 * 512,
        scratch=[pltpu.VMEM((512, 512), BF16), pltpu.SemaphoreType.DMA],
        limit=8,
        anywhere=(1, 0),
    )
    mine, *partial = local_call(
        front_rest_kernel,
        "front_rest",
        [jax.ShapeDtypeStruct((64, 512), F32)] + [jax.ShapeDtypeStruct((64, 512), BF16)] * 3,
        (where, *slices, over_both, partial),
        2 * 256 * 512 * 512,
        limit=8,
    )
    same, cross, mine = lax.optimization_barrier((*chosen, mine))
    (projected,) = local_call(
        total_kernel,
        "total",
        [jax.ShapeDtypeStruct((64, 512), BF16)],
        (where, mine, *[y_shift(partial[s - 1], -s) for s in (1, 3, 2)]),
        64 * 512 * 4,
        limit=4,
    )

    (own,) = local_call(
        join_kernel,
        "join",
        [jax.ShapeDtypeStruct((512, 128), BF16)],
        (where, projected, tp_shift(projected, 0, 1)),
        64 * 512 * 4,
        limit=4,
    )
    up1, down1 = tp_shift(own, 1, 0), tp_shift(own, -1, 0)
    far = tp_shift(own, 4, 0)
    up2, down2 = tp_shift(up1, 1, 0), tp_shift(down1, -1, 0)
    table = [jax.ShapeDtypeStruct((512, FF), F32)]
    one = 2 * 512 * 128 * FF
    (gradient,) = local_call(
        functools.partial(sum_kernel, (0, 7, 1)),
        "near_terms",
        table,
        (where, own, up1, down1, grads),
        3 * one,
    )
    up2, down2, gradient = lax.optimization_barrier((up2, down2, gradient))
    up3, down3 = tp_shift(up2, 1, 0), tp_shift(down2, -1, 0)
    (gradient,) = local_call(
        functools.partial(sum_kernel, (6, 2)),
        "middle_terms",
        table,
        (where, up2, down2, grads, gradient),
        2 * one,
        aliases={4: 0},
    )
    give, keep = local_call(
        functools.partial(last_kernel, (5, 3, 4)),
        "last_terms",
        [
            jax.ShapeDtypeStruct((8, 48, FF), BF16),
            jax.ShapeDtypeStruct((8, 48, FF), F32),
        ],
        (where, up3, down3, far, grads, gradient),
        3 * one,
        scratch=[pltpu.VMEM((560, FF), F32)],
    )

    narrow, wide = jax.ShapeDtypeStruct((48, FF), BF16), jax.ShapeDtypeStruct((48, FF), F32)
    size = 48 * FF
    up_x, down_x, far_x, up, down, beside, far, mine = local_call(
        pair_kernel,
        "pair",
        [narrow] * 5 + [wide] * 3,
        (where, keep, fsdp_flip(give, 1)),
        8 * size,
        limit=8,
    )
    up_x, down_x, far_x = y_shift(up_x, 1), y_shift(down_x, -1), fsdp_flip(far_x, 2)
    up, down = y_shift(up, 1), y_shift(down, -1)
    (far,) = local_call(add_kernel, "add_far", [narrow], (where, far, far_x), size, limit=8)
    far, up, down = lax.optimization_barrier((far, up, down))
    far = y_shift(far, 2)
    (beside,) = local_call(
        add_kernel, "add_beside", [narrow], (where, beside, up_x, down_x), 2 * size, limit=8
    )
    beside = fsdp_flip(beside, 2)
    new_first, new_second, update = local_call(
        moments_kernel,
        "moments",
        [wide, wide, narrow],
        (where, mine, up, down, far, beside, first_moment, second_moment),
        30 * size,
        limit=8,
    )

    beside = fsdp_flip(update, 2)
    up, down, far = y_shift(update, 1), y_shift(update, -1), y_shift(update, 2)
    up_x, down_x, far_x = y_shift(beside, 1), y_shift(beside, -1), fsdp_flip(far, 2)
    updates = jnp.concatenate([update, beside, up, down, far, up_x, down_x, far_x], axis=0)
    crossed = fsdp_flip(updates, 1)
    (delta,) = local_call(
        half_delta_kernel, "half_delta", table, (where, same, updates), 2 * 512 * 384 * FF
    )
    (weight_delta,) = local_call(
        delta_kernel,
        "delta",
        [jax.ShapeDtypeStruct((512, FF), BF16)],
        (where, cross, crossed, delta),
        2 * 512 * 384 * FF,
        scratch=[pltpu.VMEM((512, FF), BF16), pltpu.SemaphoreType.DMA((7,))],
        anywhere=(0, 1),
    )
    return (weight_delta, new_first, new_second)


def solution(mesh):
    return jax.shard_map(
        per_device,
        mesh=mesh,
        in_specs=(
            P("fsdp", "tp", None),
            P("fsdp", None, "tp"),
            P("fsdp", None),
            P(),
            P(),
            P("fsdp", "tp"),
            P("fsdp", "tp"),
        ),
        out_specs=(P("fsdp", "tp"), P("fsdp", "tp"), P("fsdp", "tp")),
        check_vma=False,
    )
```

time: 128 us -> 117 us (0.914)
  blocking collectives: 42.1 us -> 0 us
  starting transfers between devices: 40.1 us -> 57.4 us
  waiting for transfers between devices: 23.8 us -> 37.3 us
  Pallas kernels: 15.6 us -> 19.9 us
  local copies, waits for them, and re-layouts: 3.21 us -> 1.48 us
  other arithmetic: 1.33 us -> 0 us
    all_to_all x2 -> x0, blocking collectives: 42.1 us -> none  [the longest x1 21.3 us: per_device(): terms = lax.all_to_all(pair, 'fsdp', 0, 0, axis_index_groups=CHIP_GROUPS)]
    ppermute x6 -> x16, starting transfers between devices: 8.96 us -> 21.8 us  [y_shift(): lax.ppermute(value, 'fsdp', [(i, (i + 4 * dy) % 16) for i in range(16)])]
    ppermute x6 -> x16, waiting for transfers between devices: 8.87 us -> 17.5 us  [y_shift(): lax.ppermute(value, 'fsdp', [(i, (i + 4 * dy) % 16) for i in range(16)])]
    ppermute x5 -> x9, starting transfers between devices: 14.4 us -> 20.1 us  [fsdp_flip(): return lax.ppermute(value, 'fsdp', [(i, i ^ flip) for i in range(16)])]
    pallas_call x9 -> x15, Pallas kernels: 15.6 us -> 19.9 us  [the longest x14 18.7 us: local_call(): pl.pallas_call(kernel, in_specs=[SCALARS] + in_vmem(len(operands) - 1 - a...]
    ppermute x8, waiting for transfers between devices: 8.11 us -> 11.6 us  [tp_shift(): return lax.ppermute(value, 'tp', pairs)]
    ppermute x5 -> x9, waiting for transfers between devices: 6.86 us -> 8.29 us  [fsdp_flip(): return lax.ppermute(value, 'fsdp', [(i, i ^ flip) for i in range(16)])]
  transfers between devices with their start and end apart: 19 -> 33, of which waited for: 11 -> 15; matrix products, arithmetic and copies ran while one was open for 3% -> 0% of each run, Pallas kernels for 4% -> 8%
where the time goes in v3:
time: 117 us
  starting transfers between devices  57.4 us (49%)
  waiting for transfers between devices  37.3 us (32%)
  Pallas kernels  19.9 us (17%)
  local copies, waits for them, and re-layouts  1.48 us (1%)
  between operations  1.18 us (1%)
    ppermute x16, starting transfers between devices, y_shift(): lax.ppermute(value, 'fsdp', [(i, (i + 4 * dy) % 16) for i in range(16)])  21.8 us
    ppermute x9, starting transfers between devices, fsdp_flip(): return lax.ppermute(value, 'fsdp', [(i, i ^ flip) for i in range(16)])  20.1 us
    pallas_call x14, Pallas kernels, local_call(): pl.pallas_call(kernel, in_specs=[SCALARS] + in_vmem(len(operands) - 1 - a...  18.7 us
    ppermute x16, waiting for transfers between devices, y_shift(): lax.ppermute(value, 'fsdp', [(i, (i + 4 * dy) % 16) for i in range(16)])  17.5 us
    ppermute x8, starting transfers between devices, tp_shift(): return lax.ppermute(value, 'tp', pairs)  15.5 us
    ppermute x8, waiting for transfers between devices, tp_shift(): return lax.ppermute(value, 'tp', pairs)  11.6 us
    ppermute x9, waiting for transfers between devices, fsdp_flip(): return lax.ppermute(value, 'fsdp', [(i, i ^ flip) for i in range(16)])  8.29 us
  transfers between devices with their start and end apart: 33, of which 15 were waited for; matrix products, arithmetic and copies ran while one was open for 0% of the time, Pallas kernels for 8%

profile of v3, /device:TPU:1, one launch (start us, length us, event | category | flops | bytes accessed | tf_op | source)
XLA Modules:
  0.0 117.4 jit_solution(4816927543020465983)
XLA Ops:
  2.1 2.1 %collective-permute-start = (bf16[512,512]{1,0:T(8,128)(2,1)S(1)}, bf16[512,512]{1,0:T(8,128)(2,1)S(1)}, u32[]{:S(2)}, u32[]{:S(2)}) collective-permute-start(bf16[512,512]{1,0:T(8,128)(2,1)S(1)} %copy-done.1), channel_id=1, source_target_pairs={{0,2},{1,3},{2,0},{3,1},{4,6},{5,7},{6,4},{7,5},{8,10},{9,11},{10,... | collective-permute-start | bytes 1572872 | tf_op jit(solution)/shard_map/ppermute | solution.py:26
  5.5 2.6 %collective-permute-start.2 = (bf16[64,2048]{1,0:T(8,128)(2,1)S(1)}, bf16[64,2048]{1,0:T(8,128)(2,1)S(1)}, u32[]{:S(2)}, u32[]{:S(2)}) collective-permute-start(bf16[64,2048]{1,0:T(8,128)(2,1)S(1)} %get-tuple-element.44), channel_id=1, source_target_pairs={{0,8},{1,9},{2,10},{3,11},{4,12},{5,13},{6,14},{7,15},{8,0},{9,1},... | collective-permute-start | bytes 786440 | tf_op jit(solution)/shard_map/ppermute | solution.py:30
  12.3 6.9 %collective-permute-done.2.a2 = bf16[64,2048]{1,0:T(8,128)(2,1)S(1)} collective-permute-done((bf16[64,2048]{1,0:T(8,128)(2,1)S(1)}, bf16[64,2048]{1,0:T(8,128)(2,1)S(1)}, u32[]{:S(2)}, u32[]{:S(2)}) %collective-permute-start.2) | collective-permute-done | bytes 262176 | tf_op jit(solution)/shard_map/ppermute | solution.py:30
  25.3 2.0 %collective-permute-start.8 = (bf16[64,512]{1,0:T(8,128)(2,1)S(1)}, bf16[64,512]{1,0:T(8,128)(2,1)S(1)}, u32[]{:S(2)}, u32[]{:S(2)}) collective-permute-start(bf16[64,512]{1,0:T(8,128)(2,1)S(1)} %get-tuple-element.58), channel_id=1, source_target_pairs={{0,8},{1,9},{2,10},{3,11},{4,12},{5,13},{6,14},{7,15},{8,0},{9,1},... | collective-permute-start | bytes 196616 | tf_op jit(solution)/shard_map/ppermute | solution.py:30
  31.1 2.5 %collective-permute-start.9 = (bf16[64,512]{1,0:T(8,128)(2,1)S(1)}, bf16[64,512]{1,0:T(8,128)(2,1)S(1)}, u32[]{:S(2)}, u32[]{:S(2)}) collective-permute-start(bf16[64,512]{1,0:T(8,128)(2,1)S(1)} %total.1.mine), channel_id=1, source_target_pairs={{0,16},{16,0},{32,48},{48,32},{64,80},{80,64},{96,112},{112,96},{1... | collective-permute-start | bytes 196616 | tf_op jit(solution)/shard_map/ppermute | solution.py:35
  33.6 2.2 %collective-permute-done.9.partner = bf16[64,512]{1,0:T(8,128)(2,1)S(1)} collective-permute-done((bf16[64,512]{1,0:T(8,128)(2,1)S(1)}, bf16[64,512]{1,0:T(8,128)(2,1)S(1)}, u32[]{:S(2)}, u32[]{:S(2)}) %collective-permute-start.9) | collective-permute-done | bytes 65568 | tf_op jit(solution)/shard_map/ppermute | solution.py:35
  36.5 5.7 %collective-permute-start.12 = (bf16[512,128]{1,0:T(8,128)(2,1)S(1)}, bf16[512,128]{1,0:T(8,128)(2,1)S(1)}, u32[]{:S(2)}, u32[]{:S(2)}) collective-permute-start(bf16[512,128]{1,0:T(8,128)(2,1)S(1)} %join.1.refs_0_), channel_id=1, source_target_pairs={{0,224},{16,240},{32,0},{48,16},{64,32},{80,48},{96,64},{112,80},{... | collective-permute-start | bytes 393224 | tf_op jit(solution)/shard_map/ppermute | solution.py:35
  42.1 1.9 %collective-permute-done.12.refs_2_ = bf16[512,128]{1,0:T(8,128)(2,1)S(1)} collective-permute-done((bf16[512,128]{1,0:T(8,128)(2,1)S(1)}, bf16[512,128]{1,0:T(8,128)(2,1)S(1)}, u32[]{:S(2)}, u32[]{:S(2)}) %collective-permute-start.12) | collective-permute-done | bytes 131104 | tf_op jit(solution)/shard_map/ppermute | solution.py:35
  44.1 3.1 %collective-permute-start.13 = (bf16[512,128]{1,0:T(8,128)(2,1)S(1)}, bf16[512,128]{1,0:T(8,128)(2,1)S(1)}, u32[]{:S(2)}, u32[]{:S(2)}) collective-permute-start(bf16[512,128]{1,0:T(8,128)(2,1)S(1)} %collective-permute-done.12.refs_2_), channel_id=1, source_target_pairs={{0,224},{16,240},{32,0},{48,16},{64,32},{80,48},{96,64},{112,80},{... | collective-permute-start | bytes 393224 | tf_op jit(solution)/shard_map/ppermute | solution.py:35
  50.4 4.3 %collective-permute-done.11.refs_0_ = bf16[512,128]{1,0:T(8,128)(2,1)S(1)} collective-permute-done((bf16[512,128]{1,0:T(8,128)(2,1)S(1)}, bf16[512,128]{1,0:T(8,128)(2,1)S(1)}, u32[]{:S(2)}, u32[]{:S(2)}) %collective-permute-start.11) | collective-permute-done | bytes 131104 | tf_op jit(solution)/shard_map/ppermute | solution.py:35
  54.8 2.7 %collective-permute-start.15 = (bf16[512,128]{1,0:T(8,128)(2,1)S(1)}, bf16[512,128]{1,0:T(8,128)(2,1)S(1)}, u32[]{:S(2)}, u32[]{:S(2)}) collective-permute-start(bf16[512,128]{1,0:T(8,128)(2,1)S(1)} %collective-permute-done.13.refs_1_), channel_id=1, source_target_pairs={{0,224},{16,240},{32,0},{48,16},{64,32},{80,48},{96,64},{112,80},{... | collective-permute-start | bytes 393224 | tf_op jit(solution)/shard_map/ppermute | solution.py:35
  58.7 3.1 %collective-permute-done.14.refs_0_ = bf16[512,128]{1,0:T(8,128)(2,1)S(1)} collective-permute-done((bf16[512,128]{1,0:T(8,128)(2,1)S(1)}, bf16[512,128]{1,0:T(8,128)(2,1)S(1)}, u32[]{:S(2)}, u32[]{:S(2)}) %collective-permute-start.14) | collective-permute-done | bytes 131104 | tf_op jit(solution)/shard_map/ppermute | solution.py:35
  61.8 3.4 %last_terms.1 = (bf16[8,48,1792]{2,1,0:T(8,128)(2,1)S(1)}, f32[8,48,1792]{2,1,0:T(8,128)S(1)}) custom-call(s32[48]{0:T(128)S(1)} %table.1.where._, bf16[512,128]{1,0:T(8,128)(2,1)S(1)} %collective-permute-done.14.refs_0_, bf16[512,128]{1,0:T(8,128)(2,1)S(1)} %collective-permute-done.15.refs_1_, bf16[512,128]{1,0:T(8,128)(2,1)S(1)} %collective-permute-done.16.refs_2_, ...), custom_call_target="tpu_custom_call" | custom-call | flops 704643072 | bytes 7733440 | tf_op jit(solution)/shard_map/last_terms/pallas_call | solution.py:50
  65.2 3.2 %collective-permute-start.17 = (bf16[8,48,1792]{2,1,0:T(8,128)(2,1)S(1)}, bf16[8,48,1792]{2,1,0:T(8,128)(2,1)S(1)}, u32[]{:S(2)}, u32[]{:S(2)}) collective-permute-start(bf16[8,48,1792]{2,1,0:T(8,128)(2,1)S(1)} %get-tuple-element.63), channel_id=1, source_target_pairs={{0,1},{1,0},{2,3},{3,2},{4,5},{5,4},{6,7},{7,6},{8,9},{9,8},{10,11... | collective-permute-start | bytes 4128776 | tf_op jit(solution)/shard_map/ppermute | solution.py:26
  68.4 2.8 %collective-permute-done.17.given = bf16[8,48,1792]{2,1,0:T(8,128)(2,1)S(1)} collective-permute-done((bf16[8,48,1792]{2,1,0:T(8,128)(2,1)S(1)}, bf16[8,48,1792]{2,1,0:T(8,128)(2,1)S(1)}, u32[]{:S(2)}, u32[]{:S(2)}) %collective-permute-start.17) | collective-permute-done | bytes 1376288 | tf_op jit(solution)/shard_map/ppermute | solution.py:26
  72.6 2.4 %collective-permute-start.20 = (bf16[48,1792]{1,0:T(8,128)(2,1)S(1)}, bf16[48,1792]{1,0:T(8,128)(2,1)S(1)}, u32[]{:S(2)}, u32[]{:S(2)}) collective-permute-start(bf16[48,1792]{1,0:T(8,128)(2,1)S(1)} %get-tuple-element.68), channel_id=1, source_target_pairs={{0,12},{1,13},{2,14},{3,15},{4,0},{5,1},{6,2},{7,3},{8,4},{9,5},{1... | collective-permute-start | bytes 516104 | tf_op jit(solution)/shard_map/ppermute | solution.py:30
  74.9 2.7 %collective-permute-start.23 = (bf16[48,1792]{1,0:T(8,128)(2,1)S(1)}, bf16[48,1792]{1,0:T(8,128)(2,1)S(1)}, u32[]{:S(2)}, u32[]{:S(2)}) collective-permute-start(bf16[48,1792]{1,0:T(8,128)(2,1)S(1)} %get-tuple-element.74), channel_id=1, source_target_pairs={{0,12},{1,13},{2,14},{3,15},{4,0},{5,1},{6,2},{7,3},{8,4},{9,5},{1... | collective-permute-start | bytes 516104 | tf_op jit(solution)/shard_map/ppermute | solution.py:30
  78.7 2.1 %collective-permute-start.21 = (bf16[48,1792]{1,0:T(8,128)(2,1)S(1)}, bf16[48,1792]{1,0:T(8,128)(2,1)S(1)}, u32[]{:S(2)}, u32[]{:S(2)}) collective-permute-start(bf16[48,1792]{1,0:T(8,128)(2,1)S(1)} %add_far.1), channel_id=1, source_target_pairs={{0,8},{1,9},{2,10},{3,11},{4,12},{5,13},{6,14},{7,15},{8,0},{9,1},... | collective-permute-start | bytes 516104 | tf_op jit(solution)/shard_map/ppermute | solution.py:30
  84.5 2.3 %collective-permute-done.21.t3 = bf16[48,1792]{1,0:T(8,128)(2,1)S(1)} collective-permute-done((bf16[48,1792]{1,0:T(8,128)(2,1)S(1)}, bf16[48,1792]{1,0:T(8,128)(2,1)S(1)}, u32[]{:S(2)}, u32[]{:S(2)}) %collective-permute-start.21) | collective-permute-done | bytes 172064 | tf_op jit(solution)/shard_map/ppermute | solution.py:30
  94.1 3.0 %collective-permute-done.25 = bf16[48,1792]{1,0:T(8,128)(2,1)S(1)} collective-permute-done((bf16[48,1792]{1,0:T(8,128)(2,1)S(1)}, bf16[48,1792]{1,0:T(8,128)(2,1)S(1)}, u32[]{:S(2)}, u32[]{:S(2)}) %collective-permute-start.25) | collective-permute-done | bytes 172064 | tf_op jit(solution)/shard_map/ppermute | solution.py:26
  97.1 2.1 %collective-permute-start.30 = (bf16[48,1792]{1,0:T(8,128)(2,1)S(1)}, bf16[48,1792]{1,0:T(8,128)(2,1)S(1)}, u32[]{:S(2)}, u32[]{:S(2)}) collective-permute-start(bf16[48,1792]{1,0:T(8,128)(2,1)S(1)} %collective-permute-done.25), channel_id=1, source_target_pairs={{0,12},{1,13},{2,14},{3,15},{4,0},{5,1},{6,2},{7,3},{8,4},{9,5},{1... | collective-permute-start | bytes 516104 | tf_op jit(solution)/shard_map/ppermute | solution.py:30
  100.6 4.2 %collective-permute-done.29 = bf16[48,1792]{1,0:T(8,128)(2,1)S(1)} collective-permute-done((bf16[48,1792]{1,0:T(8,128)(2,1)S(1)}, bf16[48,1792]{1,0:T(8,128)(2,1)S(1)}, u32[]{:S(2)}, u32[]{:S(2)}) %collective-permute-start.29) | collective-permute-done | bytes 172064 | tf_op jit(solution)/shard_map/ppermute | solution.py:30
  104.8 7.1 %collective-permute-start.32 = (bf16[384,1792]{1,0:T(8,128)(2,1)S(1)}, bf16[384,1792]{1,0:T(8,128)(2,1)S(1)}, u32[]{:S(2)}, u32[]{:S(2)}) collective-permute-start(bf16[384,1792]{1,0:T(8,128)(2,1)S(1)} %constant_dynamic-update-slice_fusion.updates), channel_id=1, source_target_pairs={{0,1},{1,0},{2,3},{3,2},{4,5},{5,4},{6,7},{7,6},{8,9},{9,8},{10,11... | collective-permute-start | bytes 4128776 | tf_op jit(solution)/shard_map/ppermute | solution.py:26
  114.7 2.5 %delta.1 = bf16[512,1792]{1,0:T(8,128)(2,1)} custom-call(s32[48]{0:T(128)S(1)} %table.1.where._, bf16[512,384]{1,0:T(8,128)(2,1)S(1)} %get-tuple-element.54.chosen, bf16[384,1792]{1,0:T(8,128)(2,1)S(1)} %collective-permute-done.32.updates, f32[512,1792]{1,0:T(8,128)S(1)} %half_delta.1.before), custom_call_target="tpu_custom_call" | custom-call | flops 704643072 | bytes 5439680 | tf_op jit(solution)/shard_map/delta/pallas_call | solution.py:50
  (78 shorter events, 39.4 us)
Async XLA Ops:
  2.1 17.1 %collective-permute-start = (bf16[512,512]{1,0:T(8,128)(2,1)S(1)}, bf16[512,512]{1,0:T(8,128)(2,1)S(1)}, u32[]{:S(2)}, u32[]{:S(2)}) collective-permute-start(bf16[512,512]{1,0:T(8,128)(2,1)S(1)} %copy-done.1), channel_id=1, source_target_pairs={{0,2},{1,3},{2,0},{3,1},{4,6},{5,7},{6,4},{7,5},{8,10},{9,11},{10,... | collective-permute-start | bytes 1572872 | tf_op jit(solution)/shard_map/ppermute | solution.py:26
  4.3 8.0 %collective-permute-start.1 = (bf16[64,2048]{1,0:T(8,128)(2,1)S(1)}, bf16[64,2048]{1,0:T(8,128)(2,1)S(1)}, u32[]{:S(2)}, u32[]{:S(2)}) collective-permute-start(bf16[64,2048]{1,0:T(8,128)(2,1)S(1)} %get-tuple-element.43), channel_id=1, source_target_pairs={{0,4},{1,5},{2,6},{3,7},{4,8},{5,9},{6,10},{7,11},{8,12},{9,13},{1... | collective-permute-start | bytes 786440 | tf_op jit(solution)/shard_map/ppermute | solution.py:30
  5.5 13.6 %collective-permute-start.2 = (bf16[64,2048]{1,0:T(8,128)(2,1)S(1)}, bf16[64,2048]{1,0:T(8,128)(2,1)S(1)}, u32[]{:S(2)}, u32[]{:S(2)}) collective-permute-start(bf16[64,2048]{1,0:T(8,128)(2,1)S(1)} %get-tuple-element.44), channel_id=1, source_target_pairs={{0,8},{1,9},{2,10},{3,11},{4,12},{5,13},{6,14},{7,15},{8,0},{9,1},... | collective-permute-start | bytes 786440 | tf_op jit(solution)/shard_map/ppermute | solution.py:30
  8.2 11.0 %collective-permute-start.3 = (bf16[64,2048]{1,0:T(8,128)(2,1)S(1)}, bf16[64,2048]{1,0:T(8,128)(2,1)S(1)}, u32[]{:S(2)}, u32[]{:S(2)}) collective-permute-start(bf16[64,2048]{1,0:T(8,128)(2,1)S(1)} %get-tuple-element.45), channel_id=1, source_target_pairs={{0,12},{1,13},{2,14},{3,15},{4,0},{5,1},{6,2},{7,3},{8,4},{9,5},{1... | collective-permute-start | bytes 786440 | tf_op jit(solution)/shard_map/ppermute | solution.py:30
  9.2 11.8 %collective-permute-start.5 = (bf16[512,512]{1,0:T(8,128)(2,1)S(1)}, bf16[512,512]{1,0:T(8,128)(2,1)S(1)}, u32[]{:S(2)}, u32[]{:S(2)}) collective-permute-start(bf16[512,512]{1,0:T(8,128)(2,1)S(1)} %copy-done.1), channel_id=1, source_target_pairs={{0,1},{1,0},{2,3},{3,2},{4,5},{5,4},{6,7},{7,6},{8,9},{9,8},{10,11... | collective-permute-start | bytes 1572872 | tf_op jit(solution)/shard_map/ppermute | solution.py:26
  36.5 7.6 %collective-permute-start.12 = (bf16[512,128]{1,0:T(8,128)(2,1)S(1)}, bf16[512,128]{1,0:T(8,128)(2,1)S(1)}, u32[]{:S(2)}, u32[]{:S(2)}) collective-permute-start(bf16[512,128]{1,0:T(8,128)(2,1)S(1)} %join.1.refs_0_), channel_id=1, source_target_pairs={{0,224},{16,240},{32,0},{48,16},{64,32},{80,48},{96,64},{112,80},{... | collective-permute-start | bytes 393224 | tf_op jit(solution)/shard_map/ppermute | solution.py:35
  44.1 6.3 %collective-permute-start.13 = (bf16[512,128]{1,0:T(8,128)(2,1)S(1)}, bf16[512,128]{1,0:T(8,128)(2,1)S(1)}, u32[]{:S(2)}, u32[]{:S(2)}) collective-permute-start(bf16[512,128]{1,0:T(8,128)(2,1)S(1)} %collective-permute-done.12.refs_2_), channel_id=1, source_target_pairs={{0,224},{16,240},{32,0},{48,16},{64,32},{80,48},{96,64},{112,80},{... | collective-permute-start | bytes 393224 | tf_op jit(solution)/shard_map/ppermute | solution.py:35
  47.1 7.6 %collective-permute-start.11 = (bf16[512,128]{1,0:T(8,128)(2,1)S(1)}, bf16[512,128]{1,0:T(8,128)(2,1)S(1)}, u32[]{:S(2)}, u32[]{:S(2)}) collective-permute-start(bf16[512,128]{1,0:T(8,128)(2,1)S(1)} %collective-permute-done.10.refs_1_), channel_id=1, source_target_pairs={{0,32},{16,48},{32,64},{48,80},{64,96},{80,112},{96,128},{112,144}... | collective-permute-start | bytes 393224 | tf_op jit(solution)/shard_map/ppermute | solution.py:35
  47.1 11.5 %collective-permute-start.16 = (bf16[512,128]{1,0:T(8,128)(2,1)S(1)}, bf16[512,128]{1,0:T(8,128)(2,1)S(1)}, u32[]{:S(2)}, u32[]{:S(2)}) collective-permute-start(bf16[512,128]{1,0:T(8,128)(2,1)S(1)} %join.1.refs_0_), channel_id=1, source_target_pairs={{0,128},{16,144},{32,160},{48,176},{64,192},{80,208},{96,224},{112... | collective-permute-start | bytes 393224 | tf_op jit(solution)/shard_map/ppermute | solution.py:35
  54.7 7.0 %collective-permute-start.14 = (bf16[512,128]{1,0:T(8,128)(2,1)S(1)}, bf16[512,128]{1,0:T(8,128)(2,1)S(1)}, u32[]{:S(2)}, u32[]{:S(2)}) collective-permute-start(bf16[512,128]{1,0:T(8,128)(2,1)S(1)} %collective-permute-done.11.refs_0_), channel_id=1, source_target_pairs={{0,32},{16,48},{32,64},{48,80},{64,96},{80,112},{96,128},{112,144}... | collective-permute-start | bytes 393224 | tf_op jit(solution)/shard_map/ppermute | solution.py:35
  54.8 7.0 %collective-permute-start.15 = (bf16[512,128]{1,0:T(8,128)(2,1)S(1)}, bf16[512,128]{1,0:T(8,128)(2,1)S(1)}, u32[]{:S(2)}, u32[]{:S(2)}) collective-permute-start(bf16[512,128]{1,0:T(8,128)(2,1)S(1)} %collective-permute-done.13.refs_1_), channel_id=1, source_target_pairs={{0,224},{16,240},{32,0},{48,16},{64,32},{80,48},{96,64},{112,80},{... | collective-permute-start | bytes 393224 | tf_op jit(solution)/shard_map/ppermute | solution.py:35
  65.2 5.9 %collective-permute-start.17 = (bf16[8,48,1792]{2,1,0:T(8,128)(2,1)S(1)}, bf16[8,48,1792]{2,1,0:T(8,128)(2,1)S(1)}, u32[]{:S(2)}, u32[]{:S(2)}) collective-permute-start(bf16[8,48,1792]{2,1,0:T(8,128)(2,1)S(1)} %get-tuple-element.63), channel_id=1, source_target_pairs={{0,1},{1,0},{2,3},{3,2},{4,5},{5,4},{6,7},{7,6},{8,9},{9,8},{10,11... | collective-permute-start | bytes 4128776 | tf_op jit(solution)/shard_map/ppermute | solution.py:26
  71.9 5.7 %collective-permute-start.18 = (bf16[48,1792]{1,0:T(8,128)(2,1)S(1)}, bf16[48,1792]{1,0:T(8,128)(2,1)S(1)}, u32[]{:S(2)}, u32[]{:S(2)}) collective-permute-start(bf16[48,1792]{1,0:T(8,128)(2,1)S(1)} %get-tuple-element.66), channel_id=1, source_target_pairs={{0,2},{1,3},{2,0},{3,1},{4,6},{5,7},{6,4},{7,5},{8,10},{9,11},{10,... | collective-permute-start | bytes 516104 | tf_op jit(solution)/shard_map/ppermute | solution.py:26
  72.3 6.5 %collective-permute-start.19 = (bf16[48,1792]{1,0:T(8,128)(2,1)S(1)}, bf16[48,1792]{1,0:T(8,128)(2,1)S(1)}, u32[]{:S(2)}, u32[]{:S(2)}) collective-permute-start(bf16[48,1792]{1,0:T(8,128)(2,1)S(1)} %get-tuple-element.67), channel_id=1, source_target_pairs={{0,4},{1,5},{2,6},{3,7},{4,8},{5,9},{6,10},{7,11},{8,12},{9,13},{1... | collective-permute-start | bytes 516104 | tf_op jit(solution)/shard_map/ppermute | solution.py:30
  72.6 6.2 %collective-permute-start.20 = (bf16[48,1792]{1,0:T(8,128)(2,1)S(1)}, bf16[48,1792]{1,0:T(8,128)(2,1)S(1)}, u32[]{:S(2)}, u32[]{:S(2)}) collective-permute-start(bf16[48,1792]{1,0:T(8,128)(2,1)S(1)} %get-tuple-element.68), channel_id=1, source_target_pairs={{0,12},{1,13},{2,14},{3,15},{4,0},{5,1},{6,2},{7,3},{8,4},{9,5},{1... | collective-permute-start | bytes 516104 | tf_op jit(solution)/shard_map/ppermute | solution.py:30
  74.9 7.7 %collective-permute-start.22 = (bf16[48,1792]{1,0:T(8,128)(2,1)S(1)}, bf16[48,1792]{1,0:T(8,128)(2,1)S(1)}, u32[]{:S(2)}, u32[]{:S(2)}) collective-permute-start(bf16[48,1792]{1,0:T(8,128)(2,1)S(1)} %get-tuple-element.73), channel_id=1, source_target_pairs={{0,4},{1,5},{2,6},{3,7},{4,8},{5,9},{6,10},{7,11},{8,12},{9,13},{1... | collective-permute-start | bytes 516104 | tf_op jit(solution)/shard_map/ppermute | solution.py:30
  74.9 7.7 %collective-permute-start.23 = (bf16[48,1792]{1,0:T(8,128)(2,1)S(1)}, bf16[48,1792]{1,0:T(8,128)(2,1)S(1)}, u32[]{:S(2)}, u32[]{:S(2)}) collective-permute-start(bf16[48,1792]{1,0:T(8,128)(2,1)S(1)} %get-tuple-element.74), channel_id=1, source_target_pairs={{0,12},{1,13},{2,14},{3,15},{4,0},{5,1},{6,2},{7,3},{8,4},{9,5},{1... | collective-permute-start | bytes 516104 | tf_op jit(solution)/shard_map/ppermute | solution.py:30
  78.7 8.0 %collective-permute-start.21 = (bf16[48,1792]{1,0:T(8,128)(2,1)S(1)}, bf16[48,1792]{1,0:T(8,128)(2,1)S(1)}, u32[]{:S(2)}, u32[]{:S(2)}) collective-permute-start(bf16[48,1792]{1,0:T(8,128)(2,1)S(1)} %add_far.1), channel_id=1, source_target_pairs={{0,8},{1,9},{2,10},{3,11},{4,12},{5,13},{6,14},{7,15},{8,0},{9,1},... | collective-permute-start | bytes 516104 | tf_op jit(solution)/shard_map/ppermute | solution.py:30
  89.5 9.8 %collective-permute-start.28 = (bf16[48,1792]{1,0:T(8,128)(2,1)S(1)}, bf16[48,1792]{1,0:T(8,128)(2,1)S(1)}, u32[]{:S(2)}, u32[]{:S(2)}) collective-permute-start(bf16[48,1792]{1,0:T(8,128)(2,1)S(1)} %get-tuple-element.75), channel_id=1, source_target_pairs={{0,8},{1,9},{2,10},{3,11},{4,12},{5,13},{6,14},{7,15},{8,0},{9,1},... | collective-permute-start | bytes 516104 | tf_op jit(solution)/shard_map/ppermute | solution.py:30
  91.4 9.1 %collective-permute-start.27 = (bf16[48,1792]{1,0:T(8,128)(2,1)S(1)}, bf16[48,1792]{1,0:T(8,128)(2,1)S(1)}, u32[]{:S(2)}, u32[]{:S(2)}) collective-permute-start(bf16[48,1792]{1,0:T(8,128)(2,1)S(1)} %get-tuple-element.75), channel_id=1, source_target_pairs={{0,12},{1,13},{2,14},{3,15},{4,0},{5,1},{6,2},{7,3},{8,4},{9,5},{1... | collective-permute-start | bytes 516104 | tf_op jit(solution)/shard_map/ppermute | solution.py:30
  92.3 8.2 %collective-permute-start.26 = (bf16[48,1792]{1,0:T(8,128)(2,1)S(1)}, bf16[48,1792]{1,0:T(8,128)(2,1)S(1)}, u32[]{:S(2)}, u32[]{:S(2)}) collective-permute-start(bf16[48,1792]{1,0:T(8,128)(2,1)S(1)} %get-tuple-element.75), channel_id=1, source_target_pairs={{0,4},{1,5},{2,6},{3,7},{4,8},{5,9},{6,10},{7,11},{8,12},{9,13},{1... | collective-permute-start | bytes 516104 | tf_op jit(solution)/shard_map/ppermute | solution.py:30
  97.1 7.6 %collective-permute-start.30 = (bf16[48,1792]{1,0:T(8,128)(2,1)S(1)}, bf16[48,1792]{1,0:T(8,128)(2,1)S(1)}, u32[]{:S(2)}, u32[]{:S(2)}) collective-permute-start(bf16[48,1792]{1,0:T(8,128)(2,1)S(1)} %collective-permute-done.25), channel_id=1, source_target_pairs={{0,12},{1,13},{2,14},{3,15},{4,0},{5,1},{6,2},{7,3},{8,4},{9,5},{1... | collective-permute-start | bytes 516104 | tf_op jit(solution)/shard_map/ppermute | solution.py:30
  99.3 5.5 %collective-permute-start.31 = (bf16[48,1792]{1,0:T(8,128)(2,1)S(1)}, bf16[48,1792]{1,0:T(8,128)(2,1)S(1)}, u32[]{:S(2)}, u32[]{:S(2)}) collective-permute-start(bf16[48,1792]{1,0:T(8,128)(2,1)S(1)} %collective-permute-done.28), channel_id=1, source_target_pairs={{0,2},{1,3},{2,0},{3,1},{4,6},{5,7},{6,4},{7,5},{8,10},{9,11},{10,... | collective-permute-start | bytes 516104 | tf_op jit(solution)/shard_map/ppermute | solution.py:26
  104.8 9.8 %collective-permute-start.32 = (bf16[384,1792]{1,0:T(8,128)(2,1)S(1)}, bf16[384,1792]{1,0:T(8,128)(2,1)S(1)}, u32[]{:S(2)}, u32[]{:S(2)}) collective-permute-start(bf16[384,1792]{1,0:T(8,128)(2,1)S(1)} %constant_dynamic-update-slice_fusion.updates), channel_id=1, source_target_pairs={{0,1},{1,0},{2,3},{3,2},{4,5},{5,4},{6,7},{7,6},{8,9},{9,8},{10,11... | collective-permute-start | bytes 4128776 | tf_op jit(solution)/shard_map/ppermute | solution.py:26
  (15 other events, 123.5 us)

commit v4 on v3

--- a/solution.py
+++ b/solution.py
@@ -44,9 +44,11 @@
 
 
 def local_call(
-    kernel, name, out_shape, operands, flops, scratch=(), limit=24, aliases=None, anywhere=(0, 0)
+    kernel, name, out_shape, operands, flops, scratch=(), limit=24, aliases=None, anywhere=(0, 0), cheap=False
 ):
     size = sum(v.size * v.dtype.itemsize for v in operands)
+    if cheap:
+        flops, size = 1 << 10, 1 << 10
     return pl.pallas_call(
         kernel,
         in_specs=[SCALARS] + in_vmem(len(operands) - 1 - anywhere[0]) + [ANYWHERE] * anywhere[0],
@@ -177,8 +179,8 @@
         keep[i] = rows_from(table, where[START + owner_of(where, dy, dx, 0)])
 
 
-def pair_kernel(_, keep, given, *outs):
-    for i, out in enumerate(outs):
+def pair_kernel(first, _, keep, given, *outs):
+    for i, out in enumerate(outs, first):
         out[...] = (keep[i] + given[i].astype(F32)).astype(out.dtype)
 
 
@@ -186,18 +188,24 @@
     total = refs[0][...]
     for r in refs[1:-1]:
         total = total + r[...].astype(F32)
-    refs[-1][...] = total.astype(BF16)
-
-
-def moments_kernel(where, own, t1, t2, t3, t4, first, second, new_first, new_second, update):
+    refs[-1][...] = total.astype(refs[-1].dtype)
+
+
+def update_kernel(where, own, t1, t2, first, second, update, gradient):
     live = lax.broadcasted_iota(jnp.int32, (48, FF), 0) < where[LENGTH + where[F]]
-    gradient = own[...]
-    for t in (t1, t2, t3, t4):
-        gradient = gradient + t[...].astype(F32)
-    one, two, three = adam_rows(gradient, live, first[...], second[...])
+    total = own[...]
+    for t in (t1, t2):
+        total = total + t[...].astype(F32)
+    gradient[...] = total
+    update[...] = adam_rows(total, live, first[...], second[...])[2]
+
+
+def moments_kernel(where, update, gradient, first, second, again, new_first, new_second):
+    live = lax.broadcasted_iota(jnp.int32, (48, FF), 0) < where[LENGTH + where[F]]
+    again[...] = update[...]
+    one, two, _ = adam_rows(gradient[...], live, first[...], second[...])
     new_first[...] = one
     new_second[...] = two
-    update[...] = three
 
 
 def half_delta_kernel(_, chosen, updates, out):
@@ -305,6 +313,7 @@
         table,
         (where, own, up1, down1, grads),
         3 * one,
+        cheap=True,
     )
     up2, down2, gradient = lax.optimization_barrier((up2, down2, gradient))
     up3, down3 = tp_shift(up2, 1, 0), tp_shift(down2, -1, 0)
@@ -315,6 +324,7 @@
         (where, up2, down2, grads, gradient),
         2 * one,
         aliases={4: 0},
+        cheap=True,
     )
     give, keep = local_call(
         functools.partial(last_kernel, (5, 3, 4)),
@@ -330,33 +340,52 @@
 
     narrow, wide = jax.ShapeDtypeStruct((48, FF), BF16), jax.ShapeDtypeStruct((48, FF), F32)
     size = 48 * FF
-    up_x, down_x, far_x, up, down, beside, far, mine = local_call(
-        pair_kernel,
-        "pair",
-        [narrow] * 5 + [wide] * 3,
-        (where, keep, fsdp_flip(give, 1)),
-        8 * size,
+    given = fsdp_flip(give, 1)
+    up_x, down_x, far_x = local_call(
+        functools.partial(pair_kernel, 0),
+        "pair_first",
+        [narrow] * 3,
+        (where, keep, given),
+        3 * size,
         limit=8,
     )
     up_x, down_x, far_x = y_shift(up_x, 1), y_shift(down_x, -1), fsdp_flip(far_x, 2)
+    up, down, beside, far, mine = local_call(
+        functools.partial(pair_kernel, 3),
+        "pair_rest",
+        [narrow] * 2 + [wide] * 3,
+        (where, keep, given),
+        5 * size,
+        limit=8,
+    )
     up, down = y_shift(up, 1), y_shift(down, -1)
     (far,) = local_call(add_kernel, "add_far", [narrow], (where, far, far_x), size, limit=8)
-    far, up, down = lax.optimization_barrier((far, up, down))
     far = y_shift(far, 2)
+    (mine,) = local_call(
+        add_kernel, "add_direct", [wide], (where, mine, up, down), 2 * size, limit=8
+    )
     (beside,) = local_call(
         add_kernel, "add_beside", [narrow], (where, beside, up_x, down_x), 2 * size, limit=8
     )
     beside = fsdp_flip(beside, 2)
-    new_first, new_second, update = local_call(
+    update, gradient = local_call(
+        update_kernel,
+        "update",
+        [narrow, wide],
+        (where, mine, far, beside, first_moment, second_moment),
+        30 * size,
+        limit=8,
+    )
+
+    beside = fsdp_flip(update, 2)
+    update, new_first, new_second = local_call(
         moments_kernel,
         "moments",
-        [wide, wide, narrow],
-        (where, mine, up, down, far, beside, first_moment, second_moment),
+        [narrow, wide, wide],
+        (where, update, gradient, first_moment, second_moment),
         30 * size,
         limit=8,
     )
-
-    beside = fsdp_flip(update, 2)
     up, down, far = y_shift(update, 1), y_shift(update, -1), y_shift(update, 2)
     up_x, down_x, far_x = y_shift(beside, 1), y_shift(beside, -1), fsdp_flip(far, 2)
     updates = jnp.concatenate([update, beside, up, down, far, up_x, down_x, far_x], axis=0)

time: 117 us -> 113 us (0.966)
  starting transfers between devices: 57.4 us -> 50.1 us
  Pallas kernels: 19.9 us -> 21.8 us
    ppermute x9, starting transfers between devices: 20.1 us -> 13.6 us  [fsdp_flip(): return lax.ppermute(value, 'fsdp', [(i, i ^ flip) for i in range(16)])]
    ppermute x16, waiting for transfers between devices: 17.5 us -> 22.4 us  [y_shift(): lax.ppermute(value, 'fsdp', [(i, (i + 4 * dy) % 16) for i in range(16)])]
    ppermute x9, waiting for transfers between devices: 8.29 us -> 4.19 us  [fsdp_flip(): return lax.ppermute(value, 'fsdp', [(i, i ^ flip) for i in range(16)])]
    pallas_call x14 -> x17, Pallas kernels: 18.7 us -> 20.6 us  [local_call(): pl.pallas_call(kernel, in_specs=[SCALARS] + in_vmem(len(operands) - 1 - a...]
  transfers between devices with their start and end apart: 33 -> 33, of which waited for: 15 -> 14; matrix products, arithmetic and copies ran while one was open for 0% -> 0% of each run, Pallas kernels for 8% -> 11%
where the time goes in v4:
time: 113 us
  starting transfers between devices  50.1 us (44%)
  waiting for transfers between devices  38.2 us (34%)
  Pallas kernels  21.8 us (19%)
  local copies, waits for them, and re-layouts  1.48 us (1%)
  between operations  1.21 us (1%)
    ppermute x16, waiting for transfers between devices, y_shift(): lax.ppermute(value, 'fsdp', [(i, (i + 4 * dy) % 16) for i in range(16)])  22.4 us
    ppermute x16, starting transfers between devices, y_shift(): lax.ppermute(value, 'fsdp', [(i, (i + 4 * dy) % 16) for i in range(16)])  21 us
    pallas_call x17, Pallas kernels, local_call(): pl.pallas_call(kernel, in_specs=[SCALARS] + in_vmem(len(operands) - 1 - a...  20.6 us
    ppermute x8, starting transfers between devices, tp_shift(): return lax.ppermute(value, 'tp', pairs)  15.5 us
    ppermute x9, starting transfers between devices, fsdp_flip(): return lax.ppermute(value, 'fsdp', [(i, i ^ flip) for i in range(16)])  13.6 us
    ppermute x8, waiting for transfers between devices, tp_shift(): return lax.ppermute(value, 'tp', pairs)  11.6 us
    ppermute x9, waiting for transfers between devices, fsdp_flip(): return lax.ppermute(value, 'fsdp', [(i, i ^ flip) for i in range(16)])  4.19 us
  transfers between devices with their start and end apart: 33, of which 14 were waited for; matrix products, arithmetic and copies ran while one was open for 0% of the time, Pallas kernels for 11%

profile of v4, /device:TPU:1, one launch (start us, length us, event | category | flops | bytes accessed | tf_op | source)
XLA Modules:
  0.0 112.7 jit_solution(16786268232504322047)
XLA Ops:
  2.1 2.1 %collective-permute-start = (bf16[512,512]{1,0:T(8,128)(2,1)S(1)}, bf16[512,512]{1,0:T(8,128)(2,1)S(1)}, u32[]{:S(2)}, u32[]{:S(2)}) collective-permute-start(bf16[512,512]{1,0:T(8,128)(2,1)S(1)} %copy-done.3), channel_id=1, source_target_pairs={{0,2},{1,3},{2,0},{3,1},{4,6},{5,7},{6,4},{7,5},{8,10},{9,11},{10,... | collective-permute-start | bytes 1572872 | tf_op jit(solution)/shard_map/ppermute | solution.py:26
  5.5 2.6 %collective-permute-start.2 = (bf16[64,2048]{1,0:T(8,128)(2,1)S(1)}, bf16[64,2048]{1,0:T(8,128)(2,1)S(1)}, u32[]{:S(2)}, u32[]{:S(2)}) collective-permute-start(bf16[64,2048]{1,0:T(8,128)(2,1)S(1)} %get-tuple-element.43), channel_id=1, source_target_pairs={{0,8},{1,9},{2,10},{3,11},{4,12},{5,13},{6,14},{7,15},{8,0},{9,1},... | collective-permute-start | bytes 786440 | tf_op jit(solution)/shard_map/ppermute | solution.py:30
  12.3 6.9 %collective-permute-done.2.a2 = bf16[64,2048]{1,0:T(8,128)(2,1)S(1)} collective-permute-done((bf16[64,2048]{1,0:T(8,128)(2,1)S(1)}, bf16[64,2048]{1,0:T(8,128)(2,1)S(1)}, u32[]{:S(2)}, u32[]{:S(2)}) %collective-permute-start.2) | collective-permute-done | bytes 262176 | tf_op jit(solution)/shard_map/ppermute | solution.py:30
  25.3 2.0 %collective-permute-start.8 = (bf16[64,512]{1,0:T(8,128)(2,1)S(1)}, bf16[64,512]{1,0:T(8,128)(2,1)S(1)}, u32[]{:S(2)}, u32[]{:S(2)}) collective-permute-start(bf16[64,512]{1,0:T(8,128)(2,1)S(1)} %get-tuple-element.57), channel_id=1, source_target_pairs={{0,8},{1,9},{2,10},{3,11},{4,12},{5,13},{6,14},{7,15},{8,0},{9,1},... | collective-permute-start | bytes 196616 | tf_op jit(solution)/shard_map/ppermute | solution.py:30
  31.1 2.5 %collective-permute-start.9 = (bf16[64,512]{1,0:T(8,128)(2,1)S(1)}, bf16[64,512]{1,0:T(8,128)(2,1)S(1)}, u32[]{:S(2)}, u32[]{:S(2)}) collective-permute-start(bf16[64,512]{1,0:T(8,128)(2,1)S(1)} %total.1.mine), channel_id=1, source_target_pairs={{0,16},{16,0},{32,48},{48,32},{64,80},{80,64},{96,112},{112,96},{1... | collective-permute-start | bytes 196616 | tf_op jit(solution)/shard_map/ppermute | solution.py:35
  33.6 2.2 %collective-permute-done.9.partner = bf16[64,512]{1,0:T(8,128)(2,1)S(1)} collective-permute-done((bf16[64,512]{1,0:T(8,128)(2,1)S(1)}, bf16[64,512]{1,0:T(8,128)(2,1)S(1)}, u32[]{:S(2)}, u32[]{:S(2)}) %collective-permute-start.9) | collective-permute-done | bytes 65568 | tf_op jit(solution)/shard_map/ppermute | solution.py:35
  36.5 5.7 %collective-permute-start.12 = (bf16[512,128]{1,0:T(8,128)(2,1)S(1)}, bf16[512,128]{1,0:T(8,128)(2,1)S(1)}, u32[]{:S(2)}, u32[]{:S(2)}) collective-permute-start(bf16[512,128]{1,0:T(8,128)(2,1)S(1)} %join.1.refs_0_), channel_id=1, source_target_pairs={{0,224},{16,240},{32,0},{48,16},{64,32},{80,48},{96,64},{112,80},{... | collective-permute-start | bytes 393224 | tf_op jit(solution)/shard_map/ppermute | solution.py:35
  42.1 1.9 %collective-permute-done.12.refs_2_ = bf16[512,128]{1,0:T(8,128)(2,1)S(1)} collective-permute-done((bf16[512,128]{1,0:T(8,128)(2,1)S(1)}, bf16[512,128]{1,0:T(8,128)(2,1)S(1)}, u32[]{:S(2)}, u32[]{:S(2)}) %collective-permute-start.12) | collective-permute-done | bytes 131104 | tf_op jit(solution)/shard_map/ppermute | solution.py:35
  44.1 3.1 %collective-permute-start.13 = (bf16[512,128]{1,0:T(8,128)(2,1)S(1)}, bf16[512,128]{1,0:T(8,128)(2,1)S(1)}, u32[]{:S(2)}, u32[]{:S(2)}) collective-permute-start(bf16[512,128]{1,0:T(8,128)(2,1)S(1)} %collective-permute-done.12.refs_2_), channel_id=1, source_target_pairs={{0,224},{16,240},{32,0},{48,16},{64,32},{80,48},{96,64},{112,80},{... | collective-permute-start | bytes 393224 | tf_op jit(solution)/shard_map/ppermute | solution.py:35
  50.4 4.3 %collective-permute-done.11.refs_0_ = bf16[512,128]{1,0:T(8,128)(2,1)S(1)} collective-permute-done((bf16[512,128]{1,0:T(8,128)(2,1)S(1)}, bf16[512,128]{1,0:T(8,128)(2,1)S(1)}, u32[]{:S(2)}, u32[]{:S(2)}) %collective-permute-start.11) | collective-permute-done | bytes 131104 | tf_op jit(solution)/shard_map/ppermute | solution.py:35
  54.8 2.7 %collective-permute-start.15 = (bf16[512,128]{1,0:T(8,128)(2,1)S(1)}, bf16[512,128]{1,0:T(8,128)(2,1)S(1)}, u32[]{:S(2)}, u32[]{:S(2)}) collective-permute-start(bf16[512,128]{1,0:T(8,128)(2,1)S(1)} %collective-permute-done.13.refs_1_), channel_id=1, source_target_pairs={{0,224},{16,240},{32,0},{48,16},{64,32},{80,48},{96,64},{112,80},{... | collective-permute-start | bytes 393224 | tf_op jit(solution)/shard_map/ppermute | solution.py:35
  58.7 3.1 %collective-permute-done.14.refs_0_ = bf16[512,128]{1,0:T(8,128)(2,1)S(1)} collective-permute-done((bf16[512,128]{1,0:T(8,128)(2,1)S(1)}, bf16[512,128]{1,0:T(8,128)(2,1)S(1)}, u32[]{:S(2)}, u32[]{:S(2)}) %collective-permute-start.14) | collective-permute-done | bytes 131104 | tf_op jit(solution)/shard_map/ppermute | solution.py:35
  61.8 3.4 %last_terms.1 = (bf16[8,48,1792]{2,1,0:T(8,128)(2,1)S(1)}, f32[8,48,1792]{2,1,0:T(8,128)S(1)}) custom-call(s32[48]{0:T(128)S(1)} %table.1.where._, bf16[512,128]{1,0:T(8,128)(2,1)S(1)} %collective-permute-done.14.refs_0_, bf16[512,128]{1,0:T(8,128)(2,1)S(1)} %collective-permute-done.15.refs_1_, bf16[512,128]{1,0:T(8,128)(2,1)S(1)} %collective-permute-done.16.refs_2_, ...), custom_call_target="tpu_custom_call" | custom-call | flops 704643072 | bytes 7733440 | tf_op jit(solution)/shard_map/last_terms/pallas_call | solution.py:52
  65.2 3.2 %collective-permute-start.17 = (bf16[8,48,1792]{2,1,0:T(8,128)(2,1)S(1)}, bf16[8,48,1792]{2,1,0:T(8,128)(2,1)S(1)}, u32[]{:S(2)}, u32[]{:S(2)}) collective-permute-start(bf16[8,48,1792]{2,1,0:T(8,128)(2,1)S(1)} %get-tuple-element.62), channel_id=1, source_target_pairs={{0,1},{1,0},{2,3},{3,2},{4,5},{5,4},{6,7},{7,6},{8,9},{9,8},{10,11... | collective-permute-start | bytes 4128776 | tf_op jit(solution)/shard_map/ppermute | solution.py:26
  68.4 2.8 %collective-permute-done.17.given = bf16[8,48,1792]{2,1,0:T(8,128)(2,1)S(1)} collective-permute-done((bf16[8,48,1792]{2,1,0:T(8,128)(2,1)S(1)}, bf16[8,48,1792]{2,1,0:T(8,128)(2,1)S(1)}, u32[]{:S(2)}, u32[]{:S(2)}) %collective-permute-start.17) | collective-permute-done | bytes 1376288 | tf_op jit(solution)/shard_map/ppermute | solution.py:26
  72.4 2.4 %collective-permute-start.23 = (bf16[48,1792]{1,0:T(8,128)(2,1)S(1)}, bf16[48,1792]{1,0:T(8,128)(2,1)S(1)}, u32[]{:S(2)}, u32[]{:S(2)}) collective-permute-start(bf16[48,1792]{1,0:T(8,128)(2,1)S(1)} %get-tuple-element.70), channel_id=1, source_target_pairs={{0,12},{1,13},{2,14},{3,15},{4,0},{5,1},{6,2},{7,3},{8,4},{9,5},{1... | collective-permute-start | bytes 516104 | tf_op jit(solution)/shard_map/ppermute | solution.py:30
  75.6 2.7 %collective-permute-start.19 = (bf16[48,1792]{1,0:T(8,128)(2,1)S(1)}, bf16[48,1792]{1,0:T(8,128)(2,1)S(1)}, u32[]{:S(2)}, u32[]{:S(2)}) collective-permute-start(bf16[48,1792]{1,0:T(8,128)(2,1)S(1)} %get-tuple-element.65), channel_id=1, source_target_pairs={{0,12},{1,13},{2,14},{3,15},{4,0},{5,1},{6,2},{7,3},{8,4},{9,5},{1... | collective-permute-start | bytes 516104 | tf_op jit(solution)/shard_map/ppermute | solution.py:30
  82.5 4.4 %collective-permute-done.21.t1 = bf16[48,1792]{1,0:T(8,128)(2,1)S(1)} collective-permute-done((bf16[48,1792]{1,0:T(8,128)(2,1)S(1)}, bf16[48,1792]{1,0:T(8,128)(2,1)S(1)}, u32[]{:S(2)}, u32[]{:S(2)}) %collective-permute-start.21) | collective-permute-done | bytes 172064 | tf_op jit(solution)/shard_map/ppermute | solution.py:30
  91.0 2.7 %collective-permute-start.27 = (bf16[48,1792]{1,0:T(8,128)(2,1)S(1)}, bf16[48,1792]{1,0:T(8,128)(2,1)S(1)}, u32[]{:S(2)}, u32[]{:S(2)}) collective-permute-start(bf16[48,1792]{1,0:T(8,128)(2,1)S(1)} %get-tuple-element.73), channel_id=1, source_target_pairs={{0,12},{1,13},{2,14},{3,15},{4,0},{5,1},{6,2},{7,3},{8,4},{9,5},{1... | collective-permute-start | bytes 516104 | tf_op jit(solution)/shard_map/ppermute | solution.py:30
  93.8 2.8 %collective-permute-start.30 = (bf16[48,1792]{1,0:T(8,128)(2,1)S(1)}, bf16[48,1792]{1,0:T(8,128)(2,1)S(1)}, u32[]{:S(2)}, u32[]{:S(2)}) collective-permute-start(bf16[48,1792]{1,0:T(8,128)(2,1)S(1)} %collective-permute-done.25), channel_id=1, source_target_pairs={{0,12},{1,13},{2,14},{3,15},{4,0},{5,1},{6,2},{7,3},{8,4},{9,5},{1... | collective-permute-start | bytes 516104 | tf_op jit(solution)/shard_map/ppermute | solution.py:30
  96.8 4.5 %collective-permute-done.26 = bf16[48,1792]{1,0:T(8,128)(2,1)S(1)} collective-permute-done((bf16[48,1792]{1,0:T(8,128)(2,1)S(1)}, bf16[48,1792]{1,0:T(8,128)(2,1)S(1)}, u32[]{:S(2)}, u32[]{:S(2)}) %collective-permute-start.26) | collective-permute-done | bytes 172064 | tf_op jit(solution)/shard_map/ppermute | solution.py:30
  101.4 3.6 %collective-permute-done.29 = bf16[48,1792]{1,0:T(8,128)(2,1)S(1)} collective-permute-done((bf16[48,1792]{1,0:T(8,128)(2,1)S(1)}, bf16[48,1792]{1,0:T(8,128)(2,1)S(1)}, u32[]{:S(2)}, u32[]{:S(2)}) %collective-permute-start.29) | collective-permute-done | bytes 172064 | tf_op jit(solution)/shard_map/ppermute | solution.py:30
  105.1 2.1 %collective-permute-start.32 = (bf16[384,1792]{1,0:T(8,128)(2,1)S(1)}, bf16[384,1792]{1,0:T(8,128)(2,1)S(1)}, u32[]{:S(2)}, u32[]{:S(2)}) collective-permute-start(bf16[384,1792]{1,0:T(8,128)(2,1)S(1)} %constant_dynamic-update-slice_fusion.updates), channel_id=1, source_target_pairs={{0,1},{1,0},{2,3},{3,2},{4,5},{5,4},{6,7},{7,6},{8,9},{9,8},{10,11... | collective-permute-start | bytes 4128776 | tf_op jit(solution)/shard_map/ppermute | solution.py:26
  110.0 2.5 %delta.1 = bf16[512,1792]{1,0:T(8,128)(2,1)} custom-call(s32[48]{0:T(128)S(1)} %table.1.where._, bf16[512,384]{1,0:T(8,128)(2,1)S(1)} %get-tuple-element.53.chosen, bf16[384,1792]{1,0:T(8,128)(2,1)S(1)} %collective-permute-done.32.updates, f32[512,1792]{1,0:T(8,128)S(1)} %half_delta.1.before), custom_call_target="tpu_custom_call" | custom-call | flops 704643072 | bytes 5439680 | tf_op jit(solution)/shard_map/delta/pallas_call | solution.py:52
  (81 shorter events, 35.3 us)
Async XLA Ops:
  2.1 17.1 %collective-permute-start = (bf16[512,512]{1,0:T(8,128)(2,1)S(1)}, bf16[512,512]{1,0:T(8,128)(2,1)S(1)}, u32[]{:S(2)}, u32[]{:S(2)}) collective-permute-start(bf16[512,512]{1,0:T(8,128)(2,1)S(1)} %copy-done.3), channel_id=1, source_target_pairs={{0,2},{1,3},{2,0},{3,1},{4,6},{5,7},{6,4},{7,5},{8,10},{9,11},{10,... | collective-permute-start | bytes 1572872 | tf_op jit(solution)/shard_map/ppermute | solution.py:26
  4.3 8.0 %collective-permute-start.1 = (bf16[64,2048]{1,0:T(8,128)(2,1)S(1)}, bf16[64,2048]{1,0:T(8,128)(2,1)S(1)}, u32[]{:S(2)}, u32[]{:S(2)}) collective-permute-start(bf16[64,2048]{1,0:T(8,128)(2,1)S(1)} %get-tuple-element.42), channel_id=1, source_target_pairs={{0,4},{1,5},{2,6},{3,7},{4,8},{5,9},{6,10},{7,11},{8,12},{9,13},{1... | collective-permute-start | bytes 786440 | tf_op jit(solution)/shard_map/ppermute | solution.py:30
  5.5 13.6 %collective-permute-start.2 = (bf16[64,2048]{1,0:T(8,128)(2,1)S(1)}, bf16[64,2048]{1,0:T(8,128)(2,1)S(1)}, u32[]{:S(2)}, u32[]{:S(2)}) collective-permute-start(bf16[64,2048]{1,0:T(8,128)(2,1)S(1)} %get-tuple-element.43), channel_id=1, source_target_pairs={{0,8},{1,9},{2,10},{3,11},{4,12},{5,13},{6,14},{7,15},{8,0},{9,1},... | collective-permute-start | bytes 786440 | tf_op jit(solution)/shard_map/ppermute | solution.py:30
  8.2 11.0 %collective-permute-start.3 = (bf16[64,2048]{1,0:T(8,128)(2,1)S(1)}, bf16[64,2048]{1,0:T(8,128)(2,1)S(1)}, u32[]{:S(2)}, u32[]{:S(2)}) collective-permute-start(bf16[64,2048]{1,0:T(8,128)(2,1)S(1)} %get-tuple-element.44), channel_id=1, source_target_pairs={{0,12},{1,13},{2,14},{3,15},{4,0},{5,1},{6,2},{7,3},{8,4},{9,5},{1... | collective-permute-start | bytes 786440 | tf_op jit(solution)/shard_map/ppermute | solution.py:30
  9.2 11.8 %collective-permute-start.5 = (bf16[512,512]{1,0:T(8,128)(2,1)S(1)}, bf16[512,512]{1,0:T(8,128)(2,1)S(1)}, u32[]{:S(2)}, u32[]{:S(2)}) collective-permute-start(bf16[512,512]{1,0:T(8,128)(2,1)S(1)} %copy-done.3), channel_id=1, source_target_pairs={{0,1},{1,0},{2,3},{3,2},{4,5},{5,4},{6,7},{7,6},{8,9},{9,8},{10,11... | collective-permute-start | bytes 1572872 | tf_op jit(solution)/shard_map/ppermute | solution.py:26
  36.5 7.6 %collective-permute-start.12 = (bf16[512,128]{1,0:T(8,128)(2,1)S(1)}, bf16[512,128]{1,0:T(8,128)(2,1)S(1)}, u32[]{:S(2)}, u32[]{:S(2)}) collective-permute-start(bf16[512,128]{1,0:T(8,128)(2,1)S(1)} %join.1.refs_0_), channel_id=1, source_target_pairs={{0,224},{16,240},{32,0},{48,16},{64,32},{80,48},{96,64},{112,80},{... | collective-permute-start | bytes 393224 | tf_op jit(solution)/shard_map/ppermute | solution.py:35
  44.1 6.3 %collective-permute-start.13 = (bf16[512,128]{1,0:T(8,128)(2,1)S(1)}, bf16[512,128]{1,0:T(8,128)(2,1)S(1)}, u32[]{:S(2)}, u32[]{:S(2)}) collective-permute-start(bf16[512,128]{1,0:T(8,128)(2,1)S(1)} %collective-permute-done.12.refs_2_), channel_id=1, source_target_pairs={{0,224},{16,240},{32,0},{48,16},{64,32},{80,48},{96,64},{112,80},{... | collective-permute-start | bytes 393224 | tf_op jit(solution)/shard_map/ppermute | solution.py:35
  47.1 7.6 %collective-permute-start.11 = (bf16[512,128]{1,0:T(8,128)(2,1)S(1)}, bf16[512,128]{1,0:T(8,128)(2,1)S(1)}, u32[]{:S(2)}, u32[]{:S(2)}) collective-permute-start(bf16[512,128]{1,0:T(8,128)(2,1)S(1)} %collective-permute-done.10.refs_1_), channel_id=1, source_target_pairs={{0,32},{16,48},{32,64},{48,80},{64,96},{80,112},{96,128},{112,144}... | collective-permute-start | bytes 393224 | tf_op jit(solution)/shard_map/ppermute | solution.py:35
  47.1 11.5 %collective-permute-start.16 = (bf16[512,128]{1,0:T(8,128)(2,1)S(1)}, bf16[512,128]{1,0:T(8,128)(2,1)S(1)}, u32[]{:S(2)}, u32[]{:S(2)}) collective-permute-start(bf16[512,128]{1,0:T(8,128)(2,1)S(1)} %join.1.refs_0_), channel_id=1, source_target_pairs={{0,128},{16,144},{32,160},{48,176},{64,192},{80,208},{96,224},{112... | collective-permute-start | bytes 393224 | tf_op jit(solution)/shard_map/ppermute | solution.py:35
  54.7 7.0 %collective-permute-start.14 = (bf16[512,128]{1,0:T(8,128)(2,1)S(1)}, bf16[512,128]{1,0:T(8,128)(2,1)S(1)}, u32[]{:S(2)}, u32[]{:S(2)}) collective-permute-start(bf16[512,128]{1,0:T(8,128)(2,1)S(1)} %collective-permute-done.11.refs_0_), channel_id=1, source_target_pairs={{0,32},{16,48},{32,64},{48,80},{64,96},{80,112},{96,128},{112,144}... | collective-permute-start | bytes 393224 | tf_op jit(solution)/shard_map/ppermute | solution.py:35
  54.8 7.0 %collective-permute-start.15 = (bf16[512,128]{1,0:T(8,128)(2,1)S(1)}, bf16[512,128]{1,0:T(8,128)(2,1)S(1)}, u32[]{:S(2)}, u32[]{:S(2)}) collective-permute-start(bf16[512,128]{1,0:T(8,128)(2,1)S(1)} %collective-permute-done.13.refs_1_), channel_id=1, source_target_pairs={{0,224},{16,240},{32,0},{48,16},{64,32},{80,48},{96,64},{112,80},{... | collective-permute-start | bytes 393224 | tf_op jit(solution)/shard_map/ppermute | solution.py:35
  71.8 6.5 %collective-permute-start.20 = (bf16[48,1792]{1,0:T(8,128)(2,1)S(1)}, bf16[48,1792]{1,0:T(8,128)(2,1)S(1)}, u32[]{:S(2)}, u32[]{:S(2)}) collective-permute-start(bf16[48,1792]{1,0:T(8,128)(2,1)S(1)} %get-tuple-element.67), channel_id=1, source_target_pairs={{0,2},{1,3},{2,0},{3,1},{4,6},{5,7},{6,4},{7,5},{8,10},{9,11},{10,... | collective-permute-start | bytes 516104 | tf_op jit(solution)/shard_map/ppermute | solution.py:26
  72.1 7.8 %collective-permute-start.22 = (bf16[48,1792]{1,0:T(8,128)(2,1)S(1)}, bf16[48,1792]{1,0:T(8,128)(2,1)S(1)}, u32[]{:S(2)}, u32[]{:S(2)}) collective-permute-start(bf16[48,1792]{1,0:T(8,128)(2,1)S(1)} %get-tuple-element.69), channel_id=1, source_target_pairs={{0,4},{1,5},{2,6},{3,7},{4,8},{5,9},{6,10},{7,11},{8,12},{9,13},{1... | collective-permute-start | bytes 516104 | tf_op jit(solution)/shard_map/ppermute | solution.py:30
  72.4 7.4 %collective-permute-start.23 = (bf16[48,1792]{1,0:T(8,128)(2,1)S(1)}, bf16[48,1792]{1,0:T(8,128)(2,1)S(1)}, u32[]{:S(2)}, u32[]{:S(2)}) collective-permute-start(bf16[48,1792]{1,0:T(8,128)(2,1)S(1)} %get-tuple-element.70), channel_id=1, source_target_pairs={{0,12},{1,13},{2,14},{3,15},{4,0},{5,1},{6,2},{7,3},{8,4},{9,5},{1... | collective-permute-start | bytes 516104 | tf_op jit(solution)/shard_map/ppermute | solution.py:30
  75.5 6.4 %collective-permute-start.18 = (bf16[48,1792]{1,0:T(8,128)(2,1)S(1)}, bf16[48,1792]{1,0:T(8,128)(2,1)S(1)}, u32[]{:S(2)}, u32[]{:S(2)}) collective-permute-start(bf16[48,1792]{1,0:T(8,128)(2,1)S(1)} %get-tuple-element.64), channel_id=1, source_target_pairs={{0,4},{1,5},{2,6},{3,7},{4,8},{5,9},{6,10},{7,11},{8,12},{9,13},{1... | collective-permute-start | bytes 516104 | tf_op jit(solution)/shard_map/ppermute | solution.py:30
  75.6 6.3 %collective-permute-start.19 = (bf16[48,1792]{1,0:T(8,128)(2,1)S(1)}, bf16[48,1792]{1,0:T(8,128)(2,1)S(1)}, u32[]{:S(2)}, u32[]{:S(2)}) collective-permute-start(bf16[48,1792]{1,0:T(8,128)(2,1)S(1)} %get-tuple-element.65), channel_id=1, source_target_pairs={{0,12},{1,13},{2,14},{3,15},{4,0},{5,1},{6,2},{7,3},{8,4},{9,5},{1... | collective-permute-start | bytes 516104 | tf_op jit(solution)/shard_map/ppermute | solution.py:30
  78.8 8.1 %collective-permute-start.21 = (bf16[48,1792]{1,0:T(8,128)(2,1)S(1)}, bf16[48,1792]{1,0:T(8,128)(2,1)S(1)}, u32[]{:S(2)}, u32[]{:S(2)}) collective-permute-start(bf16[48,1792]{1,0:T(8,128)(2,1)S(1)} %add_far.1), channel_id=1, source_target_pairs={{0,8},{1,9},{2,10},{3,11},{4,12},{5,13},{6,14},{7,15},{8,0},{9,1},... | collective-permute-start | bytes 516104 | tf_op jit(solution)/shard_map/ppermute | solution.py:30
  80.5 6.5 %collective-permute-start.24 = (bf16[48,1792]{1,0:T(8,128)(2,1)S(1)}, bf16[48,1792]{1,0:T(8,128)(2,1)S(1)}, u32[]{:S(2)}, u32[]{:S(2)}) collective-permute-start(bf16[48,1792]{1,0:T(8,128)(2,1)S(1)} %add_beside.1), channel_id=1, source_target_pairs={{0,2},{1,3},{2,0},{3,1},{4,6},{5,7},{6,4},{7,5},{8,10},{9,11},{10,... | collective-permute-start | bytes 516104 | tf_op jit(solution)/shard_map/ppermute | solution.py:26
  87.8 6.0 %collective-permute-start.25 = (bf16[48,1792]{1,0:T(8,128)(2,1)S(1)}, bf16[48,1792]{1,0:T(8,128)(2,1)S(1)}, u32[]{:S(2)}, u32[]{:S(2)}) collective-permute-start(bf16[48,1792]{1,0:T(8,128)(2,1)S(1)} %get-tuple-element.71.update), channel_id=1, source_target_pairs={{0,2},{1,3},{2,0},{3,1},{4,6},{5,7},{6,4},{7,5},{8,10},{9,11},{10,... | collective-permute-start | bytes 516104 | tf_op jit(solution)/shard_map/ppermute | solution.py:26
  91.0 10.4 %collective-permute-start.27 = (bf16[48,1792]{1,0:T(8,128)(2,1)S(1)}, bf16[48,1792]{1,0:T(8,128)(2,1)S(1)}, u32[]{:S(2)}, u32[]{:S(2)}) collective-permute-start(bf16[48,1792]{1,0:T(8,128)(2,1)S(1)} %get-tuple-element.73), channel_id=1, source_target_pairs={{0,12},{1,13},{2,14},{3,15},{4,0},{5,1},{6,2},{7,3},{8,4},{9,5},{1... | collective-permute-start | bytes 516104 | tf_op jit(solution)/shard_map/ppermute | solution.py:30
  93.7 7.7 %collective-permute-start.26 = (bf16[48,1792]{1,0:T(8,128)(2,1)S(1)}, bf16[48,1792]{1,0:T(8,128)(2,1)S(1)}, u32[]{:S(2)}, u32[]{:S(2)}) collective-permute-start(bf16[48,1792]{1,0:T(8,128)(2,1)S(1)} %get-tuple-element.73), channel_id=1, source_target_pairs={{0,4},{1,5},{2,6},{3,7},{4,8},{5,9},{6,10},{7,11},{8,12},{9,13},{1... | collective-permute-start | bytes 516104 | tf_op jit(solution)/shard_map/ppermute | solution.py:30
  93.8 11.3 %collective-permute-start.30 = (bf16[48,1792]{1,0:T(8,128)(2,1)S(1)}, bf16[48,1792]{1,0:T(8,128)(2,1)S(1)}, u32[]{:S(2)}, u32[]{:S(2)}) collective-permute-start(bf16[48,1792]{1,0:T(8,128)(2,1)S(1)} %collective-permute-done.25), channel_id=1, source_target_pairs={{0,12},{1,13},{2,14},{3,15},{4,0},{5,1},{6,2},{7,3},{8,4},{9,5},{1... | collective-permute-start | bytes 516104 | tf_op jit(solution)/shard_map/ppermute | solution.py:30
  96.5 8.6 %collective-permute-start.29 = (bf16[48,1792]{1,0:T(8,128)(2,1)S(1)}, bf16[48,1792]{1,0:T(8,128)(2,1)S(1)}, u32[]{:S(2)}, u32[]{:S(2)}) collective-permute-start(bf16[48,1792]{1,0:T(8,128)(2,1)S(1)} %collective-permute-done.25), channel_id=1, source_target_pairs={{0,4},{1,5},{2,6},{3,7},{4,8},{5,9},{6,10},{7,11},{8,12},{9,13},{1... | collective-permute-start | bytes 516104 | tf_op jit(solution)/shard_map/ppermute | solution.py:30
  96.6 8.6 %collective-permute-start.31 = (bf16[48,1792]{1,0:T(8,128)(2,1)S(1)}, bf16[48,1792]{1,0:T(8,128)(2,1)S(1)}, u32[]{:S(2)}, u32[]{:S(2)}) collective-permute-start(bf16[48,1792]{1,0:T(8,128)(2,1)S(1)} %collective-permute-done.28), channel_id=1, source_target_pairs={{0,2},{1,3},{2,0},{3,1},{4,6},{5,7},{6,4},{7,5},{8,10},{9,11},{10,... | collective-permute-start | bytes 516104 | tf_op jit(solution)/shard_map/ppermute | solution.py:26
  (15 other events, 116.7 us)

commit v5 on v4

--- a/solution.py
+++ b/solution.py
@@ -171,11 +171,15 @@
 
 
 def last_kernel(offsets, where, *refs):
-    give, keep, table = refs[-3:]
+    give, table = refs[-2:]
     table[512:560, :] = jnp.zeros((48, FF), F32)
-    sum_kernel(offsets, where, *refs[:-3], table.at[0:512, :])
+    sum_kernel(offsets, where, *refs[:-2], table.at[0:512, :])
     for i, (dy, dx) in enumerate(TO_CHIPS):
         give[i] = rows_from(table, where[START + owner_of(where, dy, dx, 1)]).astype(BF16)
+
+
+def keep_kernel(where, table, keep):
+    for i, (dy, dx) in enumerate(TO_CHIPS):
         keep[i] = rows_from(table, where[START + owner_of(where, dy, dx, 0)])
 
 
@@ -200,12 +204,15 @@
     update[...] = adam_rows(total, live, first[...], second[...])[2]
 
 
-def moments_kernel(where, update, gradient, first, second, again, new_first, new_second):
+def first_kernel(where, update, gradient, first, again, new_first):
     live = lax.broadcasted_iota(jnp.int32, (48, FF), 0) < where[LENGTH + where[F]]
     again[...] = update[...]
-    one, two, _ = adam_rows(gradient[...], live, first[...], second[...])
-    new_first[...] = one
-    new_second[...] = two
+    new_first[...] = adam_rows(gradient[...], live, first[...], jnp.zeros((48, FF), F32))[0]
+
+
+def second_kernel(where, gradient, second, new_second):
+    live = lax.broadcasted_iota(jnp.int32, (48, FF), 0) < where[LENGTH + where[F]]
+    new_second[...] = adam_rows(gradient[...], live, jnp.zeros((48, FF), F32), second[...])[1]
 
 
 def half_delta_kernel(_, chosen, updates, out):
@@ -326,16 +333,15 @@
         aliases={4: 0},
         cheap=True,
     )
-    give, keep = local_call(
+    give, rows = local_call(
         functools.partial(last_kernel, (5, 3, 4)),
         "last_terms",
-        [
-            jax.ShapeDtypeStruct((8, 48, FF), BF16),
-            jax.ShapeDtypeStruct((8, 48, FF), F32),
-        ],
+        [jax.ShapeDtypeStruct((8, 48, FF), BF16), jax.ShapeDtypeStruct((560, FF), F32)],
         (where, up3, down3, far, grads, gradient),
         3 * one,
-        scratch=[pltpu.VMEM((560, FF), F32)],
+    )
+    (keep,) = local_call(
+        keep_kernel, "keep", [jax.ShapeDtypeStruct((8, 48, FF), F32)], (where, rows), 8 * 48 * FF
     )
 
     narrow, wide = jax.ShapeDtypeStruct((48, FF), BF16), jax.ShapeDtypeStruct((48, FF), F32)
@@ -378,13 +384,16 @@
     )
 
     beside = fsdp_flip(update, 2)
-    update, new_first, new_second = local_call(
-        moments_kernel,
-        "moments",
-        [narrow, wide, wide],
-        (where, update, gradient, first_moment, second_moment),
-        30 * size,
-        limit=8,
+    update, new_first = local_call(
+        first_kernel,
+        "first_moments",
+        [narrow, wide],
+        (where, update, gradient, first_moment),
+        15 * size,
+        limit=8,
+    )
+    (new_second,) = local_call(
+        second_kernel, "second_moments", [wide], (where, gradient, second_moment), 15 * size, limit=8
     )
     up, down, far = y_shift(update, 1), y_shift(update, -1), y_shift(update, 2)
     up_x, down_x, far_x = y_shift(beside, 1), y_shift(beside, -1), fsdp_flip(far, 2)

time: 113 us -> 112 us (level)
  waiting for transfers between devices: 38.2 us -> 35.8 us
  Pallas kernels: 21.8 us -> 23.3 us
    ppermute x9, waiting for transfers between devices: 4.19 us -> 1.86 us  [fsdp_flip(): return lax.ppermute(value, 'fsdp', [(i, i ^ flip) for i in range(16)])]
    pallas_call x17 -> x19, Pallas kernels: 20.6 us -> 22.2 us  [local_call(): pl.pallas_call(kernel, in_specs=[SCALARS] + in_vmem(len(operands) - 1 - a...]
  transfers between devices with their start and end apart: 33 -> 33, of which waited for: 14 -> 13; matrix products, arithmetic and copies ran while one was open for 0% -> 0% of each run, Pallas kernels for 11% -> 13%
where the time goes in v5:
time: 112 us
  starting transfers between devices  50.1 us (45%)
  waiting for transfers between devices  35.8 us (32%)
  Pallas kernels  23.3 us (21%)
  local copies, waits for them, and re-layouts  1.48 us (1%)
  between operations  1.23 us (1%)
    ppermute x16, waiting for transfers between devices, y_shift(): lax.ppermute(value, 'fsdp', [(i, (i + 4 * dy) % 16) for i in range(16)])  22.4 us
    pallas_call x19, Pallas kernels, local_call(): pl.pallas_call(kernel, in_specs=[SCALARS] + in_vmem(len(operands) - 1 - a...  22.2 us
    ppermute x16, starting transfers between devices, y_shift(): lax.ppermute(value, 'fsdp', [(i, (i + 4 * dy) % 16) for i in range(16)])  21 us
    ppermute x8, starting transfers between devices, tp_shift(): return lax.ppermute(value, 'tp', pairs)  15.5 us
    ppermute x9, starting transfers between devices, fsdp_flip(): return lax.ppermute(value, 'fsdp', [(i, i ^ flip) for i in range(16)])  13.6 us
    ppermute x8, waiting for transfers between devices, tp_shift(): return lax.ppermute(value, 'tp', pairs)  11.6 us
  transfers between devices with their start and end apart: 33, of which 13 were waited for; matrix products, arithmetic and copies ran while one was open for 0% of the time, Pallas kernels for 13%

profile of v5, /device:TPU:1, one launch (start us, length us, event | category | flops | bytes accessed | tf_op | source)
XLA Modules:
  0.0 112.0 jit_solution(4186828688338561094)
XLA Ops:
  2.1 2.1 %collective-permute-start = (bf16[512,512]{1,0:T(8,128)(2,1)S(1)}, bf16[512,512]{1,0:T(8,128)(2,1)S(1)}, u32[]{:S(2)}, u32[]{:S(2)}) collective-permute-start(bf16[512,512]{1,0:T(8,128)(2,1)S(1)} %copy-done.3), channel_id=1, source_target_pairs={{0,2},{1,3},{2,0},{3,1},{4,6},{5,7},{6,4},{7,5},{8,10},{9,11},{10,... | collective-permute-start | bytes 1572872 | tf_op jit(solution)/shard_map/ppermute | solution.py:26
  5.5 2.6 %collective-permute-start.2 = (bf16[64,2048]{1,0:T(8,128)(2,1)S(1)}, bf16[64,2048]{1,0:T(8,128)(2,1)S(1)}, u32[]{:S(2)}, u32[]{:S(2)}) collective-permute-start(bf16[64,2048]{1,0:T(8,128)(2,1)S(1)} %get-tuple-element.42), channel_id=1, source_target_pairs={{0,8},{1,9},{2,10},{3,11},{4,12},{5,13},{6,14},{7,15},{8,0},{9,1},... | collective-permute-start | bytes 786440 | tf_op jit(solution)/shard_map/ppermute | solution.py:30
  12.3 6.9 %collective-permute-done.2.a2 = bf16[64,2048]{1,0:T(8,128)(2,1)S(1)} collective-permute-done((bf16[64,2048]{1,0:T(8,128)(2,1)S(1)}, bf16[64,2048]{1,0:T(8,128)(2,1)S(1)}, u32[]{:S(2)}, u32[]{:S(2)}) %collective-permute-start.2) | collective-permute-done | bytes 262176 | tf_op jit(solution)/shard_map/ppermute | solution.py:30
  19.2 1.9 %collective-permute-start.4 = (bf16[512,512]{1,0:T(8,128)(2,1)S(1)}, bf16[512,512]{1,0:T(8,128)(2,1)S(1)}, u32[]{:S(2)}, u32[]{:S(2)}) collective-permute-start(bf16[512,512]{1,0:T(8,128)(2,1)S(1)} %collective-permute-done.p2), channel_id=1, source_target_pairs={{0,1},{1,0},{2,3},{3,2},{4,5},{5,4},{6,7},{7,6},{8,9},{9,8},{10,11... | collective-permute-start | bytes 1572872 | tf_op jit(solution)/shard_map/ppermute | solution.py:26
  25.3 2.0 %collective-permute-start.8 = (bf16[64,512]{1,0:T(8,128)(2,1)S(1)}, bf16[64,512]{1,0:T(8,128)(2,1)S(1)}, u32[]{:S(2)}, u32[]{:S(2)}) collective-permute-start(bf16[64,512]{1,0:T(8,128)(2,1)S(1)} %get-tuple-element.56), channel_id=1, source_target_pairs={{0,8},{1,9},{2,10},{3,11},{4,12},{5,13},{6,14},{7,15},{8,0},{9,1},... | collective-permute-start | bytes 196616 | tf_op jit(solution)/shard_map/ppermute | solution.py:30
  31.1 2.5 %collective-permute-start.9 = (bf16[64,512]{1,0:T(8,128)(2,1)S(1)}, bf16[64,512]{1,0:T(8,128)(2,1)S(1)}, u32[]{:S(2)}, u32[]{:S(2)}) collective-permute-start(bf16[64,512]{1,0:T(8,128)(2,1)S(1)} %total.1.mine), channel_id=1, source_target_pairs={{0,16},{16,0},{32,48},{48,32},{64,80},{80,64},{96,112},{112,96},{1... | collective-permute-start | bytes 196616 | tf_op jit(solution)/shard_map/ppermute | solution.py:35
  33.6 2.2 %collective-permute-done.9.partner = bf16[64,512]{1,0:T(8,128)(2,1)S(1)} collective-permute-done((bf16[64,512]{1,0:T(8,128)(2,1)S(1)}, bf16[64,512]{1,0:T(8,128)(2,1)S(1)}, u32[]{:S(2)}, u32[]{:S(2)}) %collective-permute-start.9) | collective-permute-done | bytes 65568 | tf_op jit(solution)/shard_map/ppermute | solution.py:35
  36.5 5.7 %collective-permute-start.12 = (bf16[512,128]{1,0:T(8,128)(2,1)S(1)}, bf16[512,128]{1,0:T(8,128)(2,1)S(1)}, u32[]{:S(2)}, u32[]{:S(2)}) collective-permute-start(bf16[512,128]{1,0:T(8,128)(2,1)S(1)} %join.1.refs_0_), channel_id=1, source_target_pairs={{0,224},{16,240},{32,0},{48,16},{64,32},{80,48},{96,64},{112,80},{... | collective-permute-start | bytes 393224 | tf_op jit(solution)/shard_map/ppermute | solution.py:35
  42.1 1.9 %collective-permute-done.12.refs_2_ = bf16[512,128]{1,0:T(8,128)(2,1)S(1)} collective-permute-done((bf16[512,128]{1,0:T(8,128)(2,1)S(1)}, bf16[512,128]{1,0:T(8,128)(2,1)S(1)}, u32[]{:S(2)}, u32[]{:S(2)}) %collective-permute-start.12) | collective-permute-done | bytes 131104 | tf_op jit(solution)/shard_map/ppermute | solution.py:35
  44.1 3.1 %collective-permute-start.13 = (bf16[512,128]{1,0:T(8,128)(2,1)S(1)}, bf16[512,128]{1,0:T(8,128)(2,1)S(1)}, u32[]{:S(2)}, u32[]{:S(2)}) collective-permute-start(bf16[512,128]{1,0:T(8,128)(2,1)S(1)} %collective-permute-done.12.refs_2_), channel_id=1, source_target_pairs={{0,224},{16,240},{32,0},{48,16},{64,32},{80,48},{96,64},{112,80},{... | collective-permute-start | bytes 393224 | tf_op jit(solution)/shard_map/ppermute | solution.py:35
  50.4 4.3 %collective-permute-done.11.refs_0_ = bf16[512,128]{1,0:T(8,128)(2,1)S(1)} collective-permute-done((bf16[512,128]{1,0:T(8,128)(2,1)S(1)}, bf16[512,128]{1,0:T(8,128)(2,1)S(1)}, u32[]{:S(2)}, u32[]{:S(2)}) %collective-permute-start.11) | collective-permute-done | bytes 131104 | tf_op jit(solution)/shard_map/ppermute | solution.py:35
  54.8 2.7 %collective-permute-start.15 = (bf16[512,128]{1,0:T(8,128)(2,1)S(1)}, bf16[512,128]{1,0:T(8,128)(2,1)S(1)}, u32[]{:S(2)}, u32[]{:S(2)}) collective-permute-start(bf16[512,128]{1,0:T(8,128)(2,1)S(1)} %collective-permute-done.13.refs_1_), channel_id=1, source_target_pairs={{0,224},{16,240},{32,0},{48,16},{64,32},{80,48},{96,64},{112,80},{... | collective-permute-start | bytes 393224 | tf_op jit(solution)/shard_map/ppermute | solution.py:35
  58.7 3.1 %collective-permute-done.14.refs_0_ = bf16[512,128]{1,0:T(8,128)(2,1)S(1)} collective-permute-done((bf16[512,128]{1,0:T(8,128)(2,1)S(1)}, bf16[512,128]{1,0:T(8,128)(2,1)S(1)}, u32[]{:S(2)}, u32[]{:S(2)}) %collective-permute-start.14) | collective-permute-done | bytes 131104 | tf_op jit(solution)/shard_map/ppermute | solution.py:35
  61.8 2.6 %last_terms.1 = (bf16[8,48,1792]{2,1,0:T(8,128)(2,1)S(1)}, f32[560,1792]{1,0:T(8,128)S(1)}) custom-call(s32[48]{0:T(128)S(1)} %table.1.where._, bf16[512,128]{1,0:T(8,128)(2,1)S(1)} %collective-permute-done.14.refs_0_, bf16[512,128]{1,0:T(8,128)(2,1)S(1)} %collective-permute-done.15.refs_1_, bf16[512,128]{1,0:T(8,128)(2,1)S(1)} %collective-permute-done.16.refs_2_, ...), custom_call_target="tpu_custom_call" | custom-call | flops 704643072 | bytes 7733440 | tf_op jit(solution)/shard_map/last_terms/pallas_call | solution.py:52
  64.4 3.2 %collective-permute-start.17 = (bf16[8,48,1792]{2,1,0:T(8,128)(2,1)S(1)}, bf16[8,48,1792]{2,1,0:T(8,128)(2,1)S(1)}, u32[]{:S(2)}, u32[]{:S(2)}) collective-permute-start(bf16[8,48,1792]{2,1,0:T(8,128)(2,1)S(1)} %get-tuple-element.61), channel_id=1, source_target_pairs={{0,1},{1,0},{2,3},{3,2},{4,5},{5,4},{6,7},{7,6},{8,9},{9,8},{10,11... | collective-permute-start | bytes 4128776 | tf_op jit(solution)/shard_map/ppermute | solution.py:26
  71.6 2.4 %collective-permute-start.23 = (bf16[48,1792]{1,0:T(8,128)(2,1)S(1)}, bf16[48,1792]{1,0:T(8,128)(2,1)S(1)}, u32[]{:S(2)}, u32[]{:S(2)}) collective-permute-start(bf16[48,1792]{1,0:T(8,128)(2,1)S(1)} %get-tuple-element.69), channel_id=1, source_target_pairs={{0,12},{1,13},{2,14},{3,15},{4,0},{5,1},{6,2},{7,3},{8,4},{9,5},{1... | collective-permute-start | bytes 516104 | tf_op jit(solution)/shard_map/ppermute | solution.py:30
  74.7 2.7 %collective-permute-start.19 = (bf16[48,1792]{1,0:T(8,128)(2,1)S(1)}, bf16[48,1792]{1,0:T(8,128)(2,1)S(1)}, u32[]{:S(2)}, u32[]{:S(2)}) collective-permute-start(bf16[48,1792]{1,0:T(8,128)(2,1)S(1)} %get-tuple-element.64), channel_id=1, source_target_pairs={{0,12},{1,13},{2,14},{3,15},{4,0},{5,1},{6,2},{7,3},{8,4},{9,5},{1... | collective-permute-start | bytes 516104 | tf_op jit(solution)/shard_map/ppermute | solution.py:30
  81.7 4.4 %collective-permute-done.21.t1 = bf16[48,1792]{1,0:T(8,128)(2,1)S(1)} collective-permute-done((bf16[48,1792]{1,0:T(8,128)(2,1)S(1)}, bf16[48,1792]{1,0:T(8,128)(2,1)S(1)}, u32[]{:S(2)}, u32[]{:S(2)}) %collective-permute-start.21) | collective-permute-done | bytes 172064 | tf_op jit(solution)/shard_map/ppermute | solution.py:30
  90.0 2.7 %collective-permute-start.27 = (bf16[48,1792]{1,0:T(8,128)(2,1)S(1)}, bf16[48,1792]{1,0:T(8,128)(2,1)S(1)}, u32[]{:S(2)}, u32[]{:S(2)}) collective-permute-start(bf16[48,1792]{1,0:T(8,128)(2,1)S(1)} %get-tuple-element.72), channel_id=1, source_target_pairs={{0,12},{1,13},{2,14},{3,15},{4,0},{5,1},{6,2},{7,3},{8,4},{9,5},{1... | collective-permute-start | bytes 516104 | tf_op jit(solution)/shard_map/ppermute | solution.py:30
  92.8 2.8 %collective-permute-start.30 = (bf16[48,1792]{1,0:T(8,128)(2,1)S(1)}, bf16[48,1792]{1,0:T(8,128)(2,1)S(1)}, u32[]{:S(2)}, u32[]{:S(2)}) collective-permute-start(bf16[48,1792]{1,0:T(8,128)(2,1)S(1)} %collective-permute-done.25), channel_id=1, source_target_pairs={{0,12},{1,13},{2,14},{3,15},{4,0},{5,1},{6,2},{7,3},{8,4},{9,5},{1... | collective-permute-start | bytes 516104 | tf_op jit(solution)/shard_map/ppermute | solution.py:30
  95.9 4.5 %collective-permute-done.26 = bf16[48,1792]{1,0:T(8,128)(2,1)S(1)} collective-permute-done((bf16[48,1792]{1,0:T(8,128)(2,1)S(1)}, bf16[48,1792]{1,0:T(8,128)(2,1)S(1)}, u32[]{:S(2)}, u32[]{:S(2)}) %collective-permute-start.26) | collective-permute-done | bytes 172064 | tf_op jit(solution)/shard_map/ppermute | solution.py:30
  100.5 3.6 %collective-permute-done.29 = bf16[48,1792]{1,0:T(8,128)(2,1)S(1)} collective-permute-done((bf16[48,1792]{1,0:T(8,128)(2,1)S(1)}, bf16[48,1792]{1,0:T(8,128)(2,1)S(1)}, u32[]{:S(2)}, u32[]{:S(2)}) %collective-permute-start.29) | collective-permute-done | bytes 172064 | tf_op jit(solution)/shard_map/ppermute | solution.py:30
  104.2 2.1 %collective-permute-start.32 = (bf16[384,1792]{1,0:T(8,128)(2,1)S(1)}, bf16[384,1792]{1,0:T(8,128)(2,1)S(1)}, u32[]{:S(2)}, u32[]{:S(2)}) collective-permute-start(bf16[384,1792]{1,0:T(8,128)(2,1)S(1)} %constant_dynamic-update-slice_fusion.updates), channel_id=1, source_target_pairs={{0,1},{1,0},{2,3},{3,2},{4,5},{5,4},{6,7},{7,6},{8,9},{9,8},{10,11... | collective-permute-start | bytes 4128776 | tf_op jit(solution)/shard_map/ppermute | solution.py:26
  109.3 2.5 %delta.1 = bf16[512,1792]{1,0:T(8,128)(2,1)} custom-call(s32[48]{0:T(128)S(1)} %table.1.where._, bf16[512,384]{1,0:T(8,128)(2,1)S(1)} %get-tuple-element.52.chosen, bf16[384,1792]{1,0:T(8,128)(2,1)S(1)} %collective-permute-done.32.updates, f32[512,1792]{1,0:T(8,128)S(1)} %half_delta.1.before), custom_call_target="tpu_custom_call" | custom-call | flops 704643072 | bytes 5439680 | tf_op jit(solution)/shard_map/delta/pallas_call | solution.py:52
  (83 shorter events, 36.3 us)
Async XLA Ops:
  2.1 17.1 %collective-permute-start = (bf16[512,512]{1,0:T(8,128)(2,1)S(1)}, bf16[512,512]{1,0:T(8,128)(2,1)S(1)}, u32[]{:S(2)}, u32[]{:S(2)}) collective-permute-start(bf16[512,512]{1,0:T(8,128)(2,1)S(1)} %copy-done.3), channel_id=1, source_target_pairs={{0,2},{1,3},{2,0},{3,1},{4,6},{5,7},{6,4},{7,5},{8,10},{9,11},{10,... | collective-permute-start | bytes 1572872 | tf_op jit(solution)/shard_map/ppermute | solution.py:26
  4.3 8.0 %collective-permute-start.1 = (bf16[64,2048]{1,0:T(8,128)(2,1)S(1)}, bf16[64,2048]{1,0:T(8,128)(2,1)S(1)}, u32[]{:S(2)}, u32[]{:S(2)}) collective-permute-start(bf16[64,2048]{1,0:T(8,128)(2,1)S(1)} %get-tuple-element.41), channel_id=1, source_target_pairs={{0,4},{1,5},{2,6},{3,7},{4,8},{5,9},{6,10},{7,11},{8,12},{9,13},{1... | collective-permute-start | bytes 786440 | tf_op jit(solution)/shard_map/ppermute | solution.py:30
  5.5 13.6 %collective-permute-start.2 = (bf16[64,2048]{1,0:T(8,128)(2,1)S(1)}, bf16[64,2048]{1,0:T(8,128)(2,1)S(1)}, u32[]{:S(2)}, u32[]{:S(2)}) collective-permute-start(bf16[64,2048]{1,0:T(8,128)(2,1)S(1)} %get-tuple-element.42), channel_id=1, source_target_pairs={{0,8},{1,9},{2,10},{3,11},{4,12},{5,13},{6,14},{7,15},{8,0},{9,1},... | collective-permute-start | bytes 786440 | tf_op jit(solution)/shard_map/ppermute | solution.py:30
  8.2 11.0 %collective-permute-start.3 = (bf16[64,2048]{1,0:T(8,128)(2,1)S(1)}, bf16[64,2048]{1,0:T(8,128)(2,1)S(1)}, u32[]{:S(2)}, u32[]{:S(2)}) collective-permute-start(bf16[64,2048]{1,0:T(8,128)(2,1)S(1)} %get-tuple-element.43), channel_id=1, source_target_pairs={{0,12},{1,13},{2,14},{3,15},{4,0},{5,1},{6,2},{7,3},{8,4},{9,5},{1... | collective-permute-start | bytes 786440 | tf_op jit(solution)/shard_map/ppermute | solution.py:30
  9.2 11.8 %collective-permute-start.5 = (bf16[512,512]{1,0:T(8,128)(2,1)S(1)}, bf16[512,512]{1,0:T(8,128)(2,1)S(1)}, u32[]{:S(2)}, u32[]{:S(2)}) collective-permute-start(bf16[512,512]{1,0:T(8,128)(2,1)S(1)} %copy-done.3), channel_id=1, source_target_pairs={{0,1},{1,0},{2,3},{3,2},{4,5},{5,4},{6,7},{7,6},{8,9},{9,8},{10,11... | collective-permute-start | bytes 1572872 | tf_op jit(solution)/shard_map/ppermute | solution.py:26
  36.5 7.6 %collective-permute-start.12 = (bf16[512,128]{1,0:T(8,128)(2,1)S(1)}, bf16[512,128]{1,0:T(8,128)(2,1)S(1)}, u32[]{:S(2)}, u32[]{:S(2)}) collective-permute-start(bf16[512,128]{1,0:T(8,128)(2,1)S(1)} %join.1.refs_0_), channel_id=1, source_target_pairs={{0,224},{16,240},{32,0},{48,16},{64,32},{80,48},{96,64},{112,80},{... | collective-permute-start | bytes 393224 | tf_op jit(solution)/shard_map/ppermute | solution.py:35
  44.1 6.3 %collective-permute-start.13 = (bf16[512,128]{1,0:T(8,128)(2,1)S(1)}, bf16[512,128]{1,0:T(8,128)(2,1)S(1)}, u32[]{:S(2)}, u32[]{:S(2)}) collective-permute-start(bf16[512,128]{1,0:T(8,128)(2,1)S(1)} %collective-permute-done.12.refs_2_), channel_id=1, source_target_pairs={{0,224},{16,240},{32,0},{48,16},{64,32},{80,48},{96,64},{112,80},{... | collective-permute-start | bytes 393224 | tf_op jit(solution)/shard_map/ppermute | solution.py:35
  47.1 7.6 %collective-permute-start.11 = (bf16[512,128]{1,0:T(8,128)(2,1)S(1)}, bf16[512,128]{1,0:T(8,128)(2,1)S(1)}, u32[]{:S(2)}, u32[]{:S(2)}) collective-permute-start(bf16[512,128]{1,0:T(8,128)(2,1)S(1)} %collective-permute-done.10.refs_1_), channel_id=1, source_target_pairs={{0,32},{16,48},{32,64},{48,80},{64,96},{80,112},{96,128},{112,144}... | collective-permute-start | bytes 393224 | tf_op jit(solution)/shard_map/ppermute | solution.py:35
  47.1 11.5 %collective-permute-start.16 = (bf16[512,128]{1,0:T(8,128)(2,1)S(1)}, bf16[512,128]{1,0:T(8,128)(2,1)S(1)}, u32[]{:S(2)}, u32[]{:S(2)}) collective-permute-start(bf16[512,128]{1,0:T(8,128)(2,1)S(1)} %join.1.refs_0_), channel_id=1, source_target_pairs={{0,128},{16,144},{32,160},{48,176},{64,192},{80,208},{96,224},{112... | collective-permute-start | bytes 393224 | tf_op jit(solution)/shard_map/ppermute | solution.py:35
  54.7 7.0 %collective-permute-start.14 = (bf16[512,128]{1,0:T(8,128)(2,1)S(1)}, bf16[512,128]{1,0:T(8,128)(2,1)S(1)}, u32[]{:S(2)}, u32[]{:S(2)}) collective-permute-start(bf16[512,128]{1,0:T(8,128)(2,1)S(1)} %collective-permute-done.11.refs_0_), channel_id=1, source_target_pairs={{0,32},{16,48},{32,64},{48,80},{64,96},{80,112},{96,128},{112,144}... | collective-permute-start | bytes 393224 | tf_op jit(solution)/shard_map/ppermute | solution.py:35
  54.8 7.0 %collective-permute-start.15 = (bf16[512,128]{1,0:T(8,128)(2,1)S(1)}, bf16[512,128]{1,0:T(8,128)(2,1)S(1)}, u32[]{:S(2)}, u32[]{:S(2)}) collective-permute-start(bf16[512,128]{1,0:T(8,128)(2,1)S(1)} %collective-permute-done.13.refs_1_), channel_id=1, source_target_pairs={{0,224},{16,240},{32,0},{48,16},{64,32},{80,48},{96,64},{112,80},{... | collective-permute-start | bytes 393224 | tf_op jit(solution)/shard_map/ppermute | solution.py:35
  64.4 5.9 %collective-permute-start.17 = (bf16[8,48,1792]{2,1,0:T(8,128)(2,1)S(1)}, bf16[8,48,1792]{2,1,0:T(8,128)(2,1)S(1)}, u32[]{:S(2)}, u32[]{:S(2)}) collective-permute-start(bf16[8,48,1792]{2,1,0:T(8,128)(2,1)S(1)} %get-tuple-element.61), channel_id=1, source_target_pairs={{0,1},{1,0},{2,3},{3,2},{4,5},{5,4},{6,7},{7,6},{8,9},{9,8},{10,11... | collective-permute-start | bytes 4128776 | tf_op jit(solution)/shard_map/ppermute | solution.py:26
  70.9 6.5 %collective-permute-start.20 = (bf16[48,1792]{1,0:T(8,128)(2,1)S(1)}, bf16[48,1792]{1,0:T(8,128)(2,1)S(1)}, u32[]{:S(2)}, u32[]{:S(2)}) collective-permute-start(bf16[48,1792]{1,0:T(8,128)(2,1)S(1)} %get-tuple-element.66), channel_id=1, source_target_pairs={{0,2},{1,3},{2,0},{3,1},{4,6},{5,7},{6,4},{7,5},{8,10},{9,11},{10,... | collective-permute-start | bytes 516104 | tf_op jit(solution)/shard_map/ppermute | solution.py:26
  71.3 7.8 %collective-permute-start.22 = (bf16[48,1792]{1,0:T(8,128)(2,1)S(1)}, bf16[48,1792]{1,0:T(8,128)(2,1)S(1)}, u32[]{:S(2)}, u32[]{:S(2)}) collective-permute-start(bf16[48,1792]{1,0:T(8,128)(2,1)S(1)} %get-tuple-element.68), channel_id=1, source_target_pairs={{0,4},{1,5},{2,6},{3,7},{4,8},{5,9},{6,10},{7,11},{8,12},{9,13},{1... | collective-permute-start | bytes 516104 | tf_op jit(solution)/shard_map/ppermute | solution.py:30
  71.6 7.4 %collective-permute-start.23 = (bf16[48,1792]{1,0:T(8,128)(2,1)S(1)}, bf16[48,1792]{1,0:T(8,128)(2,1)S(1)}, u32[]{:S(2)}, u32[]{:S(2)}) collective-permute-start(bf16[48,1792]{1,0:T(8,128)(2,1)S(1)} %get-tuple-element.69), channel_id=1, source_target_pairs={{0,12},{1,13},{2,14},{3,15},{4,0},{5,1},{6,2},{7,3},{8,4},{9,5},{1... | collective-permute-start | bytes 516104 | tf_op jit(solution)/shard_map/ppermute | solution.py:30
  74.7 6.4 %collective-permute-start.18 = (bf16[48,1792]{1,0:T(8,128)(2,1)S(1)}, bf16[48,1792]{1,0:T(8,128)(2,1)S(1)}, u32[]{:S(2)}, u32[]{:S(2)}) collective-permute-start(bf16[48,1792]{1,0:T(8,128)(2,1)S(1)} %get-tuple-element.63), channel_id=1, source_target_pairs={{0,4},{1,5},{2,6},{3,7},{4,8},{5,9},{6,10},{7,11},{8,12},{9,13},{1... | collective-permute-start | bytes 516104 | tf_op jit(solution)/shard_map/ppermute | solution.py:30
  74.7 6.3 %collective-permute-start.19 = (bf16[48,1792]{1,0:T(8,128)(2,1)S(1)}, bf16[48,1792]{1,0:T(8,128)(2,1)S(1)}, u32[]{:S(2)}, u32[]{:S(2)}) collective-permute-start(bf16[48,1792]{1,0:T(8,128)(2,1)S(1)} %get-tuple-element.64), channel_id=1, source_target_pairs={{0,12},{1,13},{2,14},{3,15},{4,0},{5,1},{6,2},{7,3},{8,4},{9,5},{1... | collective-permute-start | bytes 516104 | tf_op jit(solution)/shard_map/ppermute | solution.py:30
  78.0 8.1 %collective-permute-start.21 = (bf16[48,1792]{1,0:T(8,128)(2,1)S(1)}, bf16[48,1792]{1,0:T(8,128)(2,1)S(1)}, u32[]{:S(2)}, u32[]{:S(2)}) collective-permute-start(bf16[48,1792]{1,0:T(8,128)(2,1)S(1)} %add_far.1), channel_id=1, source_target_pairs={{0,8},{1,9},{2,10},{3,11},{4,12},{5,13},{6,14},{7,15},{8,0},{9,1},... | collective-permute-start | bytes 516104 | tf_op jit(solution)/shard_map/ppermute | solution.py:30
  79.6 6.5 %collective-permute-start.24 = (bf16[48,1792]{1,0:T(8,128)(2,1)S(1)}, bf16[48,1792]{1,0:T(8,128)(2,1)S(1)}, u32[]{:S(2)}, u32[]{:S(2)}) collective-permute-start(bf16[48,1792]{1,0:T(8,128)(2,1)S(1)} %add_beside.1), channel_id=1, source_target_pairs={{0,2},{1,3},{2,0},{3,1},{4,6},{5,7},{6,4},{7,5},{8,10},{9,11},{10,... | collective-permute-start | bytes 516104 | tf_op jit(solution)/shard_map/ppermute | solution.py:26
  90.0 10.4 %collective-permute-start.27 = (bf16[48,1792]{1,0:T(8,128)(2,1)S(1)}, bf16[48,1792]{1,0:T(8,128)(2,1)S(1)}, u32[]{:S(2)}, u32[]{:S(2)}) collective-permute-start(bf16[48,1792]{1,0:T(8,128)(2,1)S(1)} %get-tuple-element.72), channel_id=1, source_target_pairs={{0,12},{1,13},{2,14},{3,15},{4,0},{5,1},{6,2},{7,3},{8,4},{9,5},{1... | collective-permute-start | bytes 516104 | tf_op jit(solution)/shard_map/ppermute | solution.py:30
  92.7 7.7 %collective-permute-start.26 = (bf16[48,1792]{1,0:T(8,128)(2,1)S(1)}, bf16[48,1792]{1,0:T(8,128)(2,1)S(1)}, u32[]{:S(2)}, u32[]{:S(2)}) collective-permute-start(bf16[48,1792]{1,0:T(8,128)(2,1)S(1)} %get-tuple-element.72), channel_id=1, source_target_pairs={{0,4},{1,5},{2,6},{3,7},{4,8},{5,9},{6,10},{7,11},{8,12},{9,13},{1... | collective-permute-start | bytes 516104 | tf_op jit(solution)/shard_map/ppermute | solution.py:30
  92.8 11.3 %collective-permute-start.30 = (bf16[48,1792]{1,0:T(8,128)(2,1)S(1)}, bf16[48,1792]{1,0:T(8,128)(2,1)S(1)}, u32[]{:S(2)}, u32[]{:S(2)}) collective-permute-start(bf16[48,1792]{1,0:T(8,128)(2,1)S(1)} %collective-permute-done.25), channel_id=1, source_target_pairs={{0,12},{1,13},{2,14},{3,15},{4,0},{5,1},{6,2},{7,3},{8,4},{9,5},{1... | collective-permute-start | bytes 516104 | tf_op jit(solution)/shard_map/ppermute | solution.py:30
  95.5 8.6 %collective-permute-start.29 = (bf16[48,1792]{1,0:T(8,128)(2,1)S(1)}, bf16[48,1792]{1,0:T(8,128)(2,1)S(1)}, u32[]{:S(2)}, u32[]{:S(2)}) collective-permute-start(bf16[48,1792]{1,0:T(8,128)(2,1)S(1)} %collective-permute-done.25), channel_id=1, source_target_pairs={{0,4},{1,5},{2,6},{3,7},{4,8},{5,9},{6,10},{7,11},{8,12},{9,13},{1... | collective-permute-start | bytes 516104 | tf_op jit(solution)/shard_map/ppermute | solution.py:30
  95.6 8.6 %collective-permute-start.31 = (bf16[48,1792]{1,0:T(8,128)(2,1)S(1)}, bf16[48,1792]{1,0:T(8,128)(2,1)S(1)}, u32[]{:S(2)}, u32[]{:S(2)}) collective-permute-start(bf16[48,1792]{1,0:T(8,128)(2,1)S(1)} %collective-permute-done.28), channel_id=1, source_target_pairs={{0,2},{1,3},{2,0},{3,1},{4,6},{5,7},{6,4},{7,5},{8,10},{9,11},{10,... | collective-permute-start | bytes 516104 | tf_op jit(solution)/shard_map/ppermute | solution.py:26
  (15 other events, 116.8 us)

commit v6 on v5

--- a/solution.py
+++ b/solution.py
@@ -251,10 +251,13 @@
     tokens = activations[0]
     grads = grad_output[0]
     y = lax.axis_index("fsdp").astype(jnp.int32) // 4
-    slices = [lax.dynamic_slice(tokens, (0, (y + s) % 4 * 2048), (64, 2048)) for s in range(4)]
-    *slices[1:], block, lengths = lax.optimization_barrier(
-        (*slices[1:], projection, piece_lengths)
-    )
+    def token_slice(source, s):
+        return lax.dynamic_slice(source, (0, (y + s) % 4 * 2048), (64, 2048))
+
+    *slices, rest, block, lengths = lax.optimization_barrier(
+        (*[token_slice(tokens, s) for s in (1, 2, 3)], tokens, projection, piece_lengths)
+    )
+    slices = [token_slice(rest, 0), *slices]
     where = scalar_table(lengths, piece_owners)
     for s in (1, 3, 2):
         slices[s] = y_shift(slices[s], s)

time: 112 us -> 113 us (level)
  starting transfers between devices: 50.1 us -> 53.1 us
  waiting for transfers between devices: 35.8 us -> 33.2 us
    ppermute x9, starting transfers between devices: 13.6 us -> 16.2 us  [fsdp_flip(): return lax.ppermute(value, 'fsdp', [(i, i ^ flip) for i in range(16)])]
    ppermute x8, waiting for transfers between devices: 11.6 us -> 10.3 us  [tp_shift(): return lax.ppermute(value, 'tp', pairs)]
  transfers between devices with their start and end apart: 33 -> 33, of which waited for: 13 -> 12; matrix products, arithmetic and copies ran while one was open for 0% -> 1% of each run, Pallas kernels for 13% -> 13%
where the time goes in v6:
time: 113 us
  starting transfers between devices  53.1 us (47%)
  waiting for transfers between devices  33.2 us (29%)
  Pallas kernels  23.4 us (21%)
  local copies, waits for them, and re-layouts  2.36 us (2%)
  between operations  1.25 us (1%)
    pallas_call x19, Pallas kernels, local_call(): pl.pallas_call(kernel, in_specs=[SCALARS] + in_vmem(len(operands) - 1 - a...  22.2 us
    ppermute x16, starting transfers between devices, y_shift(): lax.ppermute(value, 'fsdp', [(i, (i + 4 * dy) % 16) for i in range(16)])  21.4 us
    ppermute x16, waiting for transfers between devices, y_shift(): lax.ppermute(value, 'fsdp', [(i, (i + 4 * dy) % 16) for i in range(16)])  21.4 us
    ppermute x9, starting transfers between devices, fsdp_flip(): return lax.ppermute(value, 'fsdp', [(i, i ^ flip) for i in range(16)])  16.2 us
    ppermute x8, starting transfers between devices, tp_shift(): return lax.ppermute(value, 'tp', pairs)  15.5 us
    ppermute x8, waiting for transfers between devices, tp_shift(): return lax.ppermute(value, 'tp', pairs)  10.3 us
  transfers between devices with their start and end apart: 33, of which 12 were waited for; matrix products, arithmetic and copies ran while one was open for 1% of the time, Pallas kernels for 13%

profile of v6, /device:TPU:1, one launch (start us, length us, event | category | flops | bytes accessed | tf_op | source)
XLA Modules:
  0.0 113.3 jit_solution(6626365608196466048)
XLA Ops:
  2.0 2.1 %collective-permute-start = (bf16[512,512]{1,0:T(8,128)(2,1)S(1)}, bf16[512,512]{1,0:T(8,128)(2,1)S(1)}, u32[]{:S(2)}, u32[]{:S(2)}) collective-permute-start(bf16[512,512]{1,0:T(8,128)(2,1)S(1)} %copy-done.3), channel_id=1, source_target_pairs={{0,2},{1,3},{2,0},{3,1},{4,6},{5,7},{6,4},{7,5},{8,10},{9,11},{10,... | collective-permute-start | bytes 1572872 | tf_op jit(solution)/shard_map/ppermute | solution.py:26
  5.4 2.6 %collective-permute-start.2 = (bf16[64,2048]{1,0:T(8,128)(2,1)S(1)}, bf16[64,2048]{1,0:T(8,128)(2,1)S(1)}, u32[]{:S(2)}, u32[]{:S(2)}) collective-permute-start(bf16[64,2048]{1,0:T(8,128)(2,1)S(1)} %get-tuple-element.43), channel_id=1, source_target_pairs={{0,8},{1,9},{2,10},{3,11},{4,12},{5,13},{6,14},{7,15},{8,0},{9,1},... | collective-permute-start | bytes 786440 | tf_op jit(solution)/shard_map/ppermute | solution.py:30
  12.1 6.9 %collective-permute-done.2.a2 = bf16[64,2048]{1,0:T(8,128)(2,1)S(1)} collective-permute-done((bf16[64,2048]{1,0:T(8,128)(2,1)S(1)}, bf16[64,2048]{1,0:T(8,128)(2,1)S(1)}, u32[]{:S(2)}, u32[]{:S(2)}) %collective-permute-start.2) | collective-permute-done | bytes 262176 | tf_op jit(solution)/shard_map/ppermute | solution.py:30
  25.9 2.0 %collective-permute-start.8 = (bf16[64,512]{1,0:T(8,128)(2,1)S(1)}, bf16[64,512]{1,0:T(8,128)(2,1)S(1)}, u32[]{:S(2)}, u32[]{:S(2)}) collective-permute-start(bf16[64,512]{1,0:T(8,128)(2,1)S(1)} %get-tuple-element.58), channel_id=1, source_target_pairs={{0,8},{1,9},{2,10},{3,11},{4,12},{5,13},{6,14},{7,15},{8,0},{9,1},... | collective-permute-start | bytes 196616 | tf_op jit(solution)/shard_map/ppermute | solution.py:30
  29.3 2.8 %collective-permute-done.7.c = bf16[64,512]{1,0:T(8,128)(2,1)S(1)} collective-permute-done((bf16[64,512]{1,0:T(8,128)(2,1)S(1)}, bf16[64,512]{1,0:T(8,128)(2,1)S(1)}, u32[]{:S(2)}, u32[]{:S(2)}) %collective-permute-start.7) | collective-permute-done | bytes 65568 | tf_op jit(solution)/shard_map/ppermute | solution.py:30
  32.7 2.5 %collective-permute-start.9 = (bf16[64,512]{1,0:T(8,128)(2,1)S(1)}, bf16[64,512]{1,0:T(8,128)(2,1)S(1)}, u32[]{:S(2)}, u32[]{:S(2)}) collective-permute-start(bf16[64,512]{1,0:T(8,128)(2,1)S(1)} %total.1.mine), channel_id=1, source_target_pairs={{0,16},{16,0},{32,48},{48,32},{64,80},{80,64},{96,112},{112,96},{1... | collective-permute-start | bytes 196616 | tf_op jit(solution)/shard_map/ppermute | solution.py:35
  35.2 2.2 %collective-permute-done.9.partner = bf16[64,512]{1,0:T(8,128)(2,1)S(1)} collective-permute-done((bf16[64,512]{1,0:T(8,128)(2,1)S(1)}, bf16[64,512]{1,0:T(8,128)(2,1)S(1)}, u32[]{:S(2)}, u32[]{:S(2)}) %collective-permute-start.9) | collective-permute-done | bytes 65568 | tf_op jit(solution)/shard_map/ppermute | solution.py:35
  38.1 5.6 %collective-permute-start.12 = (bf16[512,128]{1,0:T(8,128)(2,1)S(1)}, bf16[512,128]{1,0:T(8,128)(2,1)S(1)}, u32[]{:S(2)}, u32[]{:S(2)}) collective-permute-start(bf16[512,128]{1,0:T(8,128)(2,1)S(1)} %join.1.refs_0_), channel_id=1, source_target_pairs={{0,224},{16,240},{32,0},{48,16},{64,32},{80,48},{96,64},{112,80},{... | collective-permute-start | bytes 393224 | tf_op jit(solution)/shard_map/ppermute | solution.py:35
  43.7 1.9 %collective-permute-done.12.refs_2_ = bf16[512,128]{1,0:T(8,128)(2,1)S(1)} collective-permute-done((bf16[512,128]{1,0:T(8,128)(2,1)S(1)}, bf16[512,128]{1,0:T(8,128)(2,1)S(1)}, u32[]{:S(2)}, u32[]{:S(2)}) %collective-permute-start.12) | collective-permute-done | bytes 131104 | tf_op jit(solution)/shard_map/ppermute | solution.py:35
  45.7 3.1 %collective-permute-start.13 = (bf16[512,128]{1,0:T(8,128)(2,1)S(1)}, bf16[512,128]{1,0:T(8,128)(2,1)S(1)}, u32[]{:S(2)}, u32[]{:S(2)}) collective-permute-start(bf16[512,128]{1,0:T(8,128)(2,1)S(1)} %collective-permute-done.12.refs_2_), channel_id=1, source_target_pairs={{0,224},{16,240},{32,0},{48,16},{64,32},{80,48},{96,64},{112,80},{... | collective-permute-start | bytes 393224 | tf_op jit(solution)/shard_map/ppermute | solution.py:35
  52.0 3.1 %collective-permute-done.11.refs_0_ = bf16[512,128]{1,0:T(8,128)(2,1)S(1)} collective-permute-done((bf16[512,128]{1,0:T(8,128)(2,1)S(1)}, bf16[512,128]{1,0:T(8,128)(2,1)S(1)}, u32[]{:S(2)}, u32[]{:S(2)}) %collective-permute-start.11) | collective-permute-done | bytes 131104 | tf_op jit(solution)/shard_map/ppermute | solution.py:35
  55.1 2.7 %collective-permute-start.15 = (bf16[512,128]{1,0:T(8,128)(2,1)S(1)}, bf16[512,128]{1,0:T(8,128)(2,1)S(1)}, u32[]{:S(2)}, u32[]{:S(2)}) collective-permute-start(bf16[512,128]{1,0:T(8,128)(2,1)S(1)} %collective-permute-done.13.refs_1_), channel_id=1, source_target_pairs={{0,224},{16,240},{32,0},{48,16},{64,32},{80,48},{96,64},{112,80},{... | collective-permute-start | bytes 393224 | tf_op jit(solution)/shard_map/ppermute | solution.py:35
  59.0 3.1 %collective-permute-done.14.refs_0_ = bf16[512,128]{1,0:T(8,128)(2,1)S(1)} collective-permute-done((bf16[512,128]{1,0:T(8,128)(2,1)S(1)}, bf16[512,128]{1,0:T(8,128)(2,1)S(1)}, u32[]{:S(2)}, u32[]{:S(2)}) %collective-permute-start.14) | collective-permute-done | bytes 131104 | tf_op jit(solution)/shard_map/ppermute | solution.py:35
  62.1 2.6 %last_terms.1 = (bf16[8,48,1792]{2,1,0:T(8,128)(2,1)S(1)}, f32[560,1792]{1,0:T(8,128)S(1)}) custom-call(s32[48]{0:T(128)S(1)} %table.1.where._, bf16[512,128]{1,0:T(8,128)(2,1)S(1)} %collective-permute-done.14.refs_0_, bf16[512,128]{1,0:T(8,128)(2,1)S(1)} %collective-permute-done.15.refs_1_, bf16[512,128]{1,0:T(8,128)(2,1)S(1)} %collective-permute-done.16.refs_2_, ...), custom_call_target="tpu_custom_call" | custom-call | flops 704643072 | bytes 7733440 | tf_op jit(solution)/shard_map/last_terms/pallas_call | solution.py:52
  64.7 5.0 %collective-permute-start.17 = (bf16[8,48,1792]{2,1,0:T(8,128)(2,1)S(1)}, bf16[8,48,1792]{2,1,0:T(8,128)(2,1)S(1)}, u32[]{:S(2)}, u32[]{:S(2)}) collective-permute-start(bf16[8,48,1792]{2,1,0:T(8,128)(2,1)S(1)} %get-tuple-element.63), channel_id=1, source_target_pairs={{0,1},{1,0},{2,3},{3,2},{4,5},{5,4},{6,7},{7,6},{8,9},{9,8},{10,11... | collective-permute-start | bytes 4128776 | tf_op jit(solution)/shard_map/ppermute | solution.py:26
  73.3 2.7 %collective-permute-start.23 = (bf16[48,1792]{1,0:T(8,128)(2,1)S(1)}, bf16[48,1792]{1,0:T(8,128)(2,1)S(1)}, u32[]{:S(2)}, u32[]{:S(2)}) collective-permute-start(bf16[48,1792]{1,0:T(8,128)(2,1)S(1)} %get-tuple-element.71), channel_id=1, source_target_pairs={{0,12},{1,13},{2,14},{3,15},{4,0},{5,1},{6,2},{7,3},{8,4},{9,5},{1... | collective-permute-start | bytes 516104 | tf_op jit(solution)/shard_map/ppermute | solution.py:30
  76.8 2.7 %collective-permute-start.19 = (bf16[48,1792]{1,0:T(8,128)(2,1)S(1)}, bf16[48,1792]{1,0:T(8,128)(2,1)S(1)}, u32[]{:S(2)}, u32[]{:S(2)}) collective-permute-start(bf16[48,1792]{1,0:T(8,128)(2,1)S(1)} %get-tuple-element.66), channel_id=1, source_target_pairs={{0,12},{1,13},{2,14},{3,15},{4,0},{5,1},{6,2},{7,3},{8,4},{9,5},{1... | collective-permute-start | bytes 516104 | tf_op jit(solution)/shard_map/ppermute | solution.py:30
  89.8 2.3 %collective-permute-start.28 = (bf16[48,1792]{1,0:T(8,128)(2,1)S(1)}, bf16[48,1792]{1,0:T(8,128)(2,1)S(1)}, u32[]{:S(2)}, u32[]{:S(2)}) collective-permute-start(bf16[48,1792]{1,0:T(8,128)(2,1)S(1)} %get-tuple-element.74), channel_id=1, source_target_pairs={{0,8},{1,9},{2,10},{3,11},{4,12},{5,13},{6,14},{7,15},{8,0},{9,1},... | collective-permute-start | bytes 516104 | tf_op jit(solution)/shard_map/ppermute | solution.py:30
  92.2 2.0 %collective-permute-start.27 = (bf16[48,1792]{1,0:T(8,128)(2,1)S(1)}, bf16[48,1792]{1,0:T(8,128)(2,1)S(1)}, u32[]{:S(2)}, u32[]{:S(2)}) collective-permute-start(bf16[48,1792]{1,0:T(8,128)(2,1)S(1)} %get-tuple-element.74), channel_id=1, source_target_pairs={{0,12},{1,13},{2,14},{3,15},{4,0},{5,1},{6,2},{7,3},{8,4},{9,5},{1... | collective-permute-start | bytes 516104 | tf_op jit(solution)/shard_map/ppermute | solution.py:30
  94.7 2.2 %collective-permute-start.30 = (bf16[48,1792]{1,0:T(8,128)(2,1)S(1)}, bf16[48,1792]{1,0:T(8,128)(2,1)S(1)}, u32[]{:S(2)}, u32[]{:S(2)}) collective-permute-start(bf16[48,1792]{1,0:T(8,128)(2,1)S(1)} %collective-permute-done.25), channel_id=1, source_target_pairs={{0,12},{1,13},{2,14},{3,15},{4,0},{5,1},{6,2},{7,3},{8,4},{9,5},{1... | collective-permute-start | bytes 516104 | tf_op jit(solution)/shard_map/ppermute | solution.py:30
  97.2 4.7 %collective-permute-done.26 = bf16[48,1792]{1,0:T(8,128)(2,1)S(1)} collective-permute-done((bf16[48,1792]{1,0:T(8,128)(2,1)S(1)}, bf16[48,1792]{1,0:T(8,128)(2,1)S(1)}, u32[]{:S(2)}, u32[]{:S(2)}) %collective-permute-start.26) | collective-permute-done | bytes 172064 | tf_op jit(solution)/shard_map/ppermute | solution.py:30
  101.9 3.6 %collective-permute-done.29 = bf16[48,1792]{1,0:T(8,128)(2,1)S(1)} collective-permute-done((bf16[48,1792]{1,0:T(8,128)(2,1)S(1)}, bf16[48,1792]{1,0:T(8,128)(2,1)S(1)}, u32[]{:S(2)}, u32[]{:S(2)}) %collective-permute-start.29) | collective-permute-done | bytes 172064 | tf_op jit(solution)/shard_map/ppermute | solution.py:30
  105.6 2.0 %collective-permute-start.32 = (bf16[384,1792]{1,0:T(8,128)(2,1)S(1)}, bf16[384,1792]{1,0:T(8,128)(2,1)S(1)}, u32[]{:S(2)}, u32[]{:S(2)}) collective-permute-start(bf16[384,1792]{1,0:T(8,128)(2,1)S(1)} %constant_dynamic-update-slice_fusion.updates), channel_id=1, source_target_pairs={{0,1},{1,0},{2,3},{3,2},{4,5},{5,4},{6,7},{7,6},{8,9},{9,8},{10,11... | collective-permute-start | bytes 4128776 | tf_op jit(solution)/shard_map/ppermute | solution.py:26
  110.6 2.5 %delta.1 = bf16[512,1792]{1,0:T(8,128)(2,1)} custom-call(s32[48]{0:T(128)S(1)} %table.1.where._, bf16[512,384]{1,0:T(8,128)(2,1)S(1)} %get-tuple-element.54.chosen, bf16[384,1792]{1,0:T(8,128)(2,1)S(1)} %collective-permute-done.32.updates, f32[512,1792]{1,0:T(8,128)S(1)} %half_delta.1.before), custom_call_target="tpu_custom_call" | custom-call | flops 704643072 | bytes 5439680 | tf_op jit(solution)/shard_map/delta/pallas_call | solution.py:52
  (84 shorter events, 39.2 us)
Async XLA Ops:
  2.0 17.1 %collective-permute-start = (bf16[512,512]{1,0:T(8,128)(2,1)S(1)}, bf16[512,512]{1,0:T(8,128)(2,1)S(1)}, u32[]{:S(2)}, u32[]{:S(2)}) collective-permute-start(bf16[512,512]{1,0:T(8,128)(2,1)S(1)} %copy-done.3), channel_id=1, source_target_pairs={{0,2},{1,3},{2,0},{3,1},{4,6},{5,7},{6,4},{7,5},{8,10},{9,11},{10,... | collective-permute-start | bytes 1572872 | tf_op jit(solution)/shard_map/ppermute | solution.py:26
  4.1 8.0 %collective-permute-start.1 = (bf16[64,2048]{1,0:T(8,128)(2,1)S(1)}, bf16[64,2048]{1,0:T(8,128)(2,1)S(1)}, u32[]{:S(2)}, u32[]{:S(2)}) collective-permute-start(bf16[64,2048]{1,0:T(8,128)(2,1)S(1)} %get-tuple-element.42), channel_id=1, source_target_pairs={{0,4},{1,5},{2,6},{3,7},{4,8},{5,9},{6,10},{7,11},{8,12},{9,13},{1... | collective-permute-start | bytes 786440 | tf_op jit(solution)/shard_map/ppermute | solution.py:30
  5.4 13.6 %collective-permute-start.2 = (bf16[64,2048]{1,0:T(8,128)(2,1)S(1)}, bf16[64,2048]{1,0:T(8,128)(2,1)S(1)}, u32[]{:S(2)}, u32[]{:S(2)}) collective-permute-start(bf16[64,2048]{1,0:T(8,128)(2,1)S(1)} %get-tuple-element.43), channel_id=1, source_target_pairs={{0,8},{1,9},{2,10},{3,11},{4,12},{5,13},{6,14},{7,15},{8,0},{9,1},... | collective-permute-start | bytes 786440 | tf_op jit(solution)/shard_map/ppermute | solution.py:30
  8.1 11.0 %collective-permute-start.3 = (bf16[64,2048]{1,0:T(8,128)(2,1)S(1)}, bf16[64,2048]{1,0:T(8,128)(2,1)S(1)}, u32[]{:S(2)}, u32[]{:S(2)}) collective-permute-start(bf16[64,2048]{1,0:T(8,128)(2,1)S(1)} %get-tuple-element.44), channel_id=1, source_target_pairs={{0,12},{1,13},{2,14},{3,15},{4,0},{5,1},{6,2},{7,3},{8,4},{9,5},{1... | collective-permute-start | bytes 786440 | tf_op jit(solution)/shard_map/ppermute | solution.py:30
  9.1 12.8 %collective-permute-start.5 = (bf16[512,512]{1,0:T(8,128)(2,1)S(1)}, bf16[512,512]{1,0:T(8,128)(2,1)S(1)}, u32[]{:S(2)}, u32[]{:S(2)}) collective-permute-start(bf16[512,512]{1,0:T(8,128)(2,1)S(1)} %copy-done.3), channel_id=1, source_target_pairs={{0,1},{1,0},{2,3},{3,2},{4,5},{5,4},{6,7},{7,6},{8,9},{9,8},{10,11... | collective-permute-start | bytes 1572872 | tf_op jit(solution)/shard_map/ppermute | solution.py:26
  38.1 7.6 %collective-permute-start.12 = (bf16[512,128]{1,0:T(8,128)(2,1)S(1)}, bf16[512,128]{1,0:T(8,128)(2,1)S(1)}, u32[]{:S(2)}, u32[]{:S(2)}) collective-permute-start(bf16[512,128]{1,0:T(8,128)(2,1)S(1)} %join.1.refs_0_), channel_id=1, source_target_pairs={{0,224},{16,240},{32,0},{48,16},{64,32},{80,48},{96,64},{112,80},{... | collective-permute-start | bytes 393224 | tf_op jit(solution)/shard_map/ppermute | solution.py:35
  45.7 6.3 %collective-permute-start.13 = (bf16[512,128]{1,0:T(8,128)(2,1)S(1)}, bf16[512,128]{1,0:T(8,128)(2,1)S(1)}, u32[]{:S(2)}, u32[]{:S(2)}) collective-permute-start(bf16[512,128]{1,0:T(8,128)(2,1)S(1)} %collective-permute-done.12.refs_2_), channel_id=1, source_target_pairs={{0,224},{16,240},{32,0},{48,16},{64,32},{80,48},{96,64},{112,80},{... | collective-permute-start | bytes 393224 | tf_op jit(solution)/shard_map/ppermute | solution.py:35
  48.7 6.4 %collective-permute-start.11 = (bf16[512,128]{1,0:T(8,128)(2,1)S(1)}, bf16[512,128]{1,0:T(8,128)(2,1)S(1)}, u32[]{:S(2)}, u32[]{:S(2)}) collective-permute-start(bf16[512,128]{1,0:T(8,128)(2,1)S(1)} %collective-permute-done.10.refs_1_), channel_id=1, source_target_pairs={{0,32},{16,48},{32,64},{48,80},{64,96},{80,112},{96,128},{112,144}... | collective-permute-start | bytes 393224 | tf_op jit(solution)/shard_map/ppermute | solution.py:35
  48.7 10.3 %collective-permute-start.16 = (bf16[512,128]{1,0:T(8,128)(2,1)S(1)}, bf16[512,128]{1,0:T(8,128)(2,1)S(1)}, u32[]{:S(2)}, u32[]{:S(2)}) collective-permute-start(bf16[512,128]{1,0:T(8,128)(2,1)S(1)} %join.1.refs_0_), channel_id=1, source_target_pairs={{0,128},{16,144},{32,160},{48,176},{64,192},{80,208},{96,224},{112... | collective-permute-start | bytes 393224 | tf_op jit(solution)/shard_map/ppermute | solution.py:35
  55.1 7.0 %collective-permute-start.14 = (bf16[512,128]{1,0:T(8,128)(2,1)S(1)}, bf16[512,128]{1,0:T(8,128)(2,1)S(1)}, u32[]{:S(2)}, u32[]{:S(2)}) collective-permute-start(bf16[512,128]{1,0:T(8,128)(2,1)S(1)} %collective-permute-done.11.refs_0_), channel_id=1, source_target_pairs={{0,32},{16,48},{32,64},{48,80},{64,96},{80,112},{96,128},{112,144}... | collective-permute-start | bytes 393224 | tf_op jit(solution)/shard_map/ppermute | solution.py:35
  55.1 7.0 %collective-permute-start.15 = (bf16[512,128]{1,0:T(8,128)(2,1)S(1)}, bf16[512,128]{1,0:T(8,128)(2,1)S(1)}, u32[]{:S(2)}, u32[]{:S(2)}) collective-permute-start(bf16[512,128]{1,0:T(8,128)(2,1)S(1)} %collective-permute-done.13.refs_1_), channel_id=1, source_target_pairs={{0,224},{16,240},{32,0},{48,16},{64,32},{80,48},{96,64},{112,80},{... | collective-permute-start | bytes 393224 | tf_op jit(solution)/shard_map/ppermute | solution.py:35
  64.7 7.7 %collective-permute-start.17 = (bf16[8,48,1792]{2,1,0:T(8,128)(2,1)S(1)}, bf16[8,48,1792]{2,1,0:T(8,128)(2,1)S(1)}, u32[]{:S(2)}, u32[]{:S(2)}) collective-permute-start(bf16[8,48,1792]{2,1,0:T(8,128)(2,1)S(1)} %get-tuple-element.63), channel_id=1, source_target_pairs={{0,1},{1,0},{2,3},{3,2},{4,5},{5,4},{6,7},{7,6},{8,9},{9,8},{10,11... | collective-permute-start | bytes 4128776 | tf_op jit(solution)/shard_map/ppermute | solution.py:26
  73.0 6.5 %collective-permute-start.20 = (bf16[48,1792]{1,0:T(8,128)(2,1)S(1)}, bf16[48,1792]{1,0:T(8,128)(2,1)S(1)}, u32[]{:S(2)}, u32[]{:S(2)}) collective-permute-start(bf16[48,1792]{1,0:T(8,128)(2,1)S(1)} %get-tuple-element.68), channel_id=1, source_target_pairs={{0,2},{1,3},{2,0},{3,1},{4,6},{5,7},{6,4},{7,5},{8,10},{9,11},{10,... | collective-permute-start | bytes 516104 | tf_op jit(solution)/shard_map/ppermute | solution.py:26
  73.3 6.8 %collective-permute-start.22 = (bf16[48,1792]{1,0:T(8,128)(2,1)S(1)}, bf16[48,1792]{1,0:T(8,128)(2,1)S(1)}, u32[]{:S(2)}, u32[]{:S(2)}) collective-permute-start(bf16[48,1792]{1,0:T(8,128)(2,1)S(1)} %get-tuple-element.70), channel_id=1, source_target_pairs={{0,4},{1,5},{2,6},{3,7},{4,8},{5,9},{6,10},{7,11},{8,12},{9,13},{1... | collective-permute-start | bytes 516104 | tf_op jit(solution)/shard_map/ppermute | solution.py:30
  73.3 6.8 %collective-permute-start.23 = (bf16[48,1792]{1,0:T(8,128)(2,1)S(1)}, bf16[48,1792]{1,0:T(8,128)(2,1)S(1)}, u32[]{:S(2)}, u32[]{:S(2)}) collective-permute-start(bf16[48,1792]{1,0:T(8,128)(2,1)S(1)} %get-tuple-element.71), channel_id=1, source_target_pairs={{0,12},{1,13},{2,14},{3,15},{4,0},{5,1},{6,2},{7,3},{8,4},{9,5},{1... | collective-permute-start | bytes 516104 | tf_op jit(solution)/shard_map/ppermute | solution.py:30
  76.7 6.4 %collective-permute-start.18 = (bf16[48,1792]{1,0:T(8,128)(2,1)S(1)}, bf16[48,1792]{1,0:T(8,128)(2,1)S(1)}, u32[]{:S(2)}, u32[]{:S(2)}) collective-permute-start(bf16[48,1792]{1,0:T(8,128)(2,1)S(1)} %get-tuple-element.65), channel_id=1, source_target_pairs={{0,4},{1,5},{2,6},{3,7},{4,8},{5,9},{6,10},{7,11},{8,12},{9,13},{1... | collective-permute-start | bytes 516104 | tf_op jit(solution)/shard_map/ppermute | solution.py:30
  76.8 7.0 %collective-permute-start.19 = (bf16[48,1792]{1,0:T(8,128)(2,1)S(1)}, bf16[48,1792]{1,0:T(8,128)(2,1)S(1)}, u32[]{:S(2)}, u32[]{:S(2)}) collective-permute-start(bf16[48,1792]{1,0:T(8,128)(2,1)S(1)} %get-tuple-element.66), channel_id=1, source_target_pairs={{0,12},{1,13},{2,14},{3,15},{4,0},{5,1},{6,2},{7,3},{8,4},{9,5},{1... | collective-permute-start | bytes 516104 | tf_op jit(solution)/shard_map/ppermute | solution.py:30
  86.9 7.8 %collective-permute-start.25 = (bf16[48,1792]{1,0:T(8,128)(2,1)S(1)}, bf16[48,1792]{1,0:T(8,128)(2,1)S(1)}, u32[]{:S(2)}, u32[]{:S(2)}) collective-permute-start(bf16[48,1792]{1,0:T(8,128)(2,1)S(1)} %get-tuple-element.72.update), channel_id=1, source_target_pairs={{0,2},{1,3},{2,0},{3,1},{4,6},{5,7},{6,4},{7,5},{8,10},{9,11},{10,... | collective-permute-start | bytes 516104 | tf_op jit(solution)/shard_map/ppermute | solution.py:26
  89.8 7.1 %collective-permute-start.28 = (bf16[48,1792]{1,0:T(8,128)(2,1)S(1)}, bf16[48,1792]{1,0:T(8,128)(2,1)S(1)}, u32[]{:S(2)}, u32[]{:S(2)}) collective-permute-start(bf16[48,1792]{1,0:T(8,128)(2,1)S(1)} %get-tuple-element.74), channel_id=1, source_target_pairs={{0,8},{1,9},{2,10},{3,11},{4,12},{5,13},{6,14},{7,15},{8,0},{9,1},... | collective-permute-start | bytes 516104 | tf_op jit(solution)/shard_map/ppermute | solution.py:30
  92.2 9.7 %collective-permute-start.27 = (bf16[48,1792]{1,0:T(8,128)(2,1)S(1)}, bf16[48,1792]{1,0:T(8,128)(2,1)S(1)}, u32[]{:S(2)}, u32[]{:S(2)}) collective-permute-start(bf16[48,1792]{1,0:T(8,128)(2,1)S(1)} %get-tuple-element.74), channel_id=1, source_target_pairs={{0,12},{1,13},{2,14},{3,15},{4,0},{5,1},{6,2},{7,3},{8,4},{9,5},{1... | collective-permute-start | bytes 516104 | tf_op jit(solution)/shard_map/ppermute | solution.py:30
  94.1 7.7 %collective-permute-start.26 = (bf16[48,1792]{1,0:T(8,128)(2,1)S(1)}, bf16[48,1792]{1,0:T(8,128)(2,1)S(1)}, u32[]{:S(2)}, u32[]{:S(2)}) collective-permute-start(bf16[48,1792]{1,0:T(8,128)(2,1)S(1)} %get-tuple-element.74), channel_id=1, source_target_pairs={{0,4},{1,5},{2,6},{3,7},{4,8},{5,9},{6,10},{7,11},{8,12},{9,13},{1... | collective-permute-start | bytes 516104 | tf_op jit(solution)/shard_map/ppermute | solution.py:30
  94.7 10.8 %collective-permute-start.30 = (bf16[48,1792]{1,0:T(8,128)(2,1)S(1)}, bf16[48,1792]{1,0:T(8,128)(2,1)S(1)}, u32[]{:S(2)}, u32[]{:S(2)}) collective-permute-start(bf16[48,1792]{1,0:T(8,128)(2,1)S(1)} %collective-permute-done.25), channel_id=1, source_target_pairs={{0,12},{1,13},{2,14},{3,15},{4,0},{5,1},{6,2},{7,3},{8,4},{9,5},{1... | collective-permute-start | bytes 516104 | tf_op jit(solution)/shard_map/ppermute | solution.py:30
  96.9 8.6 %collective-permute-start.29 = (bf16[48,1792]{1,0:T(8,128)(2,1)S(1)}, bf16[48,1792]{1,0:T(8,128)(2,1)S(1)}, u32[]{:S(2)}, u32[]{:S(2)}) collective-permute-start(bf16[48,1792]{1,0:T(8,128)(2,1)S(1)} %collective-permute-done.25), channel_id=1, source_target_pairs={{0,4},{1,5},{2,6},{3,7},{4,8},{5,9},{6,10},{7,11},{8,12},{9,13},{1... | collective-permute-start | bytes 516104 | tf_op jit(solution)/shard_map/ppermute | solution.py:30
  96.9 8.7 %collective-permute-start.31 = (bf16[48,1792]{1,0:T(8,128)(2,1)S(1)}, bf16[48,1792]{1,0:T(8,128)(2,1)S(1)}, u32[]{:S(2)}, u32[]{:S(2)}) collective-permute-start(bf16[48,1792]{1,0:T(8,128)(2,1)S(1)} %collective-permute-done.28), channel_id=1, source_target_pairs={{0,2},{1,3},{2,0},{3,1},{4,6},{5,7},{6,4},{7,5},{8,10},{9,11},{10,... | collective-permute-start | bytes 516104 | tf_op jit(solution)/shard_map/ppermute | solution.py:26
  (15 other events, 115.5 us)
